TPU v7x, 128 devices: a whole 4x4x4 slice. The times are simulated.
128 devices in a mesh: inner: 8 (over x_lo, y), outer: 8 (over z, core), head: 2 (over x_hi).
Axes of the slice: x: 4 (x_hi: 2, x_lo: 2; x = x_hi * 2 + x_lo), y: 4, z: 4, core: 2. Of those that a mesh axis runs over, the one named last changes fastest.
Arguments:
- queries: bfloat16 [16384, 3072], P(('inner', 'outer', 'head')), may hold values from -5 to 5
- keys: bfloat16 [16384, 512], P(('inner', 'outer', 'head')), may hold values from -5 to 5
- values: bfloat16 [16384, 512], P(('inner', 'outer', 'head')), may hold values from -6 to 6
- output_gradient: bfloat16 [16384, 3072], P(('inner', 'outer', 'head')), may hold values from -6 to 6
- span_order: int32 [128], replicated, may hold values from 0 to 127, each once
Outputs:
- grad_q: bfloat16 [16384, 3072], P(('inner', 'outer', 'head'))
- key_gradient_out: bfloat16 [16384, 512], P(('inner', 'outer', 'head'))
- value_gradient_out: bfloat16 [16384, 512], P(('inner', 'outer', 'head'))
Inputs may be any that keep to these rules, and one draw needn't show every extreme that they name: A permutation; storage rows j * 128 to (j + 1) * 128 - 1 hold the sequence positions span_order[j] * 128 onward.
All inputs are finite; a program needn't handle non-finite values.
Results may differ from a plain program's by a relative error of at most 0.0077.
Values may be sent and summed in bfloat16 or wider, within the bound.
No kernel may reach another device: no remote copies, remote signals or barrier semaphores. Data moves between devices by JAX's collectives and lax.ppermute only.
A program may use at most 192 MiB of HBM per device.

v0:
```python
import math

import jax
import jax.numpy as jnp
from jax import lax
from jax.sharding import PartitionSpec as P

QUERY_HEADS = 24
KEY_VALUE_HEADS = 4
HEAD_SIZE = 128
INNER_WIN = 4
OUTER_WIN = 2


def from_behind(value, axis, by):
    peers = lax.axis_size(axis)
    return lax.ppermute(value, axis, [(i, (i + by) % peers) for i in range(peers)])


def positions(span_order, first_row, row_count, span_rows):
    row_index = first_row + jnp.arange(row_count, dtype=jnp.int32)
    slot_index = row_index // span_rows
    matches = slot_index[:, None] == jnp.arange(span_order.shape[0], dtype=jnp.int32)[None, :]
    span_ids = jnp.sum(jnp.where(matches, span_order[None, :], 0), axis=1)
    return span_ids * span_rows + row_index % span_rows


def shards(queries, keys, values, output_gradient, span_order):
    local_query, local_key, local_value, local_grad = (
        lax.all_to_all(queries, "head", split_axis=1, concat_axis=0, tiled=True),
        lax.all_to_all(keys, "head", split_axis=1, concat_axis=0, tiled=True),
        lax.all_to_all(values, "head", split_axis=1, concat_axis=0, tiled=True),
        lax.all_to_all(output_gradient, "head", split_axis=1, concat_axis=0, tiled=True),
    )
    tokens_here = local_query.shape[0]
    span_rows = tokens_here // 2
    heads_per_group = QUERY_HEADS // KEY_VALUE_HEADS
    kv_heads = local_key.shape[1] // HEAD_SIZE
    score_scaling_factor = 1.0 / math.sqrt(HEAD_SIZE)
    query_head_rows = local_query.reshape(tokens_here, kv_heads, heads_per_group, HEAD_SIZE)
    gradient_head_list = local_grad.reshape(tokens_here, kv_heads, heads_per_group, HEAD_SIZE)
    inner_count = lax.axis_size("inner")
    outer_count = lax.axis_size("outer")
    my_inner = lax.axis_index("inner")
    my_outer = lax.axis_index("outer")
    my_cycle = my_inner * outer_count + my_outer
    query_pos = positions(span_order, my_cycle * tokens_here, tokens_here, span_rows)

    def masked_scores(key_rows, key_pos):
        keys_here = key_rows.reshape(key_rows.shape[0], kv_heads, HEAD_SIZE)
        scores = (
            jnp.einsum(
                "qhgd,khd->hgqk", query_head_rows, keys_here, preferred_element_type=jnp.float32
            )
            * score_scaling_factor
        )
        visible = key_pos[None, :] <= query_pos[:, None]
        return jnp.where(visible[None, None], scores, -jnp.inf)

    def grad_products(value_rows):
        values_here = value_rows.reshape(value_rows.shape[0], kv_heads, HEAD_SIZE)
        return jnp.einsum(
            "qhgd,khd->hgqk", gradient_head_list, values_here, preferred_element_type=jnp.float32
        )

    path = []
    for outer_step in range(OUTER_WIN):
        inner_steps = range(INNER_WIN) if outer_step % 2 == 0 else range(INNER_WIN - 1, -1, -1)
        for inner_step in inner_steps:
            path.append((inner_step, outer_step))

    def move(moving, inner_by, outer_by):
        if outer_by != 0:
            return from_behind(moving, "outer", outer_by)
        return from_behind(moving, "inner", inner_by)

    stat_shape = (kv_heads, heads_per_group, tokens_here)
    running = (
        jnp.full(stat_shape, -1e30, jnp.float32),
        jnp.zeros(stat_shape, jnp.float32),
        jnp.zeros(stat_shape, jnp.float32),
    )
    moving = jnp.stack([local_key, local_value])
    kept = []
    for step_number in range(len(path)):
        inner_step, outer_step = path[step_number]
        if step_number > 0:
            last_inner, last_outer = path[step_number - 1]
            moving = move(moving, inner_step - last_inner, outer_step - last_outer)
        key_pos = positions(
            span_order,
            (
                (my_inner - inner_step) % inner_count * outer_count
                + (my_outer - outer_step) % outer_count
            )
            * tokens_here,
            tokens_here,
            span_rows,
        )
        kept.append((moving, key_pos, inner_step, outer_step))

        def fold_stats(running=running, moving=moving, key_pos=key_pos):
            running_max, running_sum, running_dot = running
            scores = masked_scores(moving[0], key_pos)
            grad_dot = grad_products(moving[1])
            new_max = jnp.maximum(running_max, jnp.max(scores, axis=-1))
            decay = jnp.exp(running_max - new_max)
            shifted = jnp.exp(scores - new_max[..., None])
            return (
                new_max,
                running_sum * decay + jnp.sum(shifted, axis=-1),
                running_dot * decay + jnp.sum(shifted * grad_dot, axis=-1),
            )

        running = fold_stats()
    running_max, running_sum, running_dot = running
    log_total = running_max + jnp.log(running_sum)
    row_dot = running_dot / running_sum
    grad_query = jnp.zeros((tokens_here, kv_heads, heads_per_group, HEAD_SIZE), jnp.float32)
    empty_terms = jnp.zeros(moving.shape, jnp.float32)
    partials = []
    for block_rows, key_pos, inner_step, outer_step in kept:

        def grad_block(block_rows=block_rows, key_pos=key_pos):
            key_rows = block_rows[0]
            value_rows = block_rows[1]
            scores = masked_scores(key_rows, key_pos)
            weights = jnp.exp(scores - log_total[..., None])
            grad_dot = grad_products(value_rows)
            score_gradient = (weights * (grad_dot - row_dot[..., None])).astype(jnp.bfloat16)
            weight_lower_precision = weights.astype(jnp.bfloat16)
            keys_here = key_rows.reshape(tokens_here, kv_heads, HEAD_SIZE)
            query_term = jnp.einsum(
                "hgqk,khd->qhgd", score_gradient, keys_here, preferred_element_type=jnp.float32
            )
            key_gradient_term = jnp.einsum(
                "emts,temc->sec",
                score_gradient,
                query_head_rows,
                preferred_element_type=jnp.float32,
            )
            value_gradient_term = jnp.einsum(
                "emts,temc->sec",
                weight_lower_precision,
                gradient_head_list,
                preferred_element_type=jnp.float32,
            )
            grad_terms = jnp.stack([key_gradient_term, value_gradient_term]).reshape(
                empty_terms.shape
            )
            return (query_term, grad_terms)

        query_term, grad_terms = grad_block()
        grad_query = grad_query + query_term
        partials.append((grad_terms, inner_step, outer_step))
    total_terms = empty_terms
    for grad_terms, inner_step, outer_step in partials:
        arrived = grad_terms
        if inner_step != 0:
            arrived = from_behind(arrived, "inner", -inner_step)
        if outer_step != 0:
            arrived = from_behind(arrived, "outer", -outer_step)
        total_terms = total_terms + arrived
    query_grad = (
        (score_scaling_factor * grad_query)
        .astype(jnp.bfloat16)
        .reshape(tokens_here, kv_heads * heads_per_group * HEAD_SIZE)
    )
    key_grad = (score_scaling_factor * total_terms[0]).astype(jnp.bfloat16)
    value_grad = total_terms[1].astype(jnp.bfloat16)
    grad_q, key_gradient_out, value_gradient_out = (
        lax.all_to_all(query_grad, "head", split_axis=0, concat_axis=1, tiled=True),
        lax.all_to_all(key_grad, "head", split_axis=0, concat_axis=1, tiled=True),
        lax.all_to_all(value_grad, "head", split_axis=0, concat_axis=1, tiled=True),
    )
    return (grad_q, key_gradient_out, value_gradient_out)


def solution(mesh):
    placed = (
        P(("inner", "outer", "head"), None),
        P(("inner", "outer", "head"), None),
        P(("inner", "outer", "head"), None),
        P(("inner", "outer", "head"), None),
        P(),
    )
    return jax.shard_map(
        shards,
        mesh=mesh,
        in_specs=placed,
        out_specs=(
            P(("inner", "outer", "head"), None),
            P(("inner", "outer", "head"), None),
            P(("inner", "outer", "head"), None),
        ),
        check_vma=False,
    )
```

profile of v0, /device:TPU:58, one launch (start us, length us, event | category | flops | bytes accessed | tf_op | source)
XLA Modules:
  0.0 297.8 jit_solution(14298340001401649324)
XLA Ops:
  2.4 3.4 %all-to-all-start = ((bf16[128,2,256]{0,2,1:T(8,128)(2,1)}), bf16[128,2,256]{0,2,1:T(8,128)(2,1)S(1)}, u32[]{:S(2)}, u32[]{:S(2)}) async-start(bf16[128,2,256]{0,2,1:T(8,128)(2,1)} %bitcast), calls=%async_computation | async-start | bytes 262144 | tf_op jit(solution)/shard_map/all_to_all | solution.py:31
  11.7 3.4 %all-to-all-start.2 = ((bf16[128,2,256]{0,2,1:T(8,128)(2,1)}), bf16[128,2,256]{0,2,1:T(8,128)(2,1)S(1)}, u32[]{:S(2)}, u32[]{:S(2)}) async-start(bf16[128,2,256]{0,2,1:T(8,128)(2,1)} %bitcast.7), calls=%async_computation.2 | async-start | bytes 262144 | tf_op jit(solution)/shard_map/all_to_all | solution.py:32
  17.4 3.7 %all-to-all-done.2 = bf16[128,2,256]{0,2,1:T(8,128)(2,1)S(1)} async-done(((bf16[128,2,256]{0,2,1:T(8,128)(2,1)}), bf16[128,2,256]{0,2,1:T(8,128)(2,1)S(1)}, u32[]{:S(2)}, u32[]{:S(2)}) %all-to-all-start.2) | async-done | bytes 131104 | tf_op jit(solution)/shard_map/all_to_all | solution.py:32
  21.1 3.5 %all-to-all-start.1 = ((bf16[128,2,1536]{0,2,1:T(8,128)(2,1)}), bf16[128,2,1536]{0,2,1:T(8,128)(2,1)S(1)}, u32[]{:S(2)}, u32[]{:S(2)}) async-start(bf16[128,2,1536]{0,2,1:T(8,128)(2,1)} %bitcast.3), calls=%async_computation.1 | async-start | bytes 1572864 | tf_op jit(solution)/shard_map/all_to_all | solution.py:30
  27.3 10.4 %all-to-all-done.1 = bf16[128,2,1536]{0,2,1:T(8,128)(2,1)S(1)} async-done(((bf16[128,2,1536]{0,2,1:T(8,128)(2,1)}), bf16[128,2,1536]{0,2,1:T(8,128)(2,1)S(1)}, u32[]{:S(2)}, u32[]{:S(2)}) %all-to-all-start.1) | async-done | bytes 786464 | tf_op jit(solution)/shard_map/all_to_all | solution.py:30
  37.7 3.5 %all-to-all-start.3 = ((bf16[128,2,1536]{0,2,1:T(8,128)(2,1)}), bf16[128,2,1536]{0,2,1:T(8,128)(2,1)S(1)}, u32[]{:S(2)}, u32[]{:S(2)}) async-start(bf16[128,2,1536]{0,2,1:T(8,128)(2,1)} %bitcast.32), calls=%async_computation.3 | async-start | bytes 1572864 | tf_op jit(solution)/shard_map/all_to_all | solution.py:33
  44.4 6.5 %copy.431 = bf16[2,128,1536]{1,0,2:T(2,128)(2,1)S(1)} copy(bf16[2,128,1536]{1,2,0:T(8,128)(2,1)S(1)} %bitcast.408) | data formatting | bytes 1572864 | tf_op jit(solution)/shard_map/all_to_all | solution.py:30
  51.7 6.5 %copy.460 = bf16[2,128,1536]{1,0,2:T(2,128)(2,1)S(1)} copy(bf16[2,128,1536]{1,2,0:T(8,128)(2,1)S(1)} %bitcast.409) | data formatting | bytes 1572864 | tf_op jit(solution)/shard_map/all_to_all | solution.py:33
  65.8 2.9 fusion.111
  68.8 3.6 %collective-permute-done.2 = bf16[2,256,256]{2,1,0:T(8,128)(2,1)S(1)} collective-permute-done((bf16[2,256,256]{2,1,0:T(8,128)(2,1)}, bf16[2,256,256]{2,1,0:T(8,128)(2,1)S(1)}, u32[]{:S(2)}, u32[]{:S(2)}) %collective-permute-start.2) | collective-permute-done | bytes 262176 | tf_op jit(solution)/shard_map/ppermute | solution.py:17
  72.7 3.0 fusion.110
  84.1 5.6 %collective-permute-done.4 = bf16[2,256,256]{2,1,0:T(8,128)(2,1)S(1)} collective-permute-done((bf16[2,256,256]{2,1,0:T(8,128)(2,1)}, bf16[2,256,256]{2,1,0:T(8,128)(2,1)S(1)}, u32[]{:S(2)}, u32[]{:S(2)}) %collective-permute-start.4) | collective-permute-done | bytes 262176 | tf_op jit(solution)/shard_map/ppermute | solution.py:17
  93.6 6.3 %collective-permute-done.5 = bf16[2,256,256]{2,1,0:T(8,128)(2,1)S(1)} collective-permute-done((bf16[2,256,256]{2,1,0:T(8,128)(2,1)}, bf16[2,256,256]{2,1,0:T(8,128)(2,1)S(1)}, u32[]{:S(2)}, u32[]{:S(2)}) %collective-permute-start.5) | collective-permute-done | bytes 262176 | tf_op jit(solution)/shard_map/ppermute | solution.py:17
  100.9 2.9 fusion.107
  103.8 5.8 %collective-permute-done.6 = bf16[2,256,256]{2,1,0:T(8,128)(2,1)S(1)} collective-permute-done((bf16[2,256,256]{2,1,0:T(8,128)(2,1)}, bf16[2,256,256]{2,1,0:T(8,128)(2,1)S(1)}, u32[]{:S(2)}, u32[]{:S(2)}) %collective-permute-start.6) | collective-permute-done | bytes 262176 | tf_op jit(solution)/shard_map/ppermute | solution.py:17
  141.2 19.6 %fusion.2 = (bf16[2,6,256,256]{2,3,1,0:T(8,128)(2,1)}, bf16[2,6,256,256]{2,3,1,0:T(8,128)(2,1)}, bf16[2,6,256,256]{2,3,1,0:T(8,128)(2,1)}, bf16[2,6,256,256]{2,3...) fusion(f32[2,256,256,6]{2,1,3,0:T(8,128)} %get-tuple-element.96, ...), kind=kLoop, calls=%fused_computation.4 | loop fusion | flops 25165824 | bytes 62939136 | tf_op jit(solution)/shard_map/convert_element_type | solution.py:130
  187.3 4.4 %all-to-all-start.4 = ((bf16[2,128,1536]{1,2,0:T(8,128)(2,1)}), bf16[2,128,1536]{1,2,0:T(8,128)(2,1)}, u32[]{:S(2)}, u32[]{:S(2)}) async-start(bf16[2,128,1536]{1,2,0:T(8,128)(2,1)} %copy.501), calls=%async_computation.4 | async-start | bytes 1572864 | tf_op jit(solution)/shard_map/all_to_all | solution.py:172
  196.4 3.3 %collective-permute-start.10 = (f32[2,256,256]{1,2,0:T(8,128)S(1)}, f32[2,256,256]{1,2,0:T(8,128)S(1)}, u32[]{:S(2)}, u32[]{:S(2)}) collective-permute-start(f32[2,256,256]{1,2,0:T(8,128)S(1)} %pad_maximum_fusion.3), channel_id=1, source_target_pairs={{0,80},{16,96},{32,112},{48,0},{64,16},{80,32},{96,48},{112,64},{1... | collective-permute-start | bytes 1572872 | tf_op jit(solution)/shard_map/ppermute | solution.py:17
  203.8 14.7 %collective-permute-done.14 = f32[2,256,256]{1,2,0:T(8,128)S(1)} collective-permute-done((f32[2,256,256]{1,2,0:T(8,128)S(1)}, f32[2,256,256]{1,2,0:T(8,128)S(1)}, u32[]{:S(2)}, u32[]{:S(2)}) %collective-permute-start.14) | collective-permute-done | bytes 524320 | tf_op jit(solution)/shard_map/ppermute | solution.py:17
  220.1 34.9 %collective-permute-done.8 = f32[2,256,256]{1,2,0:T(8,128)S(1)} collective-permute-done((f32[2,256,256]{1,2,0:T(8,128)S(1)}, f32[2,256,256]{1,2,0:T(8,128)S(1)}, u32[]{:S(2)}, u32[]{:S(2)}) %collective-permute-start.8) | collective-permute-done | bytes 524320 | tf_op jit(solution)/shard_map/ppermute | solution.py:17
  256.3 18.3 %collective-permute-done.7 = f32[2,256,256]{1,2,0:T(8,128)S(1)} collective-permute-done((f32[2,256,256]{1,2,0:T(8,128)S(1)}, f32[2,256,256]{1,2,0:T(8,128)S(1)}, u32[]{:S(2)}, u32[]{:S(2)}) %collective-permute-start.7) | collective-permute-done | bytes 524320 | tf_op jit(solution)/shard_map/ppermute | solution.py:17
  275.8 5.6 %all-to-all-start.6 = ((bf16[2,128,256]{2,1,0:T(8,128)(2,1)}), bf16[2,128,256]{2,1,0:T(8,128)(2,1)S(1)}, u32[]{:S(2)}, u32[]{:S(2)}) async-start(bf16[2,128,256]{2,1,0:T(8,128)(2,1)} %bitcast.148), calls=%async_computation.6 | async-start | bytes 262144 | tf_op jit(solution)/shard_map/all_to_all | solution.py:174
  282.1 5.2 %all-to-all-done.6 = bf16[2,128,256]{2,1,0:T(8,128)(2,1)S(1)} async-done(((bf16[2,128,256]{2,1,0:T(8,128)(2,1)}), bf16[2,128,256]{2,1,0:T(8,128)(2,1)S(1)}, u32[]{:S(2)}, u32[]{:S(2)}) %all-to-all-start.6) | async-done | bytes 131104 | tf_op jit(solution)/shard_map/all_to_all | solution.py:174
  287.3 3.4 %all-to-all-start.5 = ((bf16[2,128,256]{2,1,0:T(8,128)(2,1)}), bf16[2,128,256]{2,1,0:T(8,128)(2,1)S(1)}, u32[]{:S(2)}, u32[]{:S(2)}) async-start(bf16[2,128,256]{2,1,0:T(8,128)(2,1)} %bitcast.145), calls=%async_computation.5 | async-start | bytes 262144 | tf_op jit(solution)/shard_map/all_to_all | solution.py:173
  (222 shorter events, 115.7 us)
Async XLA Ops:
  2.4 9.4 %all-to-all-start = ((bf16[128,2,256]{0,2,1:T(8,128)(2,1)}), bf16[128,2,256]{0,2,1:T(8,128)(2,1)S(1)}, u32[]{:S(2)}, u32[]{:S(2)}) async-start(bf16[128,2,256]{0,2,1:T(8,128)(2,1)} %bitcast), calls=%async_computation | async-start | bytes 262144 | tf_op jit(solution)/shard_map/all_to_all | solution.py:31
  11.7 9.3 %all-to-all-start.2 = ((bf16[128,2,256]{0,2,1:T(8,128)(2,1)}), bf16[128,2,256]{0,2,1:T(8,128)(2,1)S(1)}, u32[]{:S(2)}, u32[]{:S(2)}) async-start(bf16[128,2,256]{0,2,1:T(8,128)(2,1)} %bitcast.7), calls=%async_computation.2 | async-start | bytes 262144 | tf_op jit(solution)/shard_map/all_to_all | solution.py:32
  21.1 16.6 %all-to-all-start.1 = ((bf16[128,2,1536]{0,2,1:T(8,128)(2,1)}), bf16[128,2,1536]{0,2,1:T(8,128)(2,1)S(1)}, u32[]{:S(2)}, u32[]{:S(2)}) async-start(bf16[128,2,1536]{0,2,1:T(8,128)(2,1)} %bitcast.3), calls=%async_computation.1 | async-start | bytes 1572864 | tf_op jit(solution)/shard_map/all_to_all | solution.py:30
  24.9 17.5 %collective-permute-start = (bf16[2,256,256]{2,1,0:T(8,128)(2,1)S(1)}, bf16[2,256,256]{2,1,0:T(8,128)(2,1)}, u32[]{:S(2)}, u32[]{:S(2)}) collective-permute-start(bf16[2,256,256]{2,1,0:T(8,128)(2,1)S(1)} %pad_maximum_fusion.7), channel_id=1, source_target_pairs={{0,16},{16,32},{32,48},{48,64},{64,80},{80,96},{96,112},{112,0},{1... | collective-permute-start | bytes 786440 | tf_op jit(solution)/shard_map/ppermute | solution.py:17
  37.7 14.0 %all-to-all-start.3 = ((bf16[128,2,1536]{0,2,1:T(8,128)(2,1)}), bf16[128,2,1536]{0,2,1:T(8,128)(2,1)S(1)}, u32[]{:S(2)}, u32[]{:S(2)}) async-start(bf16[128,2,1536]{0,2,1:T(8,128)(2,1)} %bitcast.32), calls=%async_computation.3 | async-start | bytes 1572864 | tf_op jit(solution)/shard_map/all_to_all | solution.py:33
  43.6 20.9 %collective-permute-start.1 = (bf16[2,256,256]{2,1,0:T(8,128)(2,1)}, bf16[2,256,256]{2,1,0:T(8,128)(2,1)}, u32[]{:S(2)}, u32[]{:S(2)}) collective-permute-start(bf16[2,256,256]{2,1,0:T(8,128)(2,1)} %collective-permute-done), channel_id=1, source_target_pairs={{0,16},{16,32},{32,48},{48,64},{64,80},{80,96},{96,112},{112,0},{1... | collective-permute-start | bytes 786440 | tf_op jit(solution)/shard_map/ppermute | solution.py:17
  65.8 6.7 %collective-permute-start.2 = (bf16[2,256,256]{2,1,0:T(8,128)(2,1)}, bf16[2,256,256]{2,1,0:T(8,128)(2,1)S(1)}, u32[]{:S(2)}, u32[]{:S(2)}) collective-permute-start(bf16[2,256,256]{2,1,0:T(8,128)(2,1)} %collective-permute-done.1), channel_id=1, source_target_pairs={{0,16},{16,32},{32,48},{48,64},{64,80},{80,96},{96,112},{112,0},{1... | collective-permute-start | bytes 786440 | tf_op jit(solution)/shard_map/ppermute | solution.py:17
  72.7 5.8 %collective-permute-start.3 = (bf16[2,256,256]{2,1,0:T(8,128)(2,1)S(1)}, bf16[2,256,256]{2,1,0:T(8,128)(2,1)S(1)}, u32[]{:S(2)}, u32[]{:S(2)}) collective-permute-start(bf16[2,256,256]{2,1,0:T(8,128)(2,1)S(1)} %collective-permute-done.2), channel_id=1, source_target_pairs={{0,2},{2,4},{4,6},{6,8},{8,10},{10,12},{12,14},{14,0},{1,3},{3,5},... | collective-permute-start | bytes 786440 | tf_op jit(solution)/shard_map/ppermute | solution.py:17
  79.4 10.3 %collective-permute-start.4 = (bf16[2,256,256]{2,1,0:T(8,128)(2,1)}, bf16[2,256,256]{2,1,0:T(8,128)(2,1)S(1)}, u32[]{:S(2)}, u32[]{:S(2)}) collective-permute-start(bf16[2,256,256]{2,1,0:T(8,128)(2,1)} %copy-done.37), channel_id=1, source_target_pairs={{0,112},{16,0},{32,16},{48,32},{64,48},{80,64},{96,80},{112,96},{1... | collective-permute-start | bytes 786440 | tf_op jit(solution)/shard_map/ppermute | solution.py:17
  90.6 9.2 %collective-permute-start.5 = (bf16[2,256,256]{2,1,0:T(8,128)(2,1)}, bf16[2,256,256]{2,1,0:T(8,128)(2,1)S(1)}, u32[]{:S(2)}, u32[]{:S(2)}) collective-permute-start(bf16[2,256,256]{2,1,0:T(8,128)(2,1)} %copy-done.38), channel_id=1, source_target_pairs={{0,112},{16,0},{32,16},{48,32},{64,48},{80,64},{96,80},{112,96},{1... | collective-permute-start | bytes 786440 | tf_op jit(solution)/shard_map/ppermute | solution.py:17
  100.8 8.8 %collective-permute-start.6 = (bf16[2,256,256]{2,1,0:T(8,128)(2,1)}, bf16[2,256,256]{2,1,0:T(8,128)(2,1)S(1)}, u32[]{:S(2)}, u32[]{:S(2)}) collective-permute-start(bf16[2,256,256]{2,1,0:T(8,128)(2,1)} %copy-done.39), channel_id=1, source_target_pairs={{0,112},{16,0},{32,16},{48,32},{64,48},{80,64},{96,80},{112,96},{1... | collective-permute-start | bytes 786440 | tf_op jit(solution)/shard_map/ppermute | solution.py:17
  187.3 88.4 %all-to-all-start.4 = ((bf16[2,128,1536]{1,2,0:T(8,128)(2,1)}), bf16[2,128,1536]{1,2,0:T(8,128)(2,1)}, u32[]{:S(2)}, u32[]{:S(2)}) async-start(bf16[2,128,1536]{1,2,0:T(8,128)(2,1)} %copy.501), calls=%async_computation.4 | async-start | bytes 1572864 | tf_op jit(solution)/shard_map/all_to_all | solution.py:172
  193.1 25.4 %collective-permute-start.14 = (f32[2,256,256]{1,2,0:T(8,128)S(1)}, f32[2,256,256]{1,2,0:T(8,128)S(1)}, u32[]{:S(2)}, u32[]{:S(2)}) collective-permute-start(f32[2,256,256]{1,2,0:T(8,128)S(1)} %pad_maximum_fusion.5), channel_id=1, source_target_pairs={{0,112},{16,0},{32,16},{48,32},{64,48},{80,64},{96,80},{112,96},{1... | collective-permute-start | bytes 1572872 | tf_op jit(solution)/shard_map/ppermute | solution.py:17
  194.5 24.0 %collective-permute-start.12 = (f32[2,256,256]{1,2,0:T(8,128)S(1)}, f32[2,256,256]{1,2,0:T(8,128)S(1)}, u32[]{:S(2)}, u32[]{:S(2)}) collective-permute-start(f32[2,256,256]{1,2,0:T(8,128)S(1)} %pad_maximum_fusion.4), channel_id=1, source_target_pairs={{0,96},{16,112},{32,0},{48,16},{64,32},{80,48},{96,64},{112,80},{1... | collective-permute-start | bytes 1572872 | tf_op jit(solution)/shard_map/ppermute | solution.py:17
  196.4 22.1 %collective-permute-start.10 = (f32[2,256,256]{1,2,0:T(8,128)S(1)}, f32[2,256,256]{1,2,0:T(8,128)S(1)}, u32[]{:S(2)}, u32[]{:S(2)}) collective-permute-start(f32[2,256,256]{1,2,0:T(8,128)S(1)} %pad_maximum_fusion.3), channel_id=1, source_target_pairs={{0,80},{16,96},{32,112},{48,0},{64,16},{80,32},{96,48},{112,64},{1... | collective-permute-start | bytes 1572872 | tf_op jit(solution)/shard_map/ppermute | solution.py:17
  199.7 20.4 %collective-permute-start.9 = (f32[2,256,256]{1,2,0:T(8,128)S(1)}, f32[2,256,256]{1,2,0:T(8,128)S(1)}, u32[]{:S(2)}, u32[]{:S(2)}) collective-permute-start(f32[2,256,256]{1,2,0:T(8,128)S(1)} %pad_maximum_fusion.2), channel_id=1, source_target_pairs={{0,80},{16,96},{32,112},{48,0},{64,16},{80,32},{96,48},{112,64},{1... | collective-permute-start | bytes 1572872 | tf_op jit(solution)/shard_map/ppermute | solution.py:17
  200.8 54.1 %collective-permute-start.8 = (f32[2,256,256]{1,2,0:T(8,128)S(1)}, f32[2,256,256]{1,2,0:T(8,128)S(1)}, u32[]{:S(2)}, u32[]{:S(2)}) collective-permute-start(f32[2,256,256]{1,2,0:T(8,128)S(1)} %pad_maximum_fusion.1), channel_id=1, source_target_pairs={{0,96},{16,112},{32,0},{48,16},{64,32},{80,48},{96,64},{112,80},{1... | collective-permute-start | bytes 1572872 | tf_op jit(solution)/shard_map/ppermute | solution.py:17
  218.5 56.2 %collective-permute-start.7 = (f32[2,256,256]{1,2,0:T(8,128)S(1)}, f32[2,256,256]{1,2,0:T(8,128)S(1)}, u32[]{:S(2)}, u32[]{:S(2)}) collective-permute-start(f32[2,256,256]{1,2,0:T(8,128)S(1)} %pad_maximum_fusion), channel_id=1, source_target_pairs={{0,112},{16,0},{32,16},{48,32},{64,48},{80,64},{96,80},{112,96},{1... | collective-permute-start | bytes 1572872 | tf_op jit(solution)/shard_map/ppermute | solution.py:17
  218.5 56.2 %collective-permute-start.16 = (f32[2,256,256]{1,2,0:T(8,128)S(1)}, f32[2,256,256]{1,2,0:T(8,128)S(1)}, u32[]{:S(2)}, u32[]{:S(2)}) collective-permute-start(f32[2,256,256]{1,2,0:T(8,128)S(1)} %pad_maximum_fusion.6), channel_id=1, source_target_pairs={{0,14},{2,0},{4,2},{6,4},{8,6},{10,8},{12,10},{14,12},{1,15},{3,1}... | collective-permute-start | bytes 1572872 | tf_op jit(solution)/shard_map/ppermute | solution.py:17
  218.5 56.1 %collective-permute-start.15 = (f32[2,256,256]{1,2,0:T(8,128)S(1)}, f32[2,256,256]{1,2,0:T(8,128)S(1)}, u32[]{:S(2)}, u32[]{:S(2)}) collective-permute-start(f32[2,256,256]{1,2,0:T(8,128)S(1)} %collective-permute-done.14), channel_id=1, source_target_pairs={{0,14},{2,0},{4,2},{6,4},{8,6},{10,8},{12,10},{14,12},{1,15},{3,1}... | collective-permute-start | bytes 1572872 | tf_op jit(solution)/shard_map/ppermute | solution.py:17
  220.1 54.6 %collective-permute-start.13 = (f32[2,256,256]{1,2,0:T(8,128)S(1)}, f32[2,256,256]{1,2,0:T(8,128)S(1)}, u32[]{:S(2)}, u32[]{:S(2)}) collective-permute-start(f32[2,256,256]{1,2,0:T(8,128)S(1)} %collective-permute-done.12), channel_id=1, source_target_pairs={{0,14},{2,0},{4,2},{6,4},{8,6},{10,8},{12,10},{14,12},{1,15},{3,1}... | collective-permute-start | bytes 1572872 | tf_op jit(solution)/shard_map/ppermute | solution.py:17
  255.0 19.7 %collective-permute-start.11 = (f32[2,256,256]{1,2,0:T(8,128)S(1)}, f32[2,256,256]{1,2,0:T(8,128)S(1)}, u32[]{:S(2)}, u32[]{:S(2)}) collective-permute-start(f32[2,256,256]{1,2,0:T(8,128)S(1)} %collective-permute-done.10), channel_id=1, source_target_pairs={{0,14},{2,0},{4,2},{6,4},{8,6},{10,8},{12,10},{14,12},{1,15},{3,1}... | collective-permute-start | bytes 1572872 | tf_op jit(solution)/shard_map/ppermute | solution.py:17
  275.8 11.6 %all-to-all-start.6 = ((bf16[2,128,256]{2,1,0:T(8,128)(2,1)}), bf16[2,128,256]{2,1,0:T(8,128)(2,1)S(1)}, u32[]{:S(2)}, u32[]{:S(2)}) async-start(bf16[2,128,256]{2,1,0:T(8,128)(2,1)} %bitcast.148), calls=%async_computation.6 | async-start | bytes 262144 | tf_op jit(solution)/shard_map/all_to_all | solution.py:174
  287.3 9.3 %all-to-all-start.5 = ((bf16[2,128,256]{2,1,0:T(8,128)(2,1)}), bf16[2,128,256]{2,1,0:T(8,128)(2,1)S(1)}, u32[]{:S(2)}, u32[]{:S(2)}) async-start(bf16[2,128,256]{2,1,0:T(8,128)(2,1)} %bitcast.145), calls=%async_computation.5 | async-start | bytes 262144 | tf_op jit(solution)/shard_map/all_to_all | solution.py:173
  (42 other events, 318.4 us)
where the time goes:
time: 302 us; the launch traced here: 298 us
  waiting for transfers between devices  118 us (39%)
  matrix products  70.5 us (23%)
  local copies, waits for them, and re-layouts  39.5 us (13%)
  starting transfers between devices  39 us (13%)
  other arithmetic  28.7 us (10%)
    ppermute x17, waiting for transfers between devices, from_behind(): lax.ppermute(value, axis, [(i, (i + by) % peers) for i in range(peers)])  93.6 us
    dot_general x8, matrix products, masked_scores(): jnp.einsum('qhgd,khd->hgqk', query_head_rows, keys_here, preferred_elemen...  21.1 us
    dot_general x8, matrix products, grad_products(): jnp.einsum('qhgd,khd->hgqk', gradient_head_list, values_here, preferred_e...  19.7 us
    convert_element_type x1, other arithmetic, grad_block(): (weights * (grad_dot - row_dot[..., None])).astype(jnp.bfloat16)  19.6 us
    unnamed x91, local copies, waits for them, and re-layouts  12.9 us
    ppermute x17, starting transfers between devices, from_behind(): lax.ppermute(value, axis, [(i, (i + by) % peers) for i in range(peers)])  11.7 us
    dot_general x8, matrix products, grad_block(): jnp.einsum('emts,temc->sec', score_gradient, query_head_rows, preferred_e...  11.6 us
    all_to_all x1, waiting for transfers between devices, shards(): lax.all_to_all(queries, 'head', split_axis=1, concat_axis=0, tiled=True)  10.4 us
  transfers between devices with their start and end apart: 24, of which 15 were waited for; matrix products, arithmetic and copies ran while one was open for 18% of the time, Pallas kernels for 0%

commit v1 on v0

v1 whole, which is shorter than its diff:
```python
import functools
import math

import jax
import jax.numpy as jnp
from jax import lax
from jax.experimental import pallas as pl
from jax.experimental.pallas import tpu as pltpu
from jax.sharding import PartitionSpec as P

HEAD = 128
GROUP = 6
KV = 2
WIN = 4
SPAN = 128
COLS = 2 * GROUP * HEAD
Y = 4
NEG = -1e30
SCALE = 1.0 / math.sqrt(HEAD)
SCALE2 = SCALE * math.log2(math.e)
NT = (((1,), (1,)), ((), ()))
NN = (((1,), (0,)), ((), ()))


def dot(a, b, dims):
    return lax.dot_general(a, b, dims, preferred_element_type=jnp.float32)


def attention_kernel(order, q_own, q_far, do_own, do_far, *refs):
    kv = refs[:8]
    dq_own, dq_far = refs[8:10]
    dkv = refs[10:18]
    s_scr, dp_scr, p_scr, ds_scr, kt_scr, q_scr, do_scr = refs[18:]
    inner, outer, head = lax.axis_index("inner"), lax.axis_index("outer"), lax.axis_index("head")

    def span_of(d, o, half):
        block = lax.rem(inner + 8 - d, 8) * 8 + lax.rem(outer + 8 - o, 8)
        return order[block * 2 + (head if half == 0 else 1 - head)]

    lane = lax.broadcasted_iota(jnp.int32, (1, 256), 1)
    at = [span_of(0, 0, 0), span_of(0, 0, 1)]
    hidden = []
    for n in range(8):
        for half in range(2):
            key = span_of(n % WIN, n // WIN, half)
            first = jnp.where(key <= at[0], 0.0, -NEG)
            second = jnp.where(key <= at[1], 0.0, -NEG)
            hidden.append(jnp.where(lane < SPAN, first, second).astype(jnp.float32))
    row = lax.broadcasted_iota(jnp.int32, (256, 256), 0)
    col = lax.broadcasted_iota(jnp.int32, (256, 256), 1)
    key_pos = jnp.where(row < SPAN, at[0], at[1]) * SPAN + (row & (SPAN - 1))
    row_pos = jnp.where(col < SPAN, at[0], at[1]) * SPAN + (col & (SPAN - 1))
    own_visible = key_pos <= row_pos

    for j in range(KV):
        k_at = slice(j * HEAD, (j + 1) * HEAD)
        v_at = slice((KV + j) * HEAD, (KV + j + 1) * HEAD)
        for n in range(8):
            kt_scr[:, n * 256 : (n + 1) * 256] = kv[n][:, k_at].T

        def one_head(g, carry):
            at_h = pl.ds(pl.multiple_of((j * GROUP + g) * HEAD, HEAD), HEAD)
            rows = pl.ds(pl.multiple_of(g * 256, 256), 256)
            q_h = jnp.concatenate([q_own[:, at_h], q_far[:, at_h]], axis=0)
            do_h = jnp.concatenate([do_own[:, at_h], do_far[:, at_h]], axis=0)
            q_scr[rows, :] = q_h
            do_scr[rows, :] = do_h
            top = jnp.full((1, 256), NEG, jnp.float32)
            for n in range(8):
                s = dot(kv[n][:, k_at], q_h, NT)
                if n == 0:
                    s = jnp.where(own_visible, s, NEG)
                s_scr[n * 256 : (n + 1) * 256, :] = s
                for half in range(2):
                    here = jnp.max(s[half * 128 : (half + 1) * 128], axis=0, keepdims=True)
                    top = jnp.maximum(top, here - hidden[2 * n + half] if n else here)
            top = top * SCALE2
            total = jnp.zeros((8, 256), jnp.float32)
            row_dot = jnp.zeros((8, 256), jnp.float32)
            for n in range(8):
                dp = dot(kv[n][:, v_at], do_h, NT)
                dp_scr[n * 256 : (n + 1) * 256, :] = dp
                for half in range(2):
                    at_r = slice(n * 256 + half * 128, n * 256 + half * 128 + 128)
                    lower = top + hidden[2 * n + half] if n else top
                    e = jnp.exp2(s_scr[at_r, :] * SCALE2 - lower)
                    s_scr[at_r, :] = e
                    total = total + jnp.sum(e.reshape(16, 8, 256), axis=0)
                    product = e * dp[half * 128 : (half + 1) * 128]
                    row_dot = row_dot + jnp.sum(product.reshape(16, 8, 256), axis=0)
            inverse = 1.0 / jnp.sum(total, axis=0, keepdims=True)
            row_dot = jnp.sum(row_dot, axis=0, keepdims=True) * inverse
            dq_t = jnp.zeros((HEAD, 256), jnp.float32)
            for n in range(8):
                at_r = slice(n * 256, (n + 1) * 256)
                p = s_scr[at_r, :] * inverse
                ds = (p * (dp_scr[at_r, :] - row_dot)).astype(jnp.bfloat16)
                p_scr[at_r, rows] = p.astype(jnp.bfloat16)
                ds_scr[at_r, rows] = ds
                dq_t = dq_t + dot(kt_scr[:, at_r], ds, NN)
            dq = (dq_t * SCALE).T.astype(jnp.bfloat16)
            dq_own[:, at_h] = dq[:SPAN]
            dq_far[:, at_h] = dq[SPAN:]
            return carry

        lax.fori_loop(0, GROUP, one_head, 0)
        for n in range(8):
            at_r = slice(n * 256, (n + 1) * 256)
            dk = dot(ds_scr[at_r, :], q_scr[...], NN) * SCALE
            dv = dot(p_scr[at_r, :], do_scr[...], NN)
            dkv[n][:, k_at] = dk.astype(jnp.bfloat16)
            dkv[n][:, v_at] = dv.astype(jnp.bfloat16)


def attention(order, q_own, q_far, do_own, do_far, blocks):
    vmem = pl.BlockSpec(memory_space=pltpu.VMEM)
    rows = jax.ShapeDtypeStruct((SPAN, COLS), jnp.bfloat16)
    block = jax.ShapeDtypeStruct((256, 512), jnp.bfloat16)
    out = pl.pallas_call(
        attention_kernel,
        in_specs=[pl.BlockSpec(memory_space=pltpu.SMEM)] + [vmem] * 12,
        out_specs=[vmem] * 10,
        out_shape=[rows] * 2 + [block] * 8,
        scratch_shapes=[
            pltpu.VMEM((2048, 256), jnp.float32),
            pltpu.VMEM((2048, 256), jnp.float32),
            pltpu.VMEM((2048, GROUP * 256), jnp.bfloat16),
            pltpu.VMEM((2048, GROUP * 256), jnp.bfloat16),
            pltpu.VMEM((HEAD, 2048), jnp.bfloat16),
            pltpu.VMEM((GROUP * 256, HEAD), jnp.bfloat16),
            pltpu.VMEM((GROUP * 256, HEAD), jnp.bfloat16),
        ],
        compiler_params=pltpu.CompilerParams(vmem_limit_bytes=48 * 1024 * 1024),
        cost_estimate=pl.CostEstimate(
            flops=10 * 12 * 256 * 2048 * 128, bytes_accessed=10_000_000, transcendentals=12 * 256 * 2048
        ),
    )(order, q_own, q_far, do_own, do_far, *blocks)
    return out[0], out[1], out[2:]


def to_partner(x):
    return lax.ppermute(x, "head", [(0, 1), (1, 0)])


def to_column(x, flip, rows=(0, 1, 2, 3)):
    perm = []
    for lo in range(2):
        for y in rows:
            for h in range(2):
                perm.append(((lo * Y + y) * 2 + h, ((1 - lo) * Y + y) * 2 + (h ^ flip)))
    return lax.ppermute(x, ("inner", "head"), perm)


def along_y(x, by):
    return lax.ppermute(
        x, "inner", [(lo * Y + y, lo * Y + (y + by) % Y) for lo in range(2) for y in range(Y)]
    )


def along_outer(x, by):
    return lax.ppermute(x, "outer", [(o, (o + by) % 8) for o in range(8)])


def f32(x):
    return x.astype(jnp.float32)


def shards(queries, keys, values, output_gradient, span_order):
    head = lax.axis_index("head")
    y = lax.rem(lax.axis_index("inner"), Y)

    def cols(x, of, width):
        return lax.dynamic_slice_in_dim(x, of * width, width, axis=1)

    def piece(of):
        return jnp.concatenate([cols(keys, of, 256), cols(values, of, 256)], axis=1)

    mine, theirs = piece(head), piece(1 - head)
    own = jnp.concatenate([mine, to_partner(theirs)], axis=0)
    other = jnp.concatenate([to_column(mine, 0, (1, 2, 3)), to_column(theirs, 1, (1, 2, 3))], axis=0)
    q_own, do_own = cols(queries, head, COLS), cols(output_gradient, head, COLS)
    q_far = to_partner(cols(queries, 1 - head, COLS))
    do_far = to_partner(cols(output_gradient, 1 - head, COLS))

    blocks = [own] + [along_y(jnp.where(y + k >= Y, other, own), k) for k in (1, 2, 3)]
    blocks = blocks + [along_outer(b, 1) for b in blocks]
    dq_own, dq_far, terms = attention(span_order, q_own, q_far, do_own, do_far, blocks)

    dq_back = to_partner(dq_far)
    sums = [
        (f32(terms[k]) + f32(along_outer(terms[WIN + k], -1))).astype(jnp.bfloat16)
        for k in range(WIN)
    ]
    own_sum = f32(sums[0])
    other_sum = jnp.zeros_like(own_sum)
    for k in (1, 2, 3):
        arrived = f32(along_y(sums[k], -k))
        own_sum = own_sum + jnp.where(y + k < Y, arrived, 0.0)
        other_sum = other_sum + jnp.where(y + k < Y, 0.0, arrived)
    other_sum = other_sum.astype(jnp.bfloat16)
    mine_sum = own_sum[:SPAN] + f32(to_column(other_sum[:SPAN], 0, (1, 2, 3)))
    theirs_sum = f32(to_partner(own_sum[SPAN:].astype(jnp.bfloat16))) + f32(
        to_column(other_sum[SPAN:], 1, (1, 2, 3))
    )
    mine_sum, theirs_sum = mine_sum.astype(jnp.bfloat16), theirs_sum.astype(jnp.bfloat16)

    def join(a, b):
        return jnp.where(
            head == 0, jnp.concatenate([a, b], axis=1), jnp.concatenate([b, a], axis=1)
        )

    return (
        join(dq_own, dq_back),
        join(mine_sum[:, :256], theirs_sum[:, :256]),
        join(mine_sum[:, 256:], theirs_sum[:, 256:]),
    )


def solution(mesh):
    rows = P(("inner", "outer", "head"), None)
    return jax.shard_map(
        shards,
        mesh=mesh,
        in_specs=(rows, rows, rows, rows, P()),
        out_specs=(rows, rows, rows),
        check_vma=False,
    )
```

time: 302 us -> 114 us (0.38)
  the two profiles are of different devices: /device:TPU:58 before, /device:TPU:16 now
where the time goes in v1:
time: 114 us
  starting transfers between devices  40.2 us (35%)
  waiting for transfers between devices  37.6 us (33%)
  Pallas kernels  30.6 us (27%)
  other arithmetic  3.18 us (3%)
  local copies, waits for them, and re-layouts  1.57 us (1%)
    pallas_call x1, Pallas kernels, attention(): pl.pallas_call(attention_kernel, in_specs=[pl.BlockSpec(memory_space=pltp...  30.6 us
    ppermute x4, starting transfers between devices, to_column(): return lax.ppermute(x, ('inner', 'head'), perm)  14.5 us
    ppermute x6, starting transfers between devices, along_y(): lax.ppermute(x, 'inner', [(lo * Y + y, lo * Y + (y + by) % Y) for lo in r...  12.9 us
    ppermute x6, waiting for transfers between devices, along_y(): lax.ppermute(x, 'inner', [(lo * Y + y, lo * Y + (y + by) % Y) for lo in r...  12.5 us
    ppermute x4, waiting for transfers between devices, to_column(): return lax.ppermute(x, ('inner', 'head'), perm)  9.36 us
    ppermute x5, waiting for transfers between devices, to_partner(): return lax.ppermute(x, 'head', [(0, 1), (1, 0)])  8.17 us
    ppermute x8, waiting for transfers between devices, along_outer(): return lax.ppermute(x, 'outer', [(o, (o + by) % 8) for o in range(8)])  7.58 us
    ppermute x5, starting transfers between devices, to_partner(): return lax.ppermute(x, 'head', [(0, 1), (1, 0)])  7.36 us
  transfers between devices with their start and end apart: 23, of which 14 were waited for; matrix products, arithmetic and copies ran while one was open for 2% of the time, Pallas kernels for 0%

profile of v1, /device:TPU:16, one launch (start us, length us, event | category | flops | bytes accessed | tf_op | source)
XLA Modules:
  0.0 114.0 jit_solution(6328670482870986999)
XLA Ops:
  1.6 3.4 %collective-permute-start.3 = (bf16[128,512]{1,0:T(8,128)(2,1)S(1)}, bf16[128,512]{1,0:T(8,128)(2,1)S(1)}, u32[]{:S(2)}, u32[]{:S(2)}) collective-permute-start(bf16[128,512]{1,0:T(8,128)(2,1)S(1)} %pad_maximum_fusion.1), channel_id=1, source_target_pairs={{16,80},{17,81},{32,96},{33,97},{48,112},{49,113},{80,16},{81,17},... | collective-permute-start | bytes 393224 | tf_op jit(solution)/shard_map/ppermute | solution.py:151
  5.0 4.0 %collective-permute-start.4 = (bf16[128,512]{1,0:T(8,128)(2,1)S(1)}, bf16[128,512]{1,0:T(8,128)(2,1)S(1)}, u32[]{:S(2)}, u32[]{:S(2)}) collective-permute-start(bf16[128,512]{1,0:T(8,128)(2,1)S(1)} %pad_maximum_fusion.2), channel_id=1, source_target_pairs={{16,81},{17,80},{32,97},{33,96},{48,113},{49,112},{80,17},{81,16},... | collective-permute-start | bytes 393224 | tf_op jit(solution)/shard_map/ppermute | solution.py:151
  9.8 6.1 %collective-permute-done.4 = bf16[128,512]{1,0:T(8,128)(2,1)S(1)} collective-permute-done((bf16[128,512]{1,0:T(8,128)(2,1)S(1)}, bf16[128,512]{1,0:T(8,128)(2,1)S(1)}, u32[]{:S(2)}, u32[]{:S(2)}) %collective-permute-start.4) | collective-permute-done | bytes 131104 | tf_op jit(solution)/shard_map/ppermute | solution.py:151
  17.1 1.6 %collective-permute-start = (bf16[128,1536]{1,0:T(8,128)(2,1)S(1)}, bf16[128,1536]{1,0:T(8,128)(2,1)S(1)}, u32[]{:S(2)}, u32[]{:S(2)}) collective-permute-start(bf16[128,1536]{1,0:T(8,128)(2,1)S(1)} %get-tuple-element.27), channel_id=1, source_target_pairs={{0,1},{1,0},{2,3},{3,2},{4,5},{5,4},{6,7},{7,6},{8,9},{9,8},{10,11... | collective-permute-start | bytes 1179656 | tf_op jit(solution)/shard_map/ppermute | solution.py:142
  18.7 2.5 %collective-permute-start.6 = (bf16[256,512]{1,0:T(8,128)(2,1)S(1)}, bf16[256,512]{1,0:T(8,128)(2,1)S(1)}, u32[]{:S(2)}, u32[]{:S(2)}) collective-permute-start(bf16[256,512]{1,0:T(8,128)(2,1)S(1)} %get-tuple-element.30), channel_id=1, source_target_pairs={{0,32},{16,48},{32,0},{48,16},{64,96},{80,112},{96,64},{112,80},{1... | collective-permute-start | bytes 786440 | tf_op jit(solution)/shard_map/ppermute | solution.py:155
  21.3 3.8 %collective-permute-done.7.refs_3_ = bf16[256,512]{1,0:T(8,128)(2,1)S(1)} collective-permute-done((bf16[256,512]{1,0:T(8,128)(2,1)S(1)}, bf16[256,512]{1,0:T(8,128)(2,1)S(1)}, u32[]{:S(2)}, u32[]{:S(2)}) %collective-permute-start.7) | collective-permute-done | bytes 262176 | tf_op jit(solution)/shard_map/ppermute | solution.py:155
  26.2 1.5 %collective-permute-done.6.refs_2_ = bf16[256,512]{1,0:T(8,128)(2,1)S(1)} collective-permute-done((bf16[256,512]{1,0:T(8,128)(2,1)S(1)}, bf16[256,512]{1,0:T(8,128)(2,1)S(1)}, u32[]{:S(2)}, u32[]{:S(2)}) %collective-permute-start.6) | collective-permute-done | bytes 262176 | tf_op jit(solution)/shard_map/ppermute | solution.py:155
  27.7 2.7 %collective-permute-done.5.refs_1_ = bf16[256,512]{1,0:T(8,128)(2,1)S(1)} collective-permute-done((bf16[256,512]{1,0:T(8,128)(2,1)S(1)}, bf16[256,512]{1,0:T(8,128)(2,1)S(1)}, u32[]{:S(2)}, u32[]{:S(2)}) %collective-permute-start.5) | collective-permute-done | bytes 262176 | tf_op jit(solution)/shard_map/ppermute | solution.py:155
  30.4 2.0 %collective-permute-start.9 = (bf16[256,512]{1,0:T(8,128)(2,1)S(1)}, bf16[256,512]{1,0:T(8,128)(2,1)S(1)}, u32[]{:S(2)}, u32[]{:S(2)}) collective-permute-start(bf16[256,512]{1,0:T(8,128)(2,1)S(1)} %collective-permute-done.5.refs_1_), channel_id=1, source_target_pairs={{0,2},{2,4},{4,6},{6,8},{8,10},{10,12},{12,14},{14,0},{1,3},{3,5},... | collective-permute-start | bytes 786440 | tf_op jit(solution)/shard_map/ppermute | solution.py:161
  32.4 3.7 %collective-permute-done.1.do_far = bf16[128,1536]{1,0:T(8,128)(2,1)S(1)} collective-permute-done((bf16[128,1536]{1,0:T(8,128)(2,1)S(1)}, bf16[128,1536]{1,0:T(8,128)(2,1)S(1)}, u32[]{:S(2)}, u32[]{:S(2)}) %collective-permute-start.1) | collective-permute-done | bytes 393248 | tf_op jit(solution)/shard_map/ppermute | solution.py:142
  37.5 2.8 %collective-permute-done.9.refs_5_ = bf16[256,512]{1,0:T(8,128)(2,1)S(1)} collective-permute-done((bf16[256,512]{1,0:T(8,128)(2,1)S(1)}, bf16[256,512]{1,0:T(8,128)(2,1)S(1)}, u32[]{:S(2)}, u32[]{:S(2)}) %collective-permute-start.9) | collective-permute-done | bytes 262176 | tf_op jit(solution)/shard_map/ppermute | solution.py:161
  40.3 30.6 %shard_map.76 = (bf16[128,1536]{1,0:T(8,128)(2,1)S(1)}, bf16[128,1536]{1,0:T(8,128)(2,1)S(1)}, bf16[256,512]{1,0:T(8,128)(2,1)S(1)}, bf16[256,512]{1,0:T(8,128)(...) custom-call(s32[128]{0:T(128)S(1)} %copy-done, ...), custom_call_target="tpu_custom_call" | custom-call | flops 8053063680 | bytes 10000000 | tf_op jit(solution)/shard_map/pallas_call | solution.py:119
  70.9 2.9 %collective-permute-start.16 = (bf16[256,512]{1,0:T(8,128)(2,1)S(1)}, bf16[256,512]{1,0:T(8,128)(2,1)S(1)}, u32[]{:S(2)}, u32[]{:S(2)}) collective-permute-start(bf16[256,512]{1,0:T(8,128)(2,1)S(1)} %get-tuple-element.20), channel_id=1, source_target_pairs={{0,14},{2,0},{4,2},{6,4},{8,6},{10,8},{12,10},{14,12},{1,15},{3,1}... | collective-permute-start | bytes 786440 | tf_op jit(solution)/shard_map/ppermute | solution.py:161
  74.9 1.8 %collective-permute-start.15 = (bf16[256,512]{1,0:T(8,128)(2,1)S(1)}, bf16[256,512]{1,0:T(8,128)(2,1)S(1)}, u32[]{:S(2)}, u32[]{:S(2)}) collective-permute-start(bf16[256,512]{1,0:T(8,128)(2,1)S(1)} %add_convert_fusion.2), channel_id=1, source_target_pairs={{0,48},{16,0},{32,16},{48,32},{64,112},{80,64},{96,80},{112,96},{1... | collective-permute-start | bytes 786440 | tf_op jit(solution)/shard_map/ppermute | solution.py:155
  77.8 3.7 %collective-permute-start.17 = (bf16[256,512]{1,0:T(8,128)(2,1)S(1)}, bf16[256,512]{1,0:T(8,128)(2,1)S(1)}, u32[]{:S(2)}, u32[]{:S(2)}) collective-permute-start(bf16[256,512]{1,0:T(8,128)(2,1)S(1)} %add_convert_fusion.1), channel_id=1, source_target_pairs={{0,32},{16,48},{32,0},{48,16},{64,96},{80,112},{96,64},{112,80},{1... | collective-permute-start | bytes 786440 | tf_op jit(solution)/shard_map/ppermute | solution.py:155
  81.5 1.9 %collective-permute-done.18 = bf16[256,512]{1,0:T(8,128)(2,1)S(1)} collective-permute-done((bf16[256,512]{1,0:T(8,128)(2,1)S(1)}, bf16[256,512]{1,0:T(8,128)(2,1)S(1)}, u32[]{:S(2)}, u32[]{:S(2)}) %collective-permute-start.18) | collective-permute-done | bytes 262176 | tf_op jit(solution)/shard_map/ppermute | solution.py:161
  83.4 4.4 %collective-permute-start.19 = (bf16[256,512]{1,0:T(8,128)(2,1)S(1)}, bf16[256,512]{1,0:T(8,128)(2,1)S(1)}, u32[]{:S(2)}, u32[]{:S(2)}) collective-permute-start(bf16[256,512]{1,0:T(8,128)(2,1)S(1)} %add_convert_fusion), channel_id=1, source_target_pairs={{0,16},{16,32},{32,48},{48,0},{64,80},{80,96},{96,112},{112,64},{1... | collective-permute-start | bytes 786440 | tf_op jit(solution)/shard_map/ppermute | solution.py:155
  87.8 1.9 %collective-permute-start.12 = (bf16[128,1536]{1,0:T(8,128)(2,1)S(1)}, bf16[128,1536]{1,0:T(8,128)(2,1)S(1)}, u32[]{:S(2)}, u32[]{:S(2)}) collective-permute-start(bf16[128,1536]{1,0:T(8,128)(2,1)S(1)} %get-tuple-element.14), channel_id=1, source_target_pairs={{0,1},{1,0},{2,3},{3,2},{4,5},{5,4},{6,7},{7,6},{8,9},{9,8},{10,11... | collective-permute-start | bytes 1179656 | tf_op jit(solution)/shard_map/ppermute | solution.py:142
  89.8 4.6 %collective-permute-done.19 = bf16[256,512]{1,0:T(8,128)(2,1)S(1)} collective-permute-done((bf16[256,512]{1,0:T(8,128)(2,1)S(1)}, bf16[256,512]{1,0:T(8,128)(2,1)S(1)}, u32[]{:S(2)}, u32[]{:S(2)}) %collective-permute-start.19) | collective-permute-done | bytes 262176 | tf_op jit(solution)/shard_map/ppermute | solution.py:155
  94.7 3.5 %collective-permute-start.20 = (bf16[128,512]{1,0:T(8,128)(2,1)S(1)}, bf16[128,512]{1,0:T(8,128)(2,1)S(1)}, u32[]{:S(2)}, u32[]{:S(2)}) collective-permute-start(bf16[128,512]{1,0:T(8,128)(2,1)S(1)} %get-tuple-element.32), channel_id=1, source_target_pairs={{16,80},{17,81},{32,96},{33,97},{48,112},{49,113},{80,16},{81,17},... | collective-permute-start | bytes 393224 | tf_op jit(solution)/shard_map/ppermute | solution.py:151
  98.2 3.1 %collective-permute-done.12 = bf16[128,1536]{1,0:T(8,128)(2,1)S(1)} collective-permute-done((bf16[128,1536]{1,0:T(8,128)(2,1)S(1)}, bf16[128,1536]{1,0:T(8,128)(2,1)S(1)}, u32[]{:S(2)}, u32[]{:S(2)}) %collective-permute-start.12) | collective-permute-done | bytes 393248 | tf_op jit(solution)/shard_map/ppermute | solution.py:142
  102.4 2.0 %collective-permute-start.21 = (bf16[128,512]{1,0:T(8,128)(2,1)S(1)}, bf16[128,512]{1,0:T(8,128)(2,1)S(1)}, u32[]{:S(2)}, u32[]{:S(2)}) collective-permute-start(bf16[128,512]{1,0:T(8,128)(2,1)S(1)} %slice.45), channel_id=1, source_target_pairs={{0,1},{1,0},{2,3},{3,2},{4,5},{5,4},{6,7},{7,6},{8,9},{9,8},{10,11... | collective-permute-start | bytes 393224 | tf_op jit(solution)/shard_map/ppermute | solution.py:142
  104.4 3.5 %collective-permute-start.22 = (bf16[128,512]{1,0:T(8,128)(2,1)S(1)}, bf16[128,512]{1,0:T(8,128)(2,1)S(1)}, u32[]{:S(2)}, u32[]{:S(2)}) collective-permute-start(bf16[128,512]{1,0:T(8,128)(2,1)S(1)} %get-tuple-element.33), channel_id=1, source_target_pairs={{16,81},{17,80},{32,97},{33,96},{48,113},{49,112},{80,17},{81,16},... | collective-permute-start | bytes 393224 | tf_op jit(solution)/shard_map/ppermute | solution.py:151
  109.3 3.2 %collective-permute-done.22 = bf16[128,512]{1,0:T(8,128)(2,1)S(1)} collective-permute-done((bf16[128,512]{1,0:T(8,128)(2,1)S(1)}, bf16[128,512]{1,0:T(8,128)(2,1)S(1)}, u32[]{:S(2)}, u32[]{:S(2)}) %collective-permute-start.22) | collective-permute-done | bytes 131104 | tf_op jit(solution)/shard_map/ppermute | solution.py:151
  (52 shorter events, 11.9 us)
Async XLA Ops:
  1.6 8.2 %collective-permute-start.3 = (bf16[128,512]{1,0:T(8,128)(2,1)S(1)}, bf16[128,512]{1,0:T(8,128)(2,1)S(1)}, u32[]{:S(2)}, u32[]{:S(2)}) collective-permute-start(bf16[128,512]{1,0:T(8,128)(2,1)S(1)} %pad_maximum_fusion.1), channel_id=1, source_target_pairs={{16,80},{17,81},{32,96},{33,97},{48,112},{49,113},{80,16},{81,17},... | collective-permute-start | bytes 393224 | tf_op jit(solution)/shard_map/ppermute | solution.py:151
  5.0 10.9 %collective-permute-start.4 = (bf16[128,512]{1,0:T(8,128)(2,1)S(1)}, bf16[128,512]{1,0:T(8,128)(2,1)S(1)}, u32[]{:S(2)}, u32[]{:S(2)}) collective-permute-start(bf16[128,512]{1,0:T(8,128)(2,1)S(1)} %pad_maximum_fusion.2), channel_id=1, source_target_pairs={{16,81},{17,80},{32,97},{33,96},{48,113},{49,112},{80,17},{81,16},... | collective-permute-start | bytes 393224 | tf_op jit(solution)/shard_map/ppermute | solution.py:151
  9.1 6.9 %collective-permute-start.2 = (bf16[128,512]{1,0:T(8,128)(2,1)S(1)}, bf16[128,512]{1,0:T(8,128)(2,1)S(1)}, u32[]{:S(2)}, u32[]{:S(2)}) collective-permute-start(bf16[128,512]{1,0:T(8,128)(2,1)S(1)} %pad_maximum_fusion.2), channel_id=1, source_target_pairs={{0,1},{1,0},{2,3},{3,2},{4,5},{5,4},{6,7},{7,6},{8,9},{9,8},{10,11... | collective-permute-start | bytes 393224 | tf_op jit(solution)/shard_map/ppermute | solution.py:142
  16.1 9.0 %collective-permute-start.7 = (bf16[256,512]{1,0:T(8,128)(2,1)S(1)}, bf16[256,512]{1,0:T(8,128)(2,1)S(1)}, u32[]{:S(2)}, u32[]{:S(2)}) collective-permute-start(bf16[256,512]{1,0:T(8,128)(2,1)S(1)} %get-tuple-element.29), channel_id=1, source_target_pairs={{0,48},{16,0},{32,16},{48,32},{64,112},{80,64},{96,80},{112,96},{1... | collective-permute-start | bytes 786440 | tf_op jit(solution)/shard_map/ppermute | solution.py:155
  17.1 15.3 %collective-permute-start = (bf16[128,1536]{1,0:T(8,128)(2,1)S(1)}, bf16[128,1536]{1,0:T(8,128)(2,1)S(1)}, u32[]{:S(2)}, u32[]{:S(2)}) collective-permute-start(bf16[128,1536]{1,0:T(8,128)(2,1)S(1)} %get-tuple-element.27), channel_id=1, source_target_pairs={{0,1},{1,0},{2,3},{3,2},{4,5},{5,4},{6,7},{7,6},{8,9},{9,8},{10,11... | collective-permute-start | bytes 1179656 | tf_op jit(solution)/shard_map/ppermute | solution.py:142
  18.7 9.0 %collective-permute-start.6 = (bf16[256,512]{1,0:T(8,128)(2,1)S(1)}, bf16[256,512]{1,0:T(8,128)(2,1)S(1)}, u32[]{:S(2)}, u32[]{:S(2)}) collective-permute-start(bf16[256,512]{1,0:T(8,128)(2,1)S(1)} %get-tuple-element.30), channel_id=1, source_target_pairs={{0,32},{16,48},{32,0},{48,16},{64,96},{80,112},{96,64},{112,80},{1... | collective-permute-start | bytes 786440 | tf_op jit(solution)/shard_map/ppermute | solution.py:155
  21.2 9.1 %collective-permute-start.5 = (bf16[256,512]{1,0:T(8,128)(2,1)S(1)}, bf16[256,512]{1,0:T(8,128)(2,1)S(1)}, u32[]{:S(2)}, u32[]{:S(2)}) collective-permute-start(bf16[256,512]{1,0:T(8,128)(2,1)S(1)} %get-tuple-element.31), channel_id=1, source_target_pairs={{0,16},{16,32},{32,48},{48,0},{64,80},{80,96},{96,112},{112,64},{1... | collective-permute-start | bytes 786440 | tf_op jit(solution)/shard_map/ppermute | solution.py:155
  21.2 19.1 %copy-start = (s32[128]{0:T(128)S(1)}, s32[128]{0:T(128)}, u32[]{:S(2)}) copy-start(s32[128]{0:T(128)} %order.1) | copy-start | bytes 1540
  21.3 9.1 %collective-permute-start.8 = (bf16[256,512]{1,0:T(8,128)(2,1)S(1)}, bf16[256,512]{1,0:T(8,128)(2,1)S(1)}, u32[]{:S(2)}, u32[]{:S(2)}) collective-permute-start(bf16[256,512]{1,0:T(8,128)(2,1)S(1)} %get-tuple-element.34.refs_0_), channel_id=1, source_target_pairs={{0,2},{2,4},{4,6},{6,8},{8,10},{10,12},{12,14},{14,0},{1,3},{3,5},... | collective-permute-start | bytes 786440 | tf_op jit(solution)/shard_map/ppermute | solution.py:161
  25.1 11.0 %collective-permute-start.1 = (bf16[128,1536]{1,0:T(8,128)(2,1)S(1)}, bf16[128,1536]{1,0:T(8,128)(2,1)S(1)}, u32[]{:S(2)}, u32[]{:S(2)}) collective-permute-start(bf16[128,1536]{1,0:T(8,128)(2,1)S(1)} %get-tuple-element.25), channel_id=1, source_target_pairs={{0,1},{1,0},{2,3},{3,2},{4,5},{5,4},{6,7},{7,6},{8,9},{9,8},{10,11... | collective-permute-start | bytes 1179656 | tf_op jit(solution)/shard_map/ppermute | solution.py:142
  27.7 8.5 %collective-permute-start.11 = (bf16[256,512]{1,0:T(8,128)(2,1)S(1)}, bf16[256,512]{1,0:T(8,128)(2,1)S(1)}, u32[]{:S(2)}, u32[]{:S(2)}) collective-permute-start(bf16[256,512]{1,0:T(8,128)(2,1)S(1)} %collective-permute-done.7.refs_3_), channel_id=1, source_target_pairs={{0,2},{2,4},{4,6},{6,8},{8,10},{10,12},{12,14},{14,0},{1,3},{3,5},... | collective-permute-start | bytes 786440 | tf_op jit(solution)/shard_map/ppermute | solution.py:161
  30.4 7.1 %collective-permute-start.10 = (bf16[256,512]{1,0:T(8,128)(2,1)S(1)}, bf16[256,512]{1,0:T(8,128)(2,1)S(1)}, u32[]{:S(2)}, u32[]{:S(2)}) collective-permute-start(bf16[256,512]{1,0:T(8,128)(2,1)S(1)} %collective-permute-done.6.refs_2_), channel_id=1, source_target_pairs={{0,2},{2,4},{4,6},{6,8},{8,10},{10,12},{12,14},{14,0},{1,3},{3,5},... | collective-permute-start | bytes 786440 | tf_op jit(solution)/shard_map/ppermute | solution.py:161
  30.4 9.9 %collective-permute-start.9 = (bf16[256,512]{1,0:T(8,128)(2,1)S(1)}, bf16[256,512]{1,0:T(8,128)(2,1)S(1)}, u32[]{:S(2)}, u32[]{:S(2)}) collective-permute-start(bf16[256,512]{1,0:T(8,128)(2,1)S(1)} %collective-permute-done.5.refs_1_), channel_id=1, source_target_pairs={{0,2},{2,4},{4,6},{6,8},{8,10},{10,12},{12,14},{14,0},{1,3},{3,5},... | collective-permute-start | bytes 786440 | tf_op jit(solution)/shard_map/ppermute | solution.py:161
  70.9 3.9 %collective-permute-start.14 = (bf16[256,512]{1,0:T(8,128)(2,1)S(1)}, bf16[256,512]{1,0:T(8,128)(2,1)S(1)}, u32[]{:S(2)}, u32[]{:S(2)}) collective-permute-start(bf16[256,512]{1,0:T(8,128)(2,1)S(1)} %get-tuple-element.18), channel_id=1, source_target_pairs={{0,14},{2,0},{4,2},{6,4},{8,6},{10,8},{12,10},{14,12},{1,15},{3,1}... | collective-permute-start | bytes 786440 | tf_op jit(solution)/shard_map/ppermute | solution.py:161
  70.9 6.8 %collective-permute-start.16 = (bf16[256,512]{1,0:T(8,128)(2,1)S(1)}, bf16[256,512]{1,0:T(8,128)(2,1)S(1)}, u32[]{:S(2)}, u32[]{:S(2)}) collective-permute-start(bf16[256,512]{1,0:T(8,128)(2,1)S(1)} %get-tuple-element.20), channel_id=1, source_target_pairs={{0,14},{2,0},{4,2},{6,4},{8,6},{10,8},{12,10},{14,12},{1,15},{3,1}... | collective-permute-start | bytes 786440 | tf_op jit(solution)/shard_map/ppermute | solution.py:161
  73.8 15.9 %collective-permute-start.13 = (bf16[256,512]{1,0:T(8,128)(2,1)S(1)}, bf16[256,512]{1,0:T(8,128)(2,1)S(1)}, u32[]{:S(2)}, u32[]{:S(2)}) collective-permute-start(bf16[256,512]{1,0:T(8,128)(2,1)S(1)} %get-tuple-element.16), channel_id=1, source_target_pairs={{0,14},{2,0},{4,2},{6,4},{8,6},{10,8},{12,10},{14,12},{1,15},{3,1}... | collective-permute-start | bytes 786440 | tf_op jit(solution)/shard_map/ppermute | solution.py:161
  73.9 9.5 %collective-permute-start.18 = (bf16[256,512]{1,0:T(8,128)(2,1)S(1)}, bf16[256,512]{1,0:T(8,128)(2,1)S(1)}, u32[]{:S(2)}, u32[]{:S(2)}) collective-permute-start(bf16[256,512]{1,0:T(8,128)(2,1)S(1)} %get-tuple-element.22), channel_id=1, source_target_pairs={{0,14},{2,0},{4,2},{6,4},{8,6},{10,8},{12,10},{14,12},{1,15},{3,1}... | collective-permute-start | bytes 786440 | tf_op jit(solution)/shard_map/ppermute | solution.py:161
  74.9 14.9 %collective-permute-start.15 = (bf16[256,512]{1,0:T(8,128)(2,1)S(1)}, bf16[256,512]{1,0:T(8,128)(2,1)S(1)}, u32[]{:S(2)}, u32[]{:S(2)}) collective-permute-start(bf16[256,512]{1,0:T(8,128)(2,1)S(1)} %add_convert_fusion.2), channel_id=1, source_target_pairs={{0,48},{16,0},{32,16},{48,32},{64,112},{80,64},{96,80},{112,96},{1... | collective-permute-start | bytes 786440 | tf_op jit(solution)/shard_map/ppermute | solution.py:155
  77.8 12.0 %collective-permute-start.17 = (bf16[256,512]{1,0:T(8,128)(2,1)S(1)}, bf16[256,512]{1,0:T(8,128)(2,1)S(1)}, u32[]{:S(2)}, u32[]{:S(2)}) collective-permute-start(bf16[256,512]{1,0:T(8,128)(2,1)S(1)} %add_convert_fusion.1), channel_id=1, source_target_pairs={{0,32},{16,48},{32,0},{48,16},{64,96},{80,112},{96,64},{112,80},{1... | collective-permute-start | bytes 786440 | tf_op jit(solution)/shard_map/ppermute | solution.py:155
  83.4 10.9 %collective-permute-start.19 = (bf16[256,512]{1,0:T(8,128)(2,1)S(1)}, bf16[256,512]{1,0:T(8,128)(2,1)S(1)}, u32[]{:S(2)}, u32[]{:S(2)}) collective-permute-start(bf16[256,512]{1,0:T(8,128)(2,1)S(1)} %add_convert_fusion), channel_id=1, source_target_pairs={{0,16},{16,32},{32,48},{48,0},{64,80},{80,96},{96,112},{112,64},{1... | collective-permute-start | bytes 786440 | tf_op jit(solution)/shard_map/ppermute | solution.py:155
  87.8 13.5 %collective-permute-start.12 = (bf16[128,1536]{1,0:T(8,128)(2,1)S(1)}, bf16[128,1536]{1,0:T(8,128)(2,1)S(1)}, u32[]{:S(2)}, u32[]{:S(2)}) collective-permute-start(bf16[128,1536]{1,0:T(8,128)(2,1)S(1)} %get-tuple-element.14), channel_id=1, source_target_pairs={{0,1},{1,0},{2,3},{3,2},{4,5},{5,4},{6,7},{7,6},{8,9},{9,8},{10,11... | collective-permute-start | bytes 1179656 | tf_op jit(solution)/shard_map/ppermute | solution.py:142
  94.7 13.3 %collective-permute-start.20 = (bf16[128,512]{1,0:T(8,128)(2,1)S(1)}, bf16[128,512]{1,0:T(8,128)(2,1)S(1)}, u32[]{:S(2)}, u32[]{:S(2)}) collective-permute-start(bf16[128,512]{1,0:T(8,128)(2,1)S(1)} %get-tuple-element.32), channel_id=1, source_target_pairs={{16,80},{17,81},{32,96},{33,97},{48,112},{49,113},{80,16},{81,17},... | collective-permute-start | bytes 393224 | tf_op jit(solution)/shard_map/ppermute | solution.py:151
  102.4 6.9 %collective-permute-start.21 = (bf16[128,512]{1,0:T(8,128)(2,1)S(1)}, bf16[128,512]{1,0:T(8,128)(2,1)S(1)}, u32[]{:S(2)}, u32[]{:S(2)}) collective-permute-start(bf16[128,512]{1,0:T(8,128)(2,1)S(1)} %slice.45), channel_id=1, source_target_pairs={{0,1},{1,0},{2,3},{3,2},{4,5},{5,4},{6,7},{7,6},{8,9},{9,8},{10,11... | collective-permute-start | bytes 393224 | tf_op jit(solution)/shard_map/ppermute | solution.py:142
  104.4 8.1 %collective-permute-start.22 = (bf16[128,512]{1,0:T(8,128)(2,1)S(1)}, bf16[128,512]{1,0:T(8,128)(2,1)S(1)}, u32[]{:S(2)}, u32[]{:S(2)}) collective-permute-start(bf16[128,512]{1,0:T(8,128)(2,1)S(1)} %get-tuple-element.33), channel_id=1, source_target_pairs={{16,81},{17,80},{32,97},{33,96},{48,113},{49,112},{80,17},{81,16},... | collective-permute-start | bytes 393224 | tf_op jit(solution)/shard_map/ppermute | solution.py:151
  (3 other events, 10.4 us)

commit v2 on v1

v2 whole, which is shorter than its diff:
```python
import functools
import math

import jax
import jax.numpy as jnp
from jax import lax
from jax.experimental import pallas as pl
from jax.experimental.pallas import tpu as pltpu
from jax.sharding import PartitionSpec as P

HEAD = 128
GROUP = 6
KV = 2
WIN = 4
SPAN = 128
COLS = GROUP * HEAD
Y = 4
NEG = -1e30
SCALE = 1.0 / math.sqrt(HEAD)
SCALE2 = SCALE * math.log2(math.e)
NT = (((1,), (1,)), ((), ()))
NN = (((1,), (0,)), ((), ()))
SMALL = pltpu.CompilerParams(vmem_limit_bytes=6 * 1024 * 1024)


def dot(a, b, dims):
    return lax.dot_general(a, b, dims, preferred_element_type=jnp.float32)


def attention_kernel(j, order, place, q_any, do_any, qf_any, dof_any, *refs):
    near_in, far_in = refs[:8], refs[8]
    dq_own, dq_far, near_out, far_out = refs[9:13]
    e_slots, dp_slots, p_scr, ds_scr, k_scr, v_scr, kt_scr, q_scr, do_scr = refs[13:22]
    block_scr, q_own, do_own, far, sems = refs[22:]
    inner, outer, head = place[0], place[1], place[2]
    my_cols = pl.ds(pl.multiple_of((head * KV + j) * COLS, COLS), COLS)
    copies = [
        pltpu.make_async_copy(near_in[n].at[j], block_scr.at[n], sems.at[n]) for n in range(8)
    ] + [
        pltpu.make_async_copy(far_in, block_scr.at[pl.ds(8, 8)], sems.at[8]),
        pltpu.make_async_copy(qf_any, far.at[pl.ds(0, SPAN)], sems.at[9]),
        pltpu.make_async_copy(dof_any, far.at[pl.ds(SPAN, SPAN)], sems.at[12]),
        pltpu.make_async_copy(q_any.at[:, my_cols], q_own, sems.at[10]),
        pltpu.make_async_copy(do_any.at[:, my_cols], do_own, sems.at[11]),
    ]
    for copy in copies:
        copy.start()

    def span_of(d, o, half):
        block = lax.rem(inner + 8 - d, 8) * 8 + lax.rem(outer + 8 - o, 8)
        return order[block * 2 + (head if half == 0 else 1 - head)]

    lane = lax.broadcasted_iota(jnp.int32, (1, 256), 1)
    at = [span_of(0, 0, 0), span_of(0, 0, 1)]
    hidden = []
    for n in range(8):
        for half in range(2):
            key = span_of(n % WIN, n // WIN, half)
            first = jnp.where(key <= at[0], 0.0, -NEG)
            second = jnp.where(key <= at[1], 0.0, -NEG)
            hidden.append(jnp.where(lane < SPAN, first, second).astype(jnp.float32))
    row = lax.broadcasted_iota(jnp.int32, (256, 256), 0)
    col = lax.broadcasted_iota(jnp.int32, (256, 256), 1)
    key_pos = jnp.where(row < SPAN, at[0], at[1]) * SPAN + (row & (SPAN - 1))
    row_pos = jnp.where(col < SPAN, at[0], at[1]) * SPAN + (col & (SPAN - 1))
    own_visible = key_pos <= row_pos

    for n in range(16):
        if n <= 8:
            copies[n].wait()
        both = block_scr[n]
        at_r = slice(n * SPAN, (n + 1) * SPAN)
        k_scr[at_r, :] = both[:, :HEAD]
        v_scr[at_r, :] = both[:, HEAD:]
        kt_scr[:, at_r] = both[:, :HEAD].T

    for copy in copies[9:]:
        copy.wait()
    for g in range(GROUP):
        at_h = slice(g * HEAD, (g + 1) * HEAD)
        rows = slice(g * 256, (g + 1) * 256)
        e_scr, dp_scr = e_slots.at[g % 2], dp_slots.at[g % 2]
        q_h = jnp.concatenate([q_own[:, at_h], far[:SPAN, at_h]], axis=0)
        do_h = jnp.concatenate([do_own[:, at_h], far[SPAN:, at_h]], axis=0)
        q_scr[rows, :] = q_h
        do_scr[rows, :] = do_h
        top = jnp.full((1, 256), NEG, jnp.float32)
        tops = []
        total = jnp.zeros((8, 256), jnp.float32)
        row_dot = jnp.zeros((8, 256), jnp.float32)
        for n in range(8):
            at_r = slice(n * 256, (n + 1) * 256)
            s = dot(k_scr[at_r, :], q_h, NT)
            if n == 0:
                s = jnp.where(own_visible, s, NEG)
            dp = dot(v_scr[at_r, :], do_h, NT)
            dp_scr[at_r, :] = dp
            before = top
            for half in range(2):
                here = jnp.max(s[half * 128 : (half + 1) * 128], axis=0, keepdims=True)
                top = jnp.maximum(top, (here - hidden[2 * n + half] if n else here) * SCALE2)
            tops.append(top)
            if n:
                decay = jnp.exp2(before - top)
                total, row_dot = total * decay, row_dot * decay
            for half in range(2):
                at_e = slice(n * 256 + half * 128, n * 256 + half * 128 + 128)
                lower = top + hidden[2 * n + half] if n else top
                e = jnp.exp2(s[half * 128 : (half + 1) * 128] * SCALE2 - lower)
                e_scr[at_e, :] = e
                total = total + jnp.sum(e.reshape(16, 8, 256), axis=0)
                product = e * dp[half * 128 : (half + 1) * 128]
                row_dot = row_dot + jnp.sum(product.reshape(16, 8, 256), axis=0)
        inverse = 1.0 / jnp.sum(total, axis=0, keepdims=True)
        row_dot = jnp.sum(row_dot, axis=0, keepdims=True) * inverse
        for n in range(8):
            at_r = slice(n * 256, (n + 1) * 256)
            p = e_scr[at_r, :] * (inverse * jnp.exp2(tops[n] - top))
            ds = p * (dp_scr[at_r, :] - row_dot)
            p_scr[at_r, rows] = p.astype(jnp.bfloat16)
            ds_scr[at_r, rows] = ds.astype(jnp.bfloat16)
    for n in range(8):
        at_r = slice(n * 256, (n + 1) * 256)
        dk = dot(ds_scr[at_r, :], q_scr[...], NN) * SCALE
        dv = dot(p_scr[at_r, :], do_scr[...], NN)
        out, at_o = (near_out if n < WIN else far_out), slice(n % WIN * 256, n % WIN * 256 + 256)
        out[at_o, :HEAD] = dk.astype(jnp.bfloat16)
        out[at_o, HEAD:] = dv.astype(jnp.bfloat16)
    for g in range(GROUP):
        dq = dot(kt_scr[...], ds_scr[:, g * 256 : (g + 1) * 256], NN) * SCALE
        dq = dq.T.astype(jnp.bfloat16)
        dq_own[:, g * HEAD : (g + 1) * HEAD] = dq[:SPAN]
        dq_far[:, g * HEAD : (g + 1) * HEAD] = dq[SPAN:]


def attention(j, order, place, queries, output_gradient, far, near_in, far_in):
    def whole(*shape):
        return pl.BlockSpec(shape, lambda i, order, place: (0,) * len(shape))

    hbm = pl.BlockSpec(memory_space=pltpu.HBM)
    free = pl.BlockSpec(memory_space=pl.ANY)
    rows = jax.ShapeDtypeStruct((SPAN, COLS), jnp.bfloat16)
    terms = jax.ShapeDtypeStruct((WIN * 256, 256), jnp.bfloat16)
    out = (rows, rows, terms, terms)
    return pl.pallas_call(
        functools.partial(attention_kernel, j),
        grid_spec=pltpu.PrefetchScalarGridSpec(
            num_scalar_prefetch=2,
            grid=(1,),
            in_specs=[hbm] * 4 + [free] * 8 + [hbm],
            out_specs=[whole(*o.shape) for o in out],
            scratch_shapes=[
                pltpu.VMEM((2, 2048, 256), jnp.float32),
                pltpu.VMEM((2, 2048, 256), jnp.float32),
                pltpu.VMEM((2048, GROUP * 256), jnp.bfloat16),
                pltpu.VMEM((2048, GROUP * 256), jnp.bfloat16),
                pltpu.VMEM((2048, HEAD), jnp.bfloat16),
                pltpu.VMEM((2048, HEAD), jnp.bfloat16),
                pltpu.VMEM((HEAD, 2048), jnp.bfloat16),
                pltpu.VMEM((GROUP * 256, HEAD), jnp.bfloat16),
                pltpu.VMEM((GROUP * 256, HEAD), jnp.bfloat16),
                pltpu.VMEM((16, SPAN, 256), jnp.bfloat16),
                pltpu.VMEM((SPAN, COLS), jnp.bfloat16),
                pltpu.VMEM((SPAN, COLS), jnp.bfloat16),
                pltpu.VMEM((256, COLS), jnp.bfloat16),
                pltpu.SemaphoreType.DMA((13,)),
            ],
        ),
        out_shape=out,
        compiler_params=pltpu.CompilerParams(vmem_limit_bytes=32 * 1024 * 1024),
        cost_estimate=pl.CostEstimate(
            flops=10 * 6 * 256 * 2048 * 128, bytes_accessed=5_000_000, transcendentals=6 * 256 * 2048
        ),
    )(order, place, queries, output_gradient, *far, *near_in, far_in)


def pack_kernel(*refs):
    halves, out = refs[:8], refs[9:11]
    for j in range(KV):
        for n in range(8):
            out[j][n] = halves[n][j]


def pack(near, after):
    vmem = pl.BlockSpec(memory_space=pltpu.VMEM)
    one = jax.ShapeDtypeStruct((8, SPAN, 256), jnp.bfloat16)
    return pl.pallas_call(
        pack_kernel,
        in_specs=[vmem] * 8 + [pl.BlockSpec(memory_space=pl.ANY)],
        out_specs=[vmem] * 2,
        out_shape=[one] * 2,
        compiler_params=SMALL,
    )(*near, after)


def tie_kernel(*refs):
    del refs


def tie(x, *after):
    free = pl.BlockSpec(memory_space=pl.ANY)
    return pl.pallas_call(
        tie_kernel,
        in_specs=[free] * (1 + len(after)),
        out_specs=free,
        out_shape=jax.ShapeDtypeStruct(x.shape, x.dtype),
        input_output_aliases={0: 0},
        compiler_params=SMALL,
    )(x, *after)


def join_rows_kernel(place, own0, own1, back0, back1, out):
    head = place[2]
    for x, h, j in ((own0, head, 0), (own1, head, 1), (back0, 1 - head, 0), (back1, 1 - head, 1)):
        out[:, pl.ds(pl.multiple_of((h * KV + j) * COLS, COLS), COLS)] = x[...]


def join_rows(place, own, back):
    vmem = pl.BlockSpec(memory_space=pltpu.VMEM)
    return pl.pallas_call(
        join_rows_kernel,
        in_specs=[pl.BlockSpec(memory_space=pltpu.SMEM)] + [vmem] * 4,
        out_specs=vmem,
        out_shape=jax.ShapeDtypeStruct((SPAN, 2 * KV * COLS), jnp.bfloat16),
        compiler_params=SMALL,
    )(place, *own, *back)


def cut_kernel(place, queries, output_gradient, after, *outs):
    del after
    for n, out in enumerate(outs):
        at = ((1 - place[2]) * KV + n // 2) * COLS
        at = pl.ds(pl.multiple_of(at, COLS), COLS)
        out[...] = (queries, output_gradient)[n % 2][:, at]


def cut(place, queries, output_gradient, after):
    vmem = pl.BlockSpec(memory_space=pltpu.VMEM)
    out = pl.pallas_call(
        cut_kernel,
        in_specs=[pl.BlockSpec(memory_space=pltpu.SMEM), vmem, vmem, pl.BlockSpec(memory_space=pl.ANY)],
        out_specs=[vmem] * 4,
        out_shape=[jax.ShapeDtypeStruct((SPAN, COLS), jnp.bfloat16)] * 4,
        compiler_params=SMALL,
    )(place, queries, output_gradient, after)
    return out[:2], out[2:]


def join_terms_kernel(place, mine0, mine1, theirs, dk, dv):
    head = place[2]
    for j, mine in enumerate((mine0, mine1)):
        at = pl.ds(pl.multiple_of((head * KV + j) * HEAD, HEAD), HEAD)
        there = pl.ds(pl.multiple_of(((1 - head) * KV + j) * HEAD, HEAD), HEAD)
        dk[:, at] = mine[:, :HEAD]
        dv[:, at] = mine[:, HEAD:]
        dk[:, there] = theirs[j, :, :HEAD]
        dv[:, there] = theirs[j, :, HEAD:]


def join_terms(place, mine, theirs):
    vmem = pl.BlockSpec(memory_space=pltpu.VMEM)
    out = jax.ShapeDtypeStruct((SPAN, 2 * KV * HEAD), jnp.bfloat16)
    return pl.pallas_call(
        join_terms_kernel,
        in_specs=[pl.BlockSpec(memory_space=pltpu.SMEM)] + [vmem] * 3,
        out_specs=[vmem] * 2,
        out_shape=[out] * 2,
        compiler_params=SMALL,
    )(place, *mine, theirs)


def to_partner(x):
    return lax.ppermute(x, "head", [(0, 1), (1, 0)])


def across(x):
    perm = []
    for lo in range(2):
        for y in (1, 2, 3):
            for h in range(2):
                perm.append(((lo * Y + y) * 2 + h, ((1 - lo) * Y + y) * 2 + 1 - h))
    return lax.ppermute(x, ("inner", "head"), perm)


def along_y(x, by):
    return lax.ppermute(
        x, "inner", [(lo * Y + y, lo * Y + (y + by) % Y) for lo in range(2) for y in range(Y)]
    )


def along_inner(x, by):
    return lax.ppermute(x, "inner", [(i, (i + by) % 8) for i in range(8)])


def along_outer(x, by):
    return lax.ppermute(x, "outer", [(o, (o + by) % 8) for o in range(8)])


def f32(x):
    return x.astype(jnp.float32)


def bf16(x):
    return x.astype(jnp.bfloat16)


def shards(queries, keys, values, output_gradient, span_order):
    inner, outer, head = lax.axis_index("inner"), lax.axis_index("outer"), lax.axis_index("head")
    place = jnp.stack([inner, outer, head]).astype(jnp.int32)
    y = lax.rem(inner, Y)

    def cols(x, at, width):
        return lax.dynamic_slice_in_dim(x, at, width, axis=1)

    def piece(of):
        return jnp.stack(
            [
                jnp.concatenate([cols(x, (of * KV + j) * HEAD, HEAD) for x in (keys, values)], axis=1)
                for j in range(KV)
            ]
        )

    mine, theirs = piece(head), piece(1 - head)
    near = [[mine, to_partner(theirs)]]
    other = across(theirs)
    straight = [along_inner(mine, k) for k in (1, 2, 3)]
    for k in (1, 2, 3):
        near.append([straight[k - 1], along_y(jnp.where(y + k >= Y, other, near[0][1]), k)])
    near = [half for block in near for half in block]
    far = [
        [to_partner(x) for x in two] for two in cut(place, queries, output_gradient, near[1])
    ]
    far_in = [along_outer(x, 1) for x in pack(near, far[0][0])]

    dqs, backs, sums = [], [], []
    arrived = None
    for j in range(KV):
        dq_own, dq_far, near_out, far_out = attention(
            j, span_order, place, queries, output_gradient, far[j], near, far_in[j]
        )
        dqs.append(dq_own)
        backs.append(to_partner(dq_far))
        if j:
            far_out = tie(far_out, arrived, backs[0])
        arrived = along_outer(far_out, -1)
        if j:
            near_out = tie(near_out, backs[1])
        terms = f32(near_out) + f32(arrived)
        total = terms[:256]
        for k in (1, 2, 3):
            total = total + f32(along_inner(bf16(terms[k * 256 : (k + 1) * 256]), -k))
        sums.append(total)
    theirs = to_partner(jnp.stack([bf16(s[SPAN:]) for s in sums]))
    dk, dv = join_terms(place, [bf16(s[:SPAN]) for s in sums], theirs)
    return join_rows(place, dqs, backs), dk, dv


def solution(mesh):
    rows = P(("inner", "outer", "head"), None)
    return jax.shard_map(
        shards,
        mesh=mesh,
        in_specs=(rows, rows, rows, rows, P()),
        out_specs=(rows, rows, rows),
        check_vma=False,
    )
```

time: 114 us -> 102 us (0.89); the launches traced: 114 us -> 100 us
  waiting for transfers between devices: 37.6 us -> 29.7 us
  other arithmetic: 3.18 us -> 0.66 us
  starting transfers between devices: 40.2 us -> 38.5 us
  Pallas kernels: 30.6 us -> 29.3 us
    ppermute x6 -> x3, starting transfers between devices: 12.9 us -> 3.42 us  [along_y(): lax.ppermute(x, 'inner', [(lo * Y + y, lo * Y + (y + by) % Y) for lo in r...]
    ppermute x5 -> x8, starting transfers between devices: 7.36 us -> 15.2 us  [to_partner(): return lax.ppermute(x, 'head', [(0, 1), (1, 0)])]
    ppermute x6 -> x3, waiting for transfers between devices: 12.5 us -> 5.16 us  [along_y(): lax.ppermute(x, 'inner', [(lo * Y + y, lo * Y + (y + by) % Y) for lo in r...]
    ppermute x4 -> x10, waiting for transfers between devices: 9.36 us -> 16.7 us  [the longest x9 16.7 us: along_inner(): return lax.ppermute(x, 'inner', [(i, (i + by) % 8) for i in range(8)])]
    ppermute x8 -> x4, waiting for transfers between devices: 7.58 us -> 1.42 us  [along_outer(): return lax.ppermute(x, 'outer', [(o, (o + by) % 8) for o in range(8)])]
    select_n x4 -> x1, other arithmetic: 2.6 us -> 0.03 us  [shards(): jnp.where(y + k >= Y, other, near[0][1])]
    ppermute x5 -> x8, waiting for transfers between devices: 8.17 us -> 6.5 us  [to_partner(): return lax.ppermute(x, 'head', [(0, 1), (1, 0)])]
    ppermute x8 -> x4, starting transfers between devices: 5.5 us -> 4.03 us  [along_outer(): return lax.ppermute(x, 'outer', [(o, (o + by) % 8) for o in range(8)])]
  transfers between devices with their start and end apart: 23 -> 25, of which waited for: 14 -> 13; matrix products, arithmetic and copies ran while one was open for 2% -> 0% of each run, Pallas kernels for 0% -> 28%
where the time goes in v2:
time: 102 us; the launch traced here: 100 us
  starting transfers between devices  38.5 us (38%)
  waiting for transfers between devices  29.7 us (29%)
  Pallas kernels  29.3 us (29%)
  local copies, waits for them, and re-layouts  1.11 us (1%)
    pallas_call x2, Pallas kernels, attention(): pl.pallas_call(functools.partial(attention_kernel, j), grid_spec=pltpu.Pr...  25.8 us
    ppermute x9, waiting for transfers between devices, along_inner(): return lax.ppermute(x, 'inner', [(i, (i + by) % 8) for i in range(8)])  16.7 us
    ppermute x8, starting transfers between devices, to_partner(): return lax.ppermute(x, 'head', [(0, 1), (1, 0)])  15.2 us
    ppermute x9, starting transfers between devices, along_inner(): return lax.ppermute(x, 'inner', [(i, (i + by) % 8) for i in range(8)])  11.2 us
    ppermute x8, waiting for transfers between devices, to_partner(): return lax.ppermute(x, 'head', [(0, 1), (1, 0)])  6.5 us
    ppermute x3, waiting for transfers between devices, along_y(): lax.ppermute(x, 'inner', [(lo * Y + y, lo * Y + (y + by) % Y) for lo in r...  5.16 us
    ppermute x1, starting transfers between devices, across(): return lax.ppermute(x, ('inner', 'head'), perm)  4.67 us
    ppermute x4, starting transfers between devices, along_outer(): return lax.ppermute(x, 'outer', [(o, (o + by) % 8) for o in range(8)])  4.03 us
  transfers between devices with their start and end apart: 25, of which 13 were waited for; matrix products, arithmetic and copies ran while one was open for 0% of the time, Pallas kernels for 28%

profile of v2, /device:TPU:16, one launch (start us, length us, event | category | flops | bytes accessed | tf_op | source)
XLA Modules:
  0.0 100.1 jit_solution(4631809790635806040)
XLA Ops:
  1.7 4.7 %collective-permute-start.4 = (bf16[2,128,256]{2,1,0:T(8,128)(2,1)S(1)}, bf16[2,128,256]{2,1,0:T(8,128)(2,1)S(1)}, u32[]{:S(2)}, u32[]{:S(2)}) collective-permute-start(bf16[2,128,256]{2,1,0:T(8,128)(2,1)S(1)} %pad_maximum_fusion), channel_id=1, source_target_pairs={{16,81},{17,80},{32,97},{33,96},{48,113},{49,112},{80,17},{81,16},... | collective-permute-start | bytes 393224 | tf_op jit(solution)/shard_map/ppermute | solution.py:282
  7.8 2.9 %collective-permute-start.6 = (bf16[2,128,256]{2,1,0:T(8,128)(2,1)S(1)}, bf16[2,128,256]{2,1,0:T(8,128)(2,1)S(1)}, u32[]{:S(2)}, u32[]{:S(2)}) collective-permute-start(bf16[2,128,256]{2,1,0:T(8,128)(2,1)S(1)} %pad_maximum_fusion.1.refs_0_), channel_id=1, source_target_pairs={{0,32},{16,48},{32,64},{48,80},{64,96},{80,112},{96,0},{112,16},{1... | collective-permute-start | bytes 393224 | tf_op jit(solution)/shard_map/ppermute | solution.py:292
  10.8 3.6 %collective-permute-done.after.refs_1_ = bf16[2,128,256]{2,1,0:T(8,128)(2,1)S(1)} collective-permute-done((bf16[2,128,256]{2,1,0:T(8,128)(2,1)S(1)}, bf16[2,128,256]{2,1,0:T(8,128)(2,1)S(1)}, u32[]{:S(2)}, u32[]{:S(2)}) %collective-permute-start) | collective-permute-done | bytes 131104 | tf_op jit(solution)/shard_map/ppermute | solution.py:273
  16.7 2.7 %collective-permute-start.7 = (bf16[2,128,256]{2,1,0:T(8,128)(2,1)S(1)}, bf16[2,128,256]{2,1,0:T(8,128)(2,1)S(1)}, u32[]{:S(2)}, u32[]{:S(2)}) collective-permute-start(bf16[2,128,256]{2,1,0:T(8,128)(2,1)S(1)} %get-tuple-element.46), channel_id=1, source_target_pairs={{0,32},{16,48},{32,0},{48,16},{64,96},{80,112},{96,64},{112,80},{1... | collective-permute-start | bytes 393224 | tf_op jit(solution)/shard_map/ppermute | solution.py:286
  19.4 2.1 %collective-permute-done.9.refs_7_ = bf16[2,128,256]{2,1,0:T(8,128)(2,1)S(1)} collective-permute-done((bf16[2,128,256]{2,1,0:T(8,128)(2,1)S(1)}, bf16[2,128,256]{2,1,0:T(8,128)(2,1)S(1)}, u32[]{:S(2)}, u32[]{:S(2)}) %collective-permute-start.9) | collective-permute-done | bytes 131104 | tf_op jit(solution)/shard_map/ppermute | solution.py:286
  21.5 1.7 %collective-permute-done.7.refs_5_ = bf16[2,128,256]{2,1,0:T(8,128)(2,1)S(1)} collective-permute-done((bf16[2,128,256]{2,1,0:T(8,128)(2,1)S(1)}, bf16[2,128,256]{2,1,0:T(8,128)(2,1)S(1)}, u32[]{:S(2)}, u32[]{:S(2)}) %collective-permute-start.7) | collective-permute-done | bytes 131104 | tf_op jit(solution)/shard_map/ppermute | solution.py:286
  23.2 1.4 %collective-permute-done.5.refs_3_ = bf16[2,128,256]{2,1,0:T(8,128)(2,1)S(1)} collective-permute-done((bf16[2,128,256]{2,1,0:T(8,128)(2,1)S(1)}, bf16[2,128,256]{2,1,0:T(8,128)(2,1)S(1)}, u32[]{:S(2)}, u32[]{:S(2)}) %collective-permute-start.5) | collective-permute-done | bytes 131104 | tf_op jit(solution)/shard_map/ppermute | solution.py:286
  24.7 2.6 %collective-permute-start.2 = (bf16[128,768]{1,0:T(8,128)(2,1)S(1)}, bf16[128,768]{1,0:T(8,128)(2,1)S(1)}, u32[]{:S(2)}, u32[]{:S(2)}) collective-permute-start(bf16[128,768]{1,0:T(8,128)(2,1)S(1)} %get-tuple-element.20), channel_id=1, source_target_pairs={{0,1},{1,0},{2,3},{3,2},{4,5},{5,4},{6,7},{7,6},{8,9},{9,8},{10,11... | collective-permute-start | bytes 589832 | tf_op jit(solution)/shard_map/ppermute | solution.py:273
  28.3 2.5 %collective-permute-start.12 = (bf16[128,768]{1,0:T(8,128)(2,1)S(1)}, bf16[128,768]{1,0:T(8,128)(2,1)S(1)}, u32[]{:S(2)}, u32[]{:S(2)}) collective-permute-start(bf16[128,768]{1,0:T(8,128)(2,1)S(1)} %get-tuple-element.24), channel_id=1, source_target_pairs={{0,1},{1,0},{2,3},{3,2},{4,5},{5,4},{6,7},{7,6},{8,9},{9,8},{10,11... | collective-permute-start | bytes 589832 | tf_op jit(solution)/shard_map/ppermute | solution.py:273
  33.1 1.4 %collective-permute-done.10.refs_8_ = bf16[8,128,256]{2,1,0:T(8,128)(2,1)S(1)} collective-permute-done((bf16[8,128,256]{2,1,0:T(8,128)(2,1)S(1)}, bf16[8,128,256]{2,1,0:T(8,128)(2,1)S(1)}, u32[]{:S(2)}, u32[]{:S(2)}) %collective-permute-start.10) | collective-permute-done | bytes 524320 | tf_op jit(solution)/shard_map/ppermute | solution.py:296
  34.5 12.9 %shard_map.78 = (bf16[128,768]{1,0:T(8,128)(2,1)S(1)}, bf16[128,768]{1,0:T(8,128)(2,1)S(1)}, bf16[1024,256]{1,0:T(8,128)(2,1)S(1)}, bf16[1024,256]{1,0:T(8,128)(2,1)S(1)}) custom-call(s32[128]{0:T(128)S(1)} %copy-done.2, s32[3]{0:T(128)S(1)} %pad_add_fusion.place, bf16[128,3072]{1,0:T(8,128)(2,1)S(1)} %copy-done, bf16[128,3072]{1,0:T(8,128)(2,1)S(1)} %copy-done.1, ...), custom_call_target="tpu_custom_call" | custom-call | flops 4026531840 | bytes 5000000 | tf_op jit(solution)/shard_map/pallas_call | solution.py:145
  47.4 2.8 %collective-permute-start.14 = (bf16[128,768]{1,0:T(8,128)(2,1)S(1)}, bf16[128,768]{1,0:T(8,128)(2,1)S(1)}, u32[]{:S(2)}, u32[]{:S(2)}) collective-permute-start(bf16[128,768]{1,0:T(8,128)(2,1)S(1)} %get-tuple-element.27), channel_id=1, source_target_pairs={{0,1},{1,0},{2,3},{3,2},{4,5},{5,4},{6,7},{7,6},{8,9},{9,8},{10,11... | collective-permute-start | bytes 589832 | tf_op jit(solution)/shard_map/ppermute | solution.py:273
  50.2 12.9 %shard_map.79 = (bf16[128,768]{1,0:T(8,128)(2,1)S(1)}, bf16[128,768]{1,0:T(8,128)(2,1)S(1)}, bf16[1024,256]{1,0:T(8,128)(2,1)S(1)}, bf16[1024,256]{1,0:T(8,128)(2,1)S(1)}) custom-call(s32[128]{0:T(128)S(1)} %copy-done.2, s32[3]{0:T(128)S(1)} %pad_add_fusion.place, bf16[128,3072]{1,0:T(8,128)(2,1)S(1)} %copy-done, bf16[128,3072]{1,0:T(8,128)(2,1)S(1)} %copy-done.1, ...), custom_call_target="tpu_custom_call" | custom-call | flops 4026531840 | bytes 5000000 | tf_op jit(solution)/shard_map/pallas_call | solution.py:145
  64.3 2.9 %collective-permute-start.20 = (bf16[1024,256]{1,0:T(8,128)(2,1)S(1)}, bf16[1024,256]{1,0:T(8,128)(2,1)S(1)}, u32[]{:S(2)}, u32[]{:S(2)}) collective-permute-start(bf16[1024,256]{1,0:T(8,128)(2,1)S(1)} %shard_map.82), channel_id=1, source_target_pairs={{0,14},{2,0},{4,2},{6,4},{8,6},{10,8},{12,10},{14,12},{1,15},{3,1}... | collective-permute-start | bytes 1572872 | tf_op jit(solution)/shard_map/ppermute | solution.py:296
  67.8 1.8 %collective-permute-start.19 = (bf16[256,256]{1,0:T(8,128)(2,1)S(1)}, bf16[256,256]{1,0:T(8,128)(2,1)S(1)}, u32[]{:S(2)}, u32[]{:S(2)}) collective-permute-start(bf16[256,256]{1,0:T(8,128)(2,1)S(1)} %get-tuple-element.43), channel_id=1, source_target_pairs={{0,80},{16,96},{32,112},{48,0},{64,16},{80,32},{96,48},{112,64},{1... | collective-permute-start | bytes 393224 | tf_op jit(solution)/shard_map/ppermute | solution.py:292
  69.5 4.0 %collective-permute-start.18 = (bf16[256,256]{1,0:T(8,128)(2,1)S(1)}, bf16[256,256]{1,0:T(8,128)(2,1)S(1)}, u32[]{:S(2)}, u32[]{:S(2)}) collective-permute-start(bf16[256,256]{1,0:T(8,128)(2,1)S(1)} %get-tuple-element.44), channel_id=1, source_target_pairs={{0,96},{16,112},{32,0},{48,16},{64,32},{80,48},{96,64},{112,80},{1... | collective-permute-start | bytes 393224 | tf_op jit(solution)/shard_map/ppermute | solution.py:292
  75.5 7.1 %collective-permute-done.18 = bf16[256,256]{1,0:T(8,128)(2,1)S(1)} collective-permute-done((bf16[256,256]{1,0:T(8,128)(2,1)S(1)}, bf16[256,256]{1,0:T(8,128)(2,1)S(1)}, u32[]{:S(2)}, u32[]{:S(2)}) %collective-permute-start.18) | collective-permute-done | bytes 131104 | tf_op jit(solution)/shard_map/ppermute | solution.py:292
  82.9 1.5 %collective-permute-start.23 = (bf16[256,256]{1,0:T(8,128)(2,1)S(1)}, bf16[256,256]{1,0:T(8,128)(2,1)S(1)}, u32[]{:S(2)}, u32[]{:S(2)}) collective-permute-start(bf16[256,256]{1,0:T(8,128)(2,1)S(1)} %get-tuple-element.40), channel_id=1, source_target_pairs={{0,80},{16,96},{32,112},{48,0},{64,16},{80,32},{96,48},{112,64},{1... | collective-permute-start | bytes 393224 | tf_op jit(solution)/shard_map/ppermute | solution.py:292
  84.5 4.7 %collective-permute-done.21 = bf16[256,256]{1,0:T(8,128)(2,1)S(1)} collective-permute-done((bf16[256,256]{1,0:T(8,128)(2,1)S(1)}, bf16[256,256]{1,0:T(8,128)(2,1)S(1)}, u32[]{:S(2)}, u32[]{:S(2)}) %collective-permute-start.21) | collective-permute-done | bytes 131104 | tf_op jit(solution)/shard_map/ppermute | solution.py:292
  89.2 1.6 %collective-permute-done.23 = bf16[256,256]{1,0:T(8,128)(2,1)S(1)} collective-permute-done((bf16[256,256]{1,0:T(8,128)(2,1)S(1)}, bf16[256,256]{1,0:T(8,128)(2,1)S(1)}, u32[]{:S(2)}, u32[]{:S(2)}) %collective-permute-start.23) | collective-permute-done | bytes 131104 | tf_op jit(solution)/shard_map/ppermute | solution.py:292
  90.8 1.4 %collective-permute-done.22 = bf16[256,256]{1,0:T(8,128)(2,1)S(1)} collective-permute-done((bf16[256,256]{1,0:T(8,128)(2,1)S(1)}, bf16[256,256]{1,0:T(8,128)(2,1)S(1)}, u32[]{:S(2)}, u32[]{:S(2)}) %collective-permute-start.22) | collective-permute-done | bytes 131104 | tf_op jit(solution)/shard_map/ppermute | solution.py:292
  92.3 3.3 %collective-permute-start.24 = (bf16[2,128,256]{2,1,0:T(8,128)(2,1)S(1)}, bf16[2,128,256]{2,1,0:T(8,128)(2,1)S(1)}, u32[]{:S(2)}, u32[]{:S(2)}) collective-permute-start(bf16[2,128,256]{2,1,0:T(8,128)(2,1)S(1)} %pad_maximum_fusion.2), channel_id=1, source_target_pairs={{0,1},{1,0},{2,3},{3,2},{4,5},{5,4},{6,7},{7,6},{8,9},{9,8},{10,11... | collective-permute-start | bytes 393224 | tf_op jit(solution)/shard_map/ppermute | solution.py:273
  95.6 1.5 %shard_map.80 = bf16[128,3072]{1,0:T(8,128)(2,1)} custom-call(s32[3]{0:T(128)S(1)} %pad_add_fusion.place, bf16[128,768]{1,0:T(8,128)(2,1)S(1)} %get-tuple-element.22.own0, bf16[128,768]{1,0:T(8,128)(2,1)S(1)} %get-tuple-element.26.own1, bf16[128,768]{1,0:T(8,128)(2,1)S(1)} %collective-permute-done.14.back0.refs_2_, ...), custom_call_target="tpu_custom_call" | custom-call | tf_op jit(solution)/shard_map/pallas_call | solution.py:220
  97.1 1.7 %collective-permute-done.24.theirs = bf16[2,128,256]{2,1,0:T(8,128)(2,1)S(1)} collective-permute-done((bf16[2,128,256]{2,1,0:T(8,128)(2,1)S(1)}, bf16[2,128,256]{2,1,0:T(8,128)(2,1)S(1)}, u32[]{:S(2)}, u32[]{:S(2)}) %collective-permute-start.24) | collective-permute-done | bytes 131104 | tf_op jit(solution)/shard_map/ppermute | solution.py:273
  (58 shorter events, 13.6 us)
Async XLA Ops:
  1.7 14.2 %collective-permute-start.4 = (bf16[2,128,256]{2,1,0:T(8,128)(2,1)S(1)}, bf16[2,128,256]{2,1,0:T(8,128)(2,1)S(1)}, u32[]{:S(2)}, u32[]{:S(2)}) collective-permute-start(bf16[2,128,256]{2,1,0:T(8,128)(2,1)S(1)} %pad_maximum_fusion), channel_id=1, source_target_pairs={{16,81},{17,80},{32,97},{33,96},{48,113},{49,112},{80,17},{81,16},... | collective-permute-start | bytes 393224 | tf_op jit(solution)/shard_map/ppermute | solution.py:282
  6.4 8.0 %collective-permute-start = (bf16[2,128,256]{2,1,0:T(8,128)(2,1)S(1)}, bf16[2,128,256]{2,1,0:T(8,128)(2,1)S(1)}, u32[]{:S(2)}, u32[]{:S(2)}) collective-permute-start(bf16[2,128,256]{2,1,0:T(8,128)(2,1)S(1)} %pad_maximum_fusion), channel_id=1, source_target_pairs={{0,1},{1,0},{2,3},{3,2},{4,5},{5,4},{6,7},{7,6},{8,9},{9,8},{10,11... | collective-permute-start | bytes 393224 | tf_op jit(solution)/shard_map/ppermute | solution.py:273
  7.3 9.3 %collective-permute-start.8 = (bf16[2,128,256]{2,1,0:T(8,128)(2,1)S(1)}, bf16[2,128,256]{2,1,0:T(8,128)(2,1)S(1)}, u32[]{:S(2)}, u32[]{:S(2)}) collective-permute-start(bf16[2,128,256]{2,1,0:T(8,128)(2,1)S(1)} %pad_maximum_fusion.1.refs_0_), channel_id=1, source_target_pairs={{0,48},{16,64},{32,80},{48,96},{64,112},{80,0},{96,16},{112,32},{1... | collective-permute-start | bytes 393224 | tf_op jit(solution)/shard_map/ppermute | solution.py:292
  7.8 11.5 %collective-permute-start.6 = (bf16[2,128,256]{2,1,0:T(8,128)(2,1)S(1)}, bf16[2,128,256]{2,1,0:T(8,128)(2,1)S(1)}, u32[]{:S(2)}, u32[]{:S(2)}) collective-permute-start(bf16[2,128,256]{2,1,0:T(8,128)(2,1)S(1)} %pad_maximum_fusion.1.refs_0_), channel_id=1, source_target_pairs={{0,32},{16,48},{32,64},{48,80},{64,96},{80,112},{96,0},{112,16},{1... | collective-permute-start | bytes 393224 | tf_op jit(solution)/shard_map/ppermute | solution.py:292
  10.7 8.6 %collective-permute-start.3 = (bf16[2,128,256]{2,1,0:T(8,128)(2,1)S(1)}, bf16[2,128,256]{2,1,0:T(8,128)(2,1)S(1)}, u32[]{:S(2)}, u32[]{:S(2)}) collective-permute-start(bf16[2,128,256]{2,1,0:T(8,128)(2,1)S(1)} %pad_maximum_fusion.1.refs_0_), channel_id=1, source_target_pairs={{0,16},{16,32},{32,48},{48,64},{64,80},{80,96},{96,112},{112,0},{1... | collective-permute-start | bytes 393224 | tf_op jit(solution)/shard_map/ppermute | solution.py:292
  15.0 9.5 %collective-permute-start.1 = (bf16[128,768]{1,0:T(8,128)(2,1)S(1)}, bf16[128,768]{1,0:T(8,128)(2,1)S(1)}, u32[]{:S(2)}, u32[]{:S(2)}) collective-permute-start(bf16[128,768]{1,0:T(8,128)(2,1)S(1)} %get-tuple-element.19), channel_id=1, source_target_pairs={{0,1},{1,0},{2,3},{3,2},{4,5},{5,4},{6,7},{7,6},{8,9},{9,8},{10,11... | collective-permute-start | bytes 589832 | tf_op jit(solution)/shard_map/ppermute | solution.py:273
  16.0 5.5 %collective-permute-start.9 = (bf16[2,128,256]{2,1,0:T(8,128)(2,1)S(1)}, bf16[2,128,256]{2,1,0:T(8,128)(2,1)S(1)}, u32[]{:S(2)}, u32[]{:S(2)}) collective-permute-start(bf16[2,128,256]{2,1,0:T(8,128)(2,1)S(1)} %get-tuple-element.45), channel_id=1, source_target_pairs={{0,48},{16,0},{32,16},{48,32},{64,112},{80,64},{96,80},{112,96},{1... | collective-permute-start | bytes 393224 | tf_op jit(solution)/shard_map/ppermute | solution.py:286
  16.7 6.5 %collective-permute-start.7 = (bf16[2,128,256]{2,1,0:T(8,128)(2,1)S(1)}, bf16[2,128,256]{2,1,0:T(8,128)(2,1)S(1)}, u32[]{:S(2)}, u32[]{:S(2)}) collective-permute-start(bf16[2,128,256]{2,1,0:T(8,128)(2,1)S(1)} %get-tuple-element.46), channel_id=1, source_target_pairs={{0,32},{16,48},{32,0},{48,16},{64,96},{80,112},{96,64},{112,80},{1... | collective-permute-start | bytes 393224 | tf_op jit(solution)/shard_map/ppermute | solution.py:286
  24.6 9.8 %collective-permute-start.10 = (bf16[8,128,256]{2,1,0:T(8,128)(2,1)S(1)}, bf16[8,128,256]{2,1,0:T(8,128)(2,1)S(1)}, u32[]{:S(2)}, u32[]{:S(2)}) collective-permute-start(bf16[8,128,256]{2,1,0:T(8,128)(2,1)S(1)} %get-tuple-element.21), channel_id=1, source_target_pairs={{0,2},{2,4},{4,6},{6,8},{8,10},{10,12},{12,14},{14,0},{1,3},{3,5},... | collective-permute-start | bytes 1572872 | tf_op jit(solution)/shard_map/ppermute | solution.py:296
  24.7 8.4 %collective-permute-start.2 = (bf16[128,768]{1,0:T(8,128)(2,1)S(1)}, bf16[128,768]{1,0:T(8,128)(2,1)S(1)}, u32[]{:S(2)}, u32[]{:S(2)}) collective-permute-start(bf16[128,768]{1,0:T(8,128)(2,1)S(1)} %get-tuple-element.20), channel_id=1, source_target_pairs={{0,1},{1,0},{2,3},{3,2},{4,5},{5,4},{6,7},{7,6},{8,9},{9,8},{10,11... | collective-permute-start | bytes 589832 | tf_op jit(solution)/shard_map/ppermute | solution.py:273
  27.3 23.0 %collective-permute-start.11 = (bf16[128,768]{1,0:T(8,128)(2,1)S(1)}, bf16[128,768]{1,0:T(8,128)(2,1)S(1)}, u32[]{:S(2)}, u32[]{:S(2)}) collective-permute-start(bf16[128,768]{1,0:T(8,128)(2,1)S(1)} %get-tuple-element.23), channel_id=1, source_target_pairs={{0,1},{1,0},{2,3},{3,2},{4,5},{5,4},{6,7},{7,6},{8,9},{9,8},{10,11... | collective-permute-start | bytes 589832 | tf_op jit(solution)/shard_map/ppermute | solution.py:273
  28.3 22.0 %collective-permute-start.12 = (bf16[128,768]{1,0:T(8,128)(2,1)S(1)}, bf16[128,768]{1,0:T(8,128)(2,1)S(1)}, u32[]{:S(2)}, u32[]{:S(2)}) collective-permute-start(bf16[128,768]{1,0:T(8,128)(2,1)S(1)} %get-tuple-element.24), channel_id=1, source_target_pairs={{0,1},{1,0},{2,3},{3,2},{4,5},{5,4},{6,7},{7,6},{8,9},{9,8},{10,11... | collective-permute-start | bytes 589832 | tf_op jit(solution)/shard_map/ppermute | solution.py:273
  30.8 19.4 %collective-permute-start.13 = (bf16[8,128,256]{2,1,0:T(8,128)(2,1)S(1)}, bf16[8,128,256]{2,1,0:T(8,128)(2,1)S(1)}, u32[]{:S(2)}, u32[]{:S(2)}) collective-permute-start(bf16[8,128,256]{2,1,0:T(8,128)(2,1)S(1)} %get-tuple-element.25), channel_id=1, source_target_pairs={{0,2},{2,4},{4,6},{6,8},{8,10},{10,12},{12,14},{14,0},{1,3},{3,5},... | collective-permute-start | bytes 1572872 | tf_op jit(solution)/shard_map/ppermute | solution.py:296
  47.4 16.9 %collective-permute-start.16 = (bf16[1024,256]{1,0:T(8,128)(2,1)S(1)}, bf16[1024,256]{1,0:T(8,128)(2,1)S(1)}, u32[]{:S(2)}, u32[]{:S(2)}) collective-permute-start(bf16[1024,256]{1,0:T(8,128)(2,1)S(1)} %get-tuple-element.30), channel_id=1, source_target_pairs={{0,14},{2,0},{4,2},{6,4},{8,6},{10,8},{12,10},{14,12},{1,15},{3,1}... | collective-permute-start | bytes 1572872 | tf_op jit(solution)/shard_map/ppermute | solution.py:296
  47.4 16.9 %collective-permute-start.14 = (bf16[128,768]{1,0:T(8,128)(2,1)S(1)}, bf16[128,768]{1,0:T(8,128)(2,1)S(1)}, u32[]{:S(2)}, u32[]{:S(2)}) collective-permute-start(bf16[128,768]{1,0:T(8,128)(2,1)S(1)} %get-tuple-element.27), channel_id=1, source_target_pairs={{0,1},{1,0},{2,3},{3,2},{4,5},{5,4},{6,7},{7,6},{8,9},{9,8},{10,11... | collective-permute-start | bytes 589832 | tf_op jit(solution)/shard_map/ppermute | solution.py:273
  63.2 10.4 %collective-permute-start.15 = (bf16[128,768]{1,0:T(8,128)(2,1)S(1)}, bf16[128,768]{1,0:T(8,128)(2,1)S(1)}, u32[]{:S(2)}, u32[]{:S(2)}) collective-permute-start(bf16[128,768]{1,0:T(8,128)(2,1)S(1)} %get-tuple-element.28), channel_id=1, source_target_pairs={{0,1},{1,0},{2,3},{3,2},{4,5},{5,4},{6,7},{7,6},{8,9},{9,8},{10,11... | collective-permute-start | bytes 589832 | tf_op jit(solution)/shard_map/ppermute | solution.py:273
  64.3 18.4 %collective-permute-start.20 = (bf16[1024,256]{1,0:T(8,128)(2,1)S(1)}, bf16[1024,256]{1,0:T(8,128)(2,1)S(1)}, u32[]{:S(2)}, u32[]{:S(2)}) collective-permute-start(bf16[1024,256]{1,0:T(8,128)(2,1)S(1)} %shard_map.82), channel_id=1, source_target_pairs={{0,14},{2,0},{4,2},{6,4},{8,6},{10,8},{12,10},{14,12},{1,15},{3,1}... | collective-permute-start | bytes 1572872 | tf_op jit(solution)/shard_map/ppermute | solution.py:296
  67.4 6.7 %collective-permute-start.17 = (bf16[256,256]{1,0:T(8,128)(2,1)S(1)}, bf16[256,256]{1,0:T(8,128)(2,1)S(1)}, u32[]{:S(2)}, u32[]{:S(2)}) collective-permute-start(bf16[256,256]{1,0:T(8,128)(2,1)S(1)} %get-tuple-element.42), channel_id=1, source_target_pairs={{0,112},{16,0},{32,16},{48,32},{64,48},{80,64},{96,80},{112,96},{1... | collective-permute-start | bytes 393224 | tf_op jit(solution)/shard_map/ppermute | solution.py:292
  67.8 7.7 %collective-permute-start.19 = (bf16[256,256]{1,0:T(8,128)(2,1)S(1)}, bf16[256,256]{1,0:T(8,128)(2,1)S(1)}, u32[]{:S(2)}, u32[]{:S(2)}) collective-permute-start(bf16[256,256]{1,0:T(8,128)(2,1)S(1)} %get-tuple-element.43), channel_id=1, source_target_pairs={{0,80},{16,96},{32,112},{48,0},{64,16},{80,32},{96,48},{112,64},{1... | collective-permute-start | bytes 393224 | tf_op jit(solution)/shard_map/ppermute | solution.py:292
  69.5 13.0 %collective-permute-start.18 = (bf16[256,256]{1,0:T(8,128)(2,1)S(1)}, bf16[256,256]{1,0:T(8,128)(2,1)S(1)}, u32[]{:S(2)}, u32[]{:S(2)}) collective-permute-start(bf16[256,256]{1,0:T(8,128)(2,1)S(1)} %get-tuple-element.44), channel_id=1, source_target_pairs={{0,96},{16,112},{32,0},{48,16},{64,32},{80,48},{96,64},{112,80},{1... | collective-permute-start | bytes 393224 | tf_op jit(solution)/shard_map/ppermute | solution.py:292
  82.8 6.4 %collective-permute-start.21 = (bf16[256,256]{1,0:T(8,128)(2,1)S(1)}, bf16[256,256]{1,0:T(8,128)(2,1)S(1)}, u32[]{:S(2)}, u32[]{:S(2)}) collective-permute-start(bf16[256,256]{1,0:T(8,128)(2,1)S(1)} %get-tuple-element.39), channel_id=1, source_target_pairs={{0,112},{16,0},{32,16},{48,32},{64,48},{80,64},{96,80},{112,96},{1... | collective-permute-start | bytes 393224 | tf_op jit(solution)/shard_map/ppermute | solution.py:292
  82.9 7.8 %collective-permute-start.23 = (bf16[256,256]{1,0:T(8,128)(2,1)S(1)}, bf16[256,256]{1,0:T(8,128)(2,1)S(1)}, u32[]{:S(2)}, u32[]{:S(2)}) collective-permute-start(bf16[256,256]{1,0:T(8,128)(2,1)S(1)} %get-tuple-element.40), channel_id=1, source_target_pairs={{0,80},{16,96},{32,112},{48,0},{64,16},{80,32},{96,48},{112,64},{1... | collective-permute-start | bytes 393224 | tf_op jit(solution)/shard_map/ppermute | solution.py:292
  84.4 7.8 %collective-permute-start.22 = (bf16[256,256]{1,0:T(8,128)(2,1)S(1)}, bf16[256,256]{1,0:T(8,128)(2,1)S(1)}, u32[]{:S(2)}, u32[]{:S(2)}) collective-permute-start(bf16[256,256]{1,0:T(8,128)(2,1)S(1)} %get-tuple-element.41), channel_id=1, source_target_pairs={{0,96},{16,112},{32,0},{48,16},{64,32},{80,48},{96,64},{112,80},{1... | collective-permute-start | bytes 393224 | tf_op jit(solution)/shard_map/ppermute | solution.py:292
  92.3 6.6 %collective-permute-start.24 = (bf16[2,128,256]{2,1,0:T(8,128)(2,1)S(1)}, bf16[2,128,256]{2,1,0:T(8,128)(2,1)S(1)}, u32[]{:S(2)}, u32[]{:S(2)}) collective-permute-start(bf16[2,128,256]{2,1,0:T(8,128)(2,1)S(1)} %pad_maximum_fusion.2), channel_id=1, source_target_pairs={{0,1},{1,0},{2,3},{3,2},{4,5},{5,4},{6,7},{7,6},{8,9},{9,8},{10,11... | collective-permute-start | bytes 393224 | tf_op jit(solution)/shard_map/ppermute | solution.py:273
  (4 other events, 38.9 us)

commit v3 on v2

v3 whole, which is shorter than its diff:
```python
import functools
import math

import jax
import jax.numpy as jnp
from jax import lax
from jax.experimental import pallas as pl
from jax.experimental.pallas import tpu as pltpu
from jax.sharding import PartitionSpec as P

HEAD = 128
GROUP = 6
KV = 2
WIN = 4
SPAN = 128
NEAR, FAR = (0, 1, 2, 3), (4, 5, 6, 7)
COLS = GROUP * HEAD
Y = 4
NEG = -1e30
SCALE = 1.0 / math.sqrt(HEAD)
SCALE2 = SCALE * math.log2(math.e)
NT = (((1,), (1,)), ((), ()))
NN = (((1,), (0,)), ((), ()))
SMALL = pltpu.CompilerParams(vmem_limit_bytes=6 * 1024 * 1024)


def dot(a, b, dims):
    return lax.dot_general(a, b, dims, preferred_element_type=jnp.float32)


def attend(j, order_any, ins, p_ref, ds_ref, q_ref, do_ref, kt_ref, scratch):
    q_own, do_own, q_far, do_far = ins[:4]
    near_in, far_in = ins[4:12], ins[12:]
    e_scr, dp_scr, k_scr, v_scr, order, sem = scratch
    inner, outer, head = lax.axis_index("inner"), lax.axis_index("outer"), lax.axis_index("head")
    copy = pltpu.make_async_copy(order_any, order, sem)
    copy.start()
    for n in range(16):
        both = near_in[n][j] if n < 8 else far_in[0][n - 8]
        at_r = slice(n * SPAN, (n + 1) * SPAN)
        k_scr[at_r, :] = both[:, :HEAD]
        v_scr[at_r, :] = both[:, HEAD:]
        kt_ref[:, at_r] = both[:, :HEAD].T
    copy.wait()

    def span_of(d, o, half):
        block = lax.rem(inner + 8 - d, 8) * 8 + lax.rem(outer + 8 - o, 8)
        return order[block * 2 + (head if half == 0 else 1 - head)]

    lane = lax.broadcasted_iota(jnp.int32, (1, 256), 1)
    at = [span_of(0, 0, 0), span_of(0, 0, 1)]
    hidden = []
    for n in range(8):
        for half in range(2):
            key = span_of(n % WIN, n // WIN, half)
            first = jnp.where(key <= at[0], 0.0, -NEG)
            second = jnp.where(key <= at[1], 0.0, -NEG)
            hidden.append(jnp.where(lane < SPAN, first, second).astype(jnp.float32))
    row = lax.broadcasted_iota(jnp.int32, (256, 256), 0)
    col = lax.broadcasted_iota(jnp.int32, (256, 256), 1)
    key_pos = jnp.where(row < SPAN, at[0], at[1]) * SPAN + (row & (SPAN - 1))
    row_pos = jnp.where(col < SPAN, at[0], at[1]) * SPAN + (col & (SPAN - 1))
    own_visible = key_pos <= row_pos

    for g in range(GROUP):
        at_h = slice(g * HEAD, (g + 1) * HEAD)
        rows = slice(g * 256, (g + 1) * 256)
        q_h = jnp.concatenate([q_own[:, at_h], q_far[:, at_h]], axis=0)
        do_h = jnp.concatenate([do_own[:, at_h], do_far[:, at_h]], axis=0)
        q_ref[rows, :] = q_h
        do_ref[rows, :] = do_h
        top = jnp.full((1, 256), NEG, jnp.float32)
        tops = []
        total = jnp.zeros((8, 256), jnp.float32)
        row_dot = jnp.zeros((8, 256), jnp.float32)
        for n in range(8):
            at_r = slice(n * 256, (n + 1) * 256)
            s = dot(k_scr[at_r, :], q_h, NT)
            if n == 0:
                s = jnp.where(own_visible, s, NEG)
            dp = dot(v_scr[at_r, :], do_h, NT)
            dp_scr[at_r, :] = dp
            before = top
            for half in range(2):
                here = jnp.max(s[half * 128 : (half + 1) * 128], axis=0, keepdims=True)
                top = jnp.maximum(top, (here - hidden[2 * n + half] if n else here) * SCALE2)
            tops.append(top)
            if n:
                decay = jnp.exp2(before - top)
                total, row_dot = total * decay, row_dot * decay
            for half in range(2):
                at_e = slice(n * 256 + half * 128, n * 256 + half * 128 + 128)
                lower = top + hidden[2 * n + half] if n else top
                e = jnp.exp2(s[half * 128 : (half + 1) * 128] * SCALE2 - lower)
                e_scr[at_e, :] = e
                total = total + jnp.sum(e.reshape(16, 8, 256), axis=0)
                product = e * dp[half * 128 : (half + 1) * 128]
                row_dot = row_dot + jnp.sum(product.reshape(16, 8, 256), axis=0)
        inverse = 1.0 / jnp.sum(total, axis=0, keepdims=True)
        row_dot = jnp.sum(row_dot, axis=0, keepdims=True) * inverse
        for n in range(8):
            at_r = slice(n * 256, (n + 1) * 256)
            p = e_scr[at_r, :] * (inverse * jnp.exp2(tops[n] - top))
            ds = p * (dp_scr[at_r, :] - row_dot)
            p_ref[at_r, rows] = p.astype(jnp.bfloat16)
            ds_ref[at_r, rows] = ds.astype(jnp.bfloat16)


def terms(ns, p, ds, q, do, out):
    for i, n in enumerate(ns):
        at_r, at_o = slice(n * 256, (n + 1) * 256), slice(i * 256, (i + 1) * 256)
        out[at_o, :HEAD] = (dot(ds[at_r, :], q[...], NN) * SCALE).astype(jnp.bfloat16)
        out[at_o, HEAD:] = dot(p[at_r, :], do[...], NN).astype(jnp.bfloat16)


def row_gradient(ds, kt, dq_own, dq_far):
    for g in range(GROUP):
        dq = dot(kt[...], ds[:, g * 256 : (g + 1) * 256], NN) * SCALE
        dq = dq.T.astype(jnp.bfloat16)
        dq_own[:, g * HEAD : (g + 1) * HEAD] = dq[:SPAN]
        dq_far[:, g * HEAD : (g + 1) * HEAD] = dq[SPAN:]


def whole_kernel(j, order, *refs):
    ins, (far_out, near_out, dq_own, dq_far) = refs[:13], refs[13:17]
    p, ds, q, do, kt = refs[17:22]
    attend(j, order, ins, p, ds, q, do, kt, refs[22:])
    terms(FAR, p, ds, q, do, far_out)
    terms(NEAR, p, ds, q, do, near_out)
    row_gradient(ds, kt, dq_own, dq_far)


def early_kernel(j, order, *refs):
    (q_own, do_own, far), (far_out, p, ds, q, do, kt) = refs[:3], refs[12:18]
    ins = (q_own, do_own, far.at[0], far.at[1], *refs[3:12])
    attend(j, order, ins, p, ds, q, do, kt, refs[18:])
    terms(FAR, p, ds, q, do, far_out)


def late_kernel(p, ds, q, do, kt, near_out, dq_own, dq_far):
    terms(NEAR, p, ds, q, do, near_out)
    row_gradient(ds, kt, dq_own, dq_far)


TERMS = jax.ShapeDtypeStruct((WIN * 256, 256), jnp.bfloat16)
ROWS = jax.ShapeDtypeStruct((SPAN, COLS), jnp.bfloat16)
KEPT = (
    jax.ShapeDtypeStruct((2048, GROUP * 256), jnp.bfloat16),
    jax.ShapeDtypeStruct((2048, GROUP * 256), jnp.bfloat16),
    jax.ShapeDtypeStruct((GROUP * 256, HEAD), jnp.bfloat16),
    jax.ShapeDtypeStruct((GROUP * 256, HEAD), jnp.bfloat16),
    jax.ShapeDtypeStruct((HEAD, 2048), jnp.bfloat16),
)


def work(scores, near, rows):
    flops = 8 * 6 * 256 * 2048 * 128 * (3 * scores + near + rows)
    return pl.CostEstimate(
        flops=flops, bytes_accessed=5_000_000, transcendentals=scores * 6 * 256 * 2048
    )


def attention(j, split, order, own, far, near_in, far_in):
    free = pl.BlockSpec(memory_space=pl.ANY)
    vmem = pl.BlockSpec(memory_space=pltpu.VMEM)
    kept = [pltpu.VMEM(x.shape, x.dtype) for x in KEPT]
    out = (TERMS, *KEPT) if split else (TERMS, TERMS, ROWS, ROWS)
    return pl.pallas_call(
        functools.partial(early_kernel if split else whole_kernel, j),
        in_specs=[free] + [vmem] * (2 + len(far) + 8 + len(far_in)),
        out_specs=[vmem] * len(out),
        out_shape=out,
        scratch_shapes=([] if split else kept)
        + [
            pltpu.VMEM((2048, 256), jnp.float32),
            pltpu.VMEM((2048, 256), jnp.float32),
            pltpu.VMEM((2048, HEAD), jnp.bfloat16),
            pltpu.VMEM((2048, HEAD), jnp.bfloat16),
            pltpu.SMEM((2 * 64,), jnp.int32),
            pltpu.SemaphoreType.DMA,
        ],
        compiler_params=pltpu.CompilerParams(vmem_limit_bytes=(20 if split else 32) * 1024 * 1024),
        cost_estimate=work(1, 0 if split else 1, 0 if split else 1),
    )(order, *own, *far, *near_in, *far_in)


def rest(kept):
    vmem = pl.BlockSpec(memory_space=pltpu.VMEM)
    return pl.pallas_call(
        late_kernel,
        in_specs=[vmem] * 5,
        out_specs=[vmem] * 3,
        out_shape=(TERMS, ROWS, ROWS),
        compiler_params=pltpu.CompilerParams(vmem_limit_bytes=8 * 1024 * 1024),
        cost_estimate=pl.CostEstimate(flops=1_000_000, bytes_accessed=1_000_000, transcendentals=0),
    )(*kept)


def pack_kernel(*refs):
    halves, out = refs[:8], refs[-2:]
    for j in range(KV):
        for n in range(8):
            out[j][n] = halves[n][j]


def pack(near, *after):
    vmem = pl.BlockSpec(memory_space=pltpu.VMEM)
    one = jax.ShapeDtypeStruct((8, SPAN, 256), jnp.bfloat16)
    return pl.pallas_call(
        pack_kernel,
        in_specs=[vmem] * 8 + [pl.BlockSpec(memory_space=pl.ANY)] * len(after),
        out_specs=[vmem] * 2,
        out_shape=[one] * 2,
        compiler_params=SMALL,
    )(*near, *after)


def tie_kernel(*refs):
    del refs


def tie(x, *after):
    free = pl.BlockSpec(memory_space=pl.ANY)
    return pl.pallas_call(
        tie_kernel,
        in_specs=[free] * (1 + len(after)),
        out_specs=free,
        out_shape=jax.ShapeDtypeStruct(x.shape, x.dtype),
        input_output_aliases={0: 0},
        compiler_params=SMALL,
    )(x, *after)


def join_rows_kernel(own0, own1, back0, back1, out):
    head = lax.axis_index("head")
    for x, h, j in ((own0, head, 0), (own1, head, 1), (back0, 1 - head, 0), (back1, 1 - head, 1)):
        out[:, pl.ds(pl.multiple_of((h * KV + j) * COLS, COLS), COLS)] = x[...]


def join_rows(own, back):
    vmem = pl.BlockSpec(memory_space=pltpu.VMEM)
    return pl.pallas_call(
        join_rows_kernel,
        in_specs=[vmem] * 4,
        out_specs=vmem,
        out_shape=jax.ShapeDtypeStruct((SPAN, 2 * KV * COLS), jnp.bfloat16),
        compiler_params=SMALL,
    )(*own, *back)


def cut_kernel(queries, output_gradient, order, after, *refs):
    del after
    order_out, sems = refs[5:]
    outs = [*refs[:4], refs[4].at[0], refs[4].at[1]]
    head = lax.axis_index("head")
    copies = [pltpu.make_async_copy(order, order_out, sems.at[6])]
    for n, out in enumerate(outs):
        at, m = (head, n) if n < 4 else (1 - head, n - 2)
        at = pl.ds(pl.multiple_of((at * KV + m // 2) * COLS, COLS), COLS)
        copies.append(
            pltpu.make_async_copy((queries, output_gradient)[m % 2].at[:, at], out, sems.at[n])
        )
    for copy in copies:
        copy.start()
    for copy in copies:
        copy.wait()


def cut(queries, output_gradient, order, after):
    vmem = pl.BlockSpec(memory_space=pltpu.VMEM)
    free = pl.BlockSpec(memory_space=pl.ANY)
    out = pl.pallas_call(
        cut_kernel,
        in_specs=[free] * 4,
        out_specs=[vmem] * 6,
        out_shape=[ROWS] * 4
        + [
            jax.ShapeDtypeStruct((2, *ROWS.shape), ROWS.dtype),
            jax.ShapeDtypeStruct(order.shape, order.dtype),
        ],
        scratch_shapes=[pltpu.SemaphoreType.DMA((7,))],
        compiler_params=pltpu.CompilerParams(vmem_limit_bytes=6 * 1024 * 1024),
    )(queries, output_gradient, order, after)
    return (out[:2], out[2:4]), out[4], out[5]


def join_terms_kernel(mine0, mine1, theirs, dk, dv):
    head = lax.axis_index("head")
    for j, mine in enumerate((mine0, mine1)):
        at = pl.ds(pl.multiple_of((head * KV + j) * HEAD, HEAD), HEAD)
        there = pl.ds(pl.multiple_of(((1 - head) * KV + j) * HEAD, HEAD), HEAD)
        dk[:, at] = mine[:, :HEAD]
        dv[:, at] = mine[:, HEAD:]
        dk[:, there] = theirs[j, :, :HEAD]
        dv[:, there] = theirs[j, :, HEAD:]


def join_terms(mine, theirs):
    vmem = pl.BlockSpec(memory_space=pltpu.VMEM)
    out = jax.ShapeDtypeStruct((SPAN, 2 * KV * HEAD), jnp.bfloat16)
    return pl.pallas_call(
        join_terms_kernel,
        in_specs=[vmem] * 3,
        out_specs=[vmem] * 2,
        out_shape=[out] * 2,
        compiler_params=SMALL,
    )(*mine, theirs)


def to_partner(x):
    return lax.ppermute(x, "head", [(0, 1), (1, 0)])


def across(x):
    perm = []
    for lo in range(2):
        for y in (1, 2, 3):
            for h in range(2):
                perm.append(((lo * Y + y) * 2 + h, ((1 - lo) * Y + y) * 2 + 1 - h))
    return lax.ppermute(x, ("inner", "head"), perm)


def along_y(x, by):
    return lax.ppermute(
        x, "inner", [(lo * Y + y, lo * Y + (y + by) % Y) for lo in range(2) for y in range(Y)]
    )


def along_inner(x, by):
    return lax.ppermute(x, "inner", [(i, (i + by) % 8) for i in range(8)])


def along_outer(x, by):
    return lax.ppermute(x, "outer", [(o, (o + by) % 8) for o in range(8)])


def f32(x):
    return x.astype(jnp.float32)


def bf16(x):
    return x.astype(jnp.bfloat16)


def send_terms(near_out, arrived):
    total = f32(near_out) + f32(arrived)
    return total[:256], [along_inner(bf16(total[k * 256 : (k + 1) * 256]), -k) for k in (1, 2, 3)]


def shards(queries, keys, values, output_gradient, span_order):
    inner, head = lax.axis_index("inner"), lax.axis_index("head")
    y = lax.rem(inner, Y)

    def cols(x, at, width):
        return lax.dynamic_slice_in_dim(x, at, width, axis=1)

    def piece(of):
        return jnp.stack(
            [
                jnp.concatenate([cols(x, (of * KV + j) * HEAD, HEAD) for x in (keys, values)], axis=1)
                for j in range(KV)
            ]
        )

    mine, theirs = piece(head), piece(1 - head)
    near = [[mine, to_partner(theirs)]]
    other = across(theirs)
    straight = [along_inner(mine, k) for k in (1, 2, 3)]
    for k in (1, 2, 3):
        near.append([straight[k - 1], along_y(jnp.where(y + k >= Y, other, near[0][1]), k)])
    near = [half for block in near for half in block]
    own, far, order = cut(queries, output_gradient, span_order, near[3])
    first_far = [cols(x, (1 - head) * KV * COLS, COLS) for x in (queries, output_gradient)]
    far = [[to_partner(x) for x in first_far], [to_partner(far)]]
    far_in = [(along_outer(x, 1),) for x in pack(near, far[0][0])]
    far_out0, near_out0, dq_own0, dq_far0 = attention(0, False, order, own[0], far[0], near, far_in[0])
    back0 = to_partner(dq_far0)
    arrived0 = along_outer(far_out0, -1)
    far_out1, *kept = attention(1, True, order, own[1], far[1], near, far_in[1])
    arrived1 = along_outer(tie(far_out1, arrived0), -1)
    total0, moved0 = send_terms(tie(near_out0, back0), arrived0)
    near_out1, dq_own1, dq_far1 = rest(kept)
    back1 = to_partner(dq_far1)
    total1, moved1 = send_terms(tie(near_out1, *moved0), arrived1)
    sums = [total0, total1]
    for n, moved in enumerate((moved0, moved1)):
        for x in moved:
            sums[n] = sums[n] + f32(x)
    theirs = to_partner(jnp.stack([bf16(s[SPAN:]) for s in sums]))
    dk, dv = join_terms([bf16(s[:SPAN]) for s in sums], theirs)
    return join_rows((dq_own0, dq_own1), (back0, back1)), dk, dv


def solution(mesh):
    rows = P(("inner", "outer", "head"), None)
    return jax.shard_map(
        shards,
        mesh=mesh,
        in_specs=(rows, rows, rows, rows, P()),
        out_specs=(rows, rows, rows),
        check_vma=False,
    )
```

time: 102 us -> 92.8 us (0.910); the launches traced: 100 us -> 92.4 us
  waiting for transfers between devices: 29.7 us -> 21.8 us
  local copies, waits for them, and re-layouts: 1.11 us -> 5.79 us
  Pallas kernels: 29.3 us -> 25.2 us
    ppermute x9, waiting for transfers between devices: 16.7 us -> 12.5 us  [along_inner(): return lax.ppermute(x, 'inner', [(i, (i + by) % 8) for i in range(8)])]
    pallas_call x5 -> x6, Pallas kernels: 29.2 us -> 25.1 us  [the longest x2 20.5 us: attention(): pl.pallas_call(functools.partial(early_kernel if split else whole_kernel,...]
    unnamed x6, local copies, waits for them, and re-layouts: 0.01 us -> 2.92 us
    dynamic_slice x1 -> x3, local copies, waits for them, and re-layouts: 1.02 us -> 2.8 us  [cols(): return lax.dynamic_slice_in_dim(x, at, width, axis=1)]
    ppermute x1, starting transfers between devices: 4.67 us -> 3.04 us  [across(): return lax.ppermute(x, ('inner', 'head'), perm)]
    ppermute x4, waiting for transfers between devices: 1.42 us -> 0.08 us  [along_outer(): return lax.ppermute(x, 'outer', [(o, (o + by) % 8) for o in range(8)])]
    ppermute x8 -> x7, waiting for transfers between devices: 6.5 us -> 5.22 us  [to_partner(): return lax.ppermute(x, 'head', [(0, 1), (1, 0)])]
    ppermute x3, waiting for transfers between devices: 5.16 us -> 3.95 us  [along_y(): lax.ppermute(x, 'inner', [(lo * Y + y, lo * Y + (y + by) % Y) for lo in r...]
  transfers between devices with their start and end apart: 25 -> 24, of which waited for: 13 -> 10; matrix products, arithmetic and copies ran while one was open for 0% -> 3% of each run, Pallas kernels for 28% -> 26%
where the time goes in v3:
time: 92.8 us; the launch traced here: 92.4 us
  starting transfers between devices  38.2 us (41%)
  Pallas kernels  25.2 us (27%)
  waiting for transfers between devices  21.8 us (23%)
  local copies, waits for them, and re-layouts  5.79 us (6%)
    pallas_call x2, Pallas kernels, attention(): pl.pallas_call(functools.partial(early_kernel if split else whole_kernel,...  20.5 us
    ppermute x7, starting transfers between devices, to_partner(): return lax.ppermute(x, 'head', [(0, 1), (1, 0)])  15.7 us
    ppermute x9, waiting for transfers between devices, along_inner(): return lax.ppermute(x, 'inner', [(i, (i + by) % 8) for i in range(8)])  12.5 us
    ppermute x9, starting transfers between devices, along_inner(): return lax.ppermute(x, 'inner', [(i, (i + by) % 8) for i in range(8)])  10.5 us
    ppermute x7, waiting for transfers between devices, to_partner(): return lax.ppermute(x, 'head', [(0, 1), (1, 0)])  5.22 us
    ppermute x4, starting transfers between devices, along_outer(): return lax.ppermute(x, 'outer', [(o, (o + by) % 8) for o in range(8)])  4.75 us
    ppermute x3, starting transfers between devices, along_y(): lax.ppermute(x, 'inner', [(lo * Y + y, lo * Y + (y + by) % Y) for lo in r...  4.3 us
    ppermute x3, waiting for transfers between devices, along_y(): lax.ppermute(x, 'inner', [(lo * Y + y, lo * Y + (y + by) % Y) for lo in r...  3.95 us
  transfers between devices with their start and end apart: 24, of which 10 were waited for; matrix products, arithmetic and copies ran while one was open for 3% of the time, Pallas kernels for 26%

profile of v3, /device:TPU:16, one launch (start us, length us, event | category | flops | bytes accessed | tf_op | source)
XLA Modules:
  0.0 92.4 jit_solution(14976193889090183956)
XLA Ops:
  1.6 3.1 %collective-permute-start.1 = (bf16[2,128,256]{2,1,0:T(8,128)(2,1)S(1)}, bf16[2,128,256]{2,1,0:T(8,128)(2,1)S(1)}, u32[]{:S(2)}, u32[]{:S(2)}) collective-permute-start(bf16[2,128,256]{2,1,0:T(8,128)(2,1)S(1)} %pad_maximum_fusion), channel_id=1, source_target_pairs={{0,1},{1,0},{2,3},{3,2},{4,5},{5,4},{6,7},{7,6},{8,9},{9,8},{10,11... | collective-permute-start | bytes 393224 | tf_op jit(solution)/shard_map/ppermute | solution.py:311
  4.7 3.0 %collective-permute-start = (bf16[2,128,256]{2,1,0:T(8,128)(2,1)S(1)}, bf16[2,128,256]{2,1,0:T(8,128)(2,1)S(1)}, u32[]{:S(2)}, u32[]{:S(2)}) collective-permute-start(bf16[2,128,256]{2,1,0:T(8,128)(2,1)S(1)} %pad_maximum_fusion), channel_id=1, source_target_pairs={{16,81},{17,80},{32,97},{33,96},{48,113},{49,112},{80,17},{81,16},... | collective-permute-start | bytes 393224 | tf_op jit(solution)/shard_map/ppermute | solution.py:320
  7.9 2.2 %collective-permute-start.6 = (bf16[2,128,256]{2,1,0:T(8,128)(2,1)S(1)}, bf16[2,128,256]{2,1,0:T(8,128)(2,1)S(1)}, u32[]{:S(2)}, u32[]{:S(2)}) collective-permute-start(bf16[2,128,256]{2,1,0:T(8,128)(2,1)S(1)} %pad_maximum_fusion.1.refs_0_.refs_4_.refs_3_), channel_id=1, source_target_pairs={{0,32},{16,48},{32,64},{48,80},{64,96},{80,112},{96,0},{112,16},{1... | collective-permute-start | bytes 393224 | tf_op jit(solution)/shard_map/ppermute | solution.py:330
  11.1 4.2 %collective-permute-start.3 = (bf16[128,768]{1,0:T(8,128)(2,1)S(1)}, bf16[128,768]{1,0:T(8,128)(2,1)S(1)}, u32[]{:S(2)}, u32[]{:S(2)}) collective-permute-start(bf16[128,768]{1,0:T(8,128)(2,1)S(1)} %constant_dynamic-slice_fusion.5), channel_id=1, source_target_pairs={{0,1},{1,0},{2,3},{3,2},{4,5},{5,4},{6,7},{7,6},{8,9},{9,8},{10,11... | collective-permute-start | bytes 589832 | tf_op jit(solution)/shard_map/ppermute | solution.py:311
  15.3 2.1 %collective-permute-start.9 = (bf16[2,128,256]{2,1,0:T(8,128)(2,1)S(1)}, bf16[2,128,256]{2,1,0:T(8,128)(2,1)S(1)}, u32[]{:S(2)}, u32[]{:S(2)}) collective-permute-start(bf16[2,128,256]{2,1,0:T(8,128)(2,1)S(1)} %get-tuple-element.59), channel_id=1, source_target_pairs={{0,48},{16,0},{32,16},{48,32},{64,112},{80,64},{96,80},{112,96},{1... | collective-permute-start | bytes 393224 | tf_op jit(solution)/shard_map/ppermute | solution.py:324
  17.4 1.5 %collective-permute-start.7 = (bf16[2,128,256]{2,1,0:T(8,128)(2,1)S(1)}, bf16[2,128,256]{2,1,0:T(8,128)(2,1)S(1)}, u32[]{:S(2)}, u32[]{:S(2)}) collective-permute-start(bf16[2,128,256]{2,1,0:T(8,128)(2,1)S(1)} %get-tuple-element.60), channel_id=1, source_target_pairs={{0,32},{16,48},{32,0},{48,16},{64,96},{80,112},{96,64},{112,80},{1... | collective-permute-start | bytes 393224 | tf_op jit(solution)/shard_map/ppermute | solution.py:324
  19.6 1.7 %collective-permute-done.3.refs_8_.refs_2_ = bf16[128,768]{1,0:T(8,128)(2,1)S(1)} collective-permute-done((bf16[128,768]{1,0:T(8,128)(2,1)S(1)}, bf16[128,768]{1,0:T(8,128)(2,1)S(1)}, u32[]{:S(2)}, u32[]{:S(2)}) %collective-permute-start.3) | collective-permute-done | bytes 196640 | tf_op jit(solution)/shard_map/ppermute | solution.py:311
  22.1 1.9 %collective-permute-done.7.refs_5_.refs_9_.refs_8_ = bf16[2,128,256]{2,1,0:T(8,128)(2,1)S(1)} collective-permute-done((bf16[2,128,256]{2,1,0:T(8,128)(2,1)S(1)}, bf16[2,128,256]{2,1,0:T(8,128)(2,1)S(1)}, u32[]{:S(2)}, u32[]{:S(2)}) %collective-permute-start.7) | collective-permute-done | bytes 131104 | tf_op jit(solution)/shard_map/ppermute | solution.py:324
  26.8 1.7 %collective-permute-start.12 = (bf16[8,128,256]{2,1,0:T(8,128)(2,1)S(1)}, bf16[8,128,256]{2,1,0:T(8,128)(2,1)S(1)}, u32[]{:S(2)}, u32[]{:S(2)}) collective-permute-start(bf16[8,128,256]{2,1,0:T(8,128)(2,1)S(1)} %get-tuple-element.34), channel_id=1, source_target_pairs={{0,2},{2,4},{4,6},{6,8},{8,10},{10,12},{12,14},{14,0},{1,3},{3,5},... | collective-permute-start | bytes 1572872 | tf_op jit(solution)/shard_map/ppermute | solution.py:334
  31.7 3.4 %collective-permute-start.11 = (bf16[2,128,768]{2,1,0:T(8,128)(2,1)S(1)}, bf16[2,128,768]{2,1,0:T(8,128)(2,1)S(1)}, u32[]{:S(2)}, u32[]{:S(2)}) collective-permute-start(bf16[2,128,768]{2,1,0:T(8,128)(2,1)S(1)} %get-tuple-element.33), channel_id=1, source_target_pairs={{0,1},{1,0},{2,3},{3,2},{4,5},{5,4},{6,7},{7,6},{8,9},{9,8},{10,11... | collective-permute-start | bytes 1179656 | tf_op jit(solution)/shard_map/ppermute | solution.py:311
  35.2 10.9 %shard_map.78 = (bf16[1024,256]{1,0:T(8,128)(2,1)S(1)}, bf16[1024,256]{1,0:T(8,128)(2,1)S(1)}, bf16[128,768]{1,0:T(8,128)(2,1)S(1)}, bf16[128,768]{1,0:T(8,128)(2,1)S(1)}) custom-call(s32[128]{0:T(128)S(1)} %get-tuple-element.26.order, bf16[128,768]{1,0:T(8,128)(2,1)S(1)} %get-tuple-element.27.refs_0_, bf16[128,768]{1,0:T(8,128)(2,1)S(1)} %get-tuple-element.28.refs_1_, ...), custom_call_target="tpu_custom_call" | custom-call | flops 16106127360 | bytes 5000000 | tf_op jit(solution)/shard_map/pallas_call | solution.py:168
  47.4 9.6 %shard_map.79 = (bf16[1024,256]{1,0:T(8,128)(2,1)S(1)}, bf16[2048,1536]{1,0:T(8,128)(2,1)S(1)}, bf16[2048,1536]{1,0:T(8,128)(2,1)S(1)}, bf16[1536,128]{1,0:T(8,1...) custom-call(s32[128]{0:T(128)S(1)} %get-tuple-element.26.order, ...), custom_call_target="tpu_custom_call" | custom-call | flops 9663676416 | bytes 5000000 | tf_op jit(solution)/shard_map/pallas_call | solution.py:168
  57.0 2.4 %collective-permute-start.19 = (bf16[1024,256]{1,0:T(8,128)(2,1)S(1)}, bf16[1024,256]{1,0:T(8,128)(2,1)S(1)}, u32[]{:S(2)}, u32[]{:S(2)}) collective-permute-start(bf16[1024,256]{1,0:T(8,128)(2,1)S(1)} %shard_map.84), channel_id=1, source_target_pairs={{0,14},{2,0},{4,2},{6,4},{8,6},{10,8},{12,10},{14,12},{1,15},{3,1}... | collective-permute-start | bytes 1572872 | tf_op jit(solution)/shard_map/ppermute | solution.py:334
  60.3 2.4 %collective-permute-start.18 = (bf16[256,256]{1,0:T(8,128)(2,1)S(1)}, bf16[256,256]{1,0:T(8,128)(2,1)S(1)}, u32[]{:S(2)}, u32[]{:S(2)}) collective-permute-start(bf16[256,256]{1,0:T(8,128)(2,1)S(1)} %get-tuple-element.57), channel_id=1, source_target_pairs={{0,80},{16,96},{32,112},{48,0},{64,16},{80,32},{96,48},{112,64},{1... | collective-permute-start | bytes 393224 | tf_op jit(solution)/shard_map/ppermute | solution.py:330
  62.7 3.1 %collective-permute-start.17 = (bf16[256,256]{1,0:T(8,128)(2,1)S(1)}, bf16[256,256]{1,0:T(8,128)(2,1)S(1)}, u32[]{:S(2)}, u32[]{:S(2)}) collective-permute-start(bf16[256,256]{1,0:T(8,128)(2,1)S(1)} %get-tuple-element.58), channel_id=1, source_target_pairs={{0,96},{16,112},{32,0},{48,16},{64,32},{80,48},{96,64},{112,80},{1... | collective-permute-start | bytes 393224 | tf_op jit(solution)/shard_map/ppermute | solution.py:330
  65.8 2.7 %shard_map.80 = (bf16[1024,256]{1,0:T(8,128)(2,1)S(1)}, bf16[128,768]{1,0:T(8,128)(2,1)S(1)}, bf16[128,768]{1,0:T(8,128)(2,1)S(1)}) custom-call(bf16[2048,1536]{1,0:T(8,128)(2,1)S(1)} %get-tuple-element.35.p, bf16[2048,1536]{1,0:T(8,128)(2,1)S(1)} %get-tuple-element.36.ds, bf16[1536,128]{1,0:T(8,128)(2,1)S(1)} %get-tuple-element.37.q, ...), custom_call_target="tpu_custom_call" | custom-call | flops 1000000 | bytes 1000000 | tf_op jit(solution)/shard_map/pallas_call | solution.py:189
  68.5 1.8 %collective-permute-start.14 = (bf16[128,768]{1,0:T(8,128)(2,1)S(1)}, bf16[128,768]{1,0:T(8,128)(2,1)S(1)}, u32[]{:S(2)}, u32[]{:S(2)}) collective-permute-start(bf16[128,768]{1,0:T(8,128)(2,1)S(1)} %get-tuple-element.42), channel_id=1, source_target_pairs={{0,1},{1,0},{2,3},{3,2},{4,5},{5,4},{6,7},{7,6},{8,9},{9,8},{10,11... | collective-permute-start | bytes 589832 | tf_op jit(solution)/shard_map/ppermute | solution.py:311
  70.3 3.9 %collective-permute-done.17.refs_2_ = bf16[256,256]{1,0:T(8,128)(2,1)S(1)} collective-permute-done((bf16[256,256]{1,0:T(8,128)(2,1)S(1)}, bf16[256,256]{1,0:T(8,128)(2,1)S(1)}, u32[]{:S(2)}, u32[]{:S(2)}) %collective-permute-start.17) | collective-permute-done | bytes 131104 | tf_op jit(solution)/shard_map/ppermute | solution.py:330
  74.5 1.9 %collective-permute-start.22 = (bf16[256,256]{1,0:T(8,128)(2,1)S(1)}, bf16[256,256]{1,0:T(8,128)(2,1)S(1)}, u32[]{:S(2)}, u32[]{:S(2)}) collective-permute-start(bf16[256,256]{1,0:T(8,128)(2,1)S(1)} %get-tuple-element.54), channel_id=1, source_target_pairs={{0,80},{16,96},{32,112},{48,0},{64,16},{80,32},{96,48},{112,64},{1... | collective-permute-start | bytes 393224 | tf_op jit(solution)/shard_map/ppermute | solution.py:330
  76.3 3.1 %collective-permute-done.20 = bf16[256,256]{1,0:T(8,128)(2,1)S(1)} collective-permute-done((bf16[256,256]{1,0:T(8,128)(2,1)S(1)}, bf16[256,256]{1,0:T(8,128)(2,1)S(1)}, u32[]{:S(2)}, u32[]{:S(2)}) %collective-permute-start.20) | collective-permute-done | bytes 131104 | tf_op jit(solution)/shard_map/ppermute | solution.py:330
  79.4 1.8 %collective-permute-done.22 = bf16[256,256]{1,0:T(8,128)(2,1)S(1)} collective-permute-done((bf16[256,256]{1,0:T(8,128)(2,1)S(1)}, bf16[256,256]{1,0:T(8,128)(2,1)S(1)}, u32[]{:S(2)}, u32[]{:S(2)}) %collective-permute-start.22) | collective-permute-done | bytes 131104 | tf_op jit(solution)/shard_map/ppermute | solution.py:330
  81.2 3.8 %collective-permute-done.21 = bf16[256,256]{1,0:T(8,128)(2,1)S(1)} collective-permute-done((bf16[256,256]{1,0:T(8,128)(2,1)S(1)}, bf16[256,256]{1,0:T(8,128)(2,1)S(1)}, u32[]{:S(2)}, u32[]{:S(2)}) %collective-permute-start.21) | collective-permute-done | bytes 131104 | tf_op jit(solution)/shard_map/ppermute | solution.py:330
  85.1 2.1 %collective-permute-start.23 = (bf16[2,128,256]{2,1,0:T(8,128)(2,1)S(1)}, bf16[2,128,256]{2,1,0:T(8,128)(2,1)S(1)}, u32[]{:S(2)}, u32[]{:S(2)}) collective-permute-start(bf16[2,128,256]{2,1,0:T(8,128)(2,1)S(1)} %pad_maximum_fusion.2), channel_id=1, source_target_pairs={{0,1},{1,0},{2,3},{3,2},{4,5},{5,4},{6,7},{7,6},{8,9},{9,8},{10,11... | collective-permute-start | bytes 393224 | tf_op jit(solution)/shard_map/ppermute | solution.py:311
  88.1 3.5 %collective-permute-done.23.theirs = bf16[2,128,256]{2,1,0:T(8,128)(2,1)S(1)} collective-permute-done((bf16[2,128,256]{2,1,0:T(8,128)(2,1)S(1)}, bf16[2,128,256]{2,1,0:T(8,128)(2,1)S(1)}, u32[]{:S(2)}, u32[]{:S(2)}) %collective-permute-start.23) | collective-permute-done | bytes 131104 | tf_op jit(solution)/shard_map/ppermute | solution.py:311
  (59 shorter events, 13.9 us)
Async XLA Ops:
  1.6 9.5 %collective-permute-start.1 = (bf16[2,128,256]{2,1,0:T(8,128)(2,1)S(1)}, bf16[2,128,256]{2,1,0:T(8,128)(2,1)S(1)}, u32[]{:S(2)}, u32[]{:S(2)}) collective-permute-start(bf16[2,128,256]{2,1,0:T(8,128)(2,1)S(1)} %pad_maximum_fusion), channel_id=1, source_target_pairs={{0,1},{1,0},{2,3},{3,2},{4,5},{5,4},{6,7},{7,6},{8,9},{9,8},{10,11... | collective-permute-start | bytes 393224 | tf_op jit(solution)/shard_map/ppermute | solution.py:311
  4.7 10.6 %collective-permute-start = (bf16[2,128,256]{2,1,0:T(8,128)(2,1)S(1)}, bf16[2,128,256]{2,1,0:T(8,128)(2,1)S(1)}, u32[]{:S(2)}, u32[]{:S(2)}) collective-permute-start(bf16[2,128,256]{2,1,0:T(8,128)(2,1)S(1)} %pad_maximum_fusion), channel_id=1, source_target_pairs={{16,81},{17,80},{32,97},{33,96},{48,113},{49,112},{80,17},{81,16},... | collective-permute-start | bytes 393224 | tf_op jit(solution)/shard_map/ppermute | solution.py:320
  7.8 9.6 %collective-permute-start.8 = (bf16[2,128,256]{2,1,0:T(8,128)(2,1)S(1)}, bf16[2,128,256]{2,1,0:T(8,128)(2,1)S(1)}, u32[]{:S(2)}, u32[]{:S(2)}) collective-permute-start(bf16[2,128,256]{2,1,0:T(8,128)(2,1)S(1)} %pad_maximum_fusion.1.refs_0_.refs_4_.refs_3_), channel_id=1, source_target_pairs={{0,48},{16,64},{32,80},{48,96},{64,112},{80,0},{96,16},{112,32},{1... | collective-permute-start | bytes 393224 | tf_op jit(solution)/shard_map/ppermute | solution.py:330
  7.9 11.0 %collective-permute-start.6 = (bf16[2,128,256]{2,1,0:T(8,128)(2,1)S(1)}, bf16[2,128,256]{2,1,0:T(8,128)(2,1)S(1)}, u32[]{:S(2)}, u32[]{:S(2)}) collective-permute-start(bf16[2,128,256]{2,1,0:T(8,128)(2,1)S(1)} %pad_maximum_fusion.1.refs_0_.refs_4_.refs_3_), channel_id=1, source_target_pairs={{0,32},{16,48},{32,64},{48,80},{64,96},{80,112},{96,0},{112,16},{1... | collective-permute-start | bytes 393224 | tf_op jit(solution)/shard_map/ppermute | solution.py:330
  10.1 9.5 %collective-permute-start.5 = (bf16[2,128,256]{2,1,0:T(8,128)(2,1)S(1)}, bf16[2,128,256]{2,1,0:T(8,128)(2,1)S(1)}, u32[]{:S(2)}, u32[]{:S(2)}) collective-permute-start(bf16[2,128,256]{2,1,0:T(8,128)(2,1)S(1)} %pad_maximum_fusion.1.refs_0_.refs_4_.refs_3_), channel_id=1, source_target_pairs={{0,16},{16,32},{32,48},{48,64},{64,80},{80,96},{96,112},{112,0},{1... | collective-permute-start | bytes 393224 | tf_op jit(solution)/shard_map/ppermute | solution.py:330
  11.1 10.2 %collective-permute-start.3 = (bf16[128,768]{1,0:T(8,128)(2,1)S(1)}, bf16[128,768]{1,0:T(8,128)(2,1)S(1)}, u32[]{:S(2)}, u32[]{:S(2)}) collective-permute-start(bf16[128,768]{1,0:T(8,128)(2,1)S(1)} %constant_dynamic-slice_fusion.5), channel_id=1, source_target_pairs={{0,1},{1,0},{2,3},{3,2},{4,5},{5,4},{6,7},{7,6},{8,9},{9,8},{10,11... | collective-permute-start | bytes 589832 | tf_op jit(solution)/shard_map/ppermute | solution.py:311
  15.3 6.8 %collective-permute-start.9 = (bf16[2,128,256]{2,1,0:T(8,128)(2,1)S(1)}, bf16[2,128,256]{2,1,0:T(8,128)(2,1)S(1)}, u32[]{:S(2)}, u32[]{:S(2)}) collective-permute-start(bf16[2,128,256]{2,1,0:T(8,128)(2,1)S(1)} %get-tuple-element.59), channel_id=1, source_target_pairs={{0,48},{16,0},{32,16},{48,32},{64,112},{80,64},{96,80},{112,96},{1... | collective-permute-start | bytes 393224 | tf_op jit(solution)/shard_map/ppermute | solution.py:324
  17.4 6.6 %collective-permute-start.7 = (bf16[2,128,256]{2,1,0:T(8,128)(2,1)S(1)}, bf16[2,128,256]{2,1,0:T(8,128)(2,1)S(1)}, u32[]{:S(2)}, u32[]{:S(2)}) collective-permute-start(bf16[2,128,256]{2,1,0:T(8,128)(2,1)S(1)} %get-tuple-element.60), channel_id=1, source_target_pairs={{0,32},{16,48},{32,0},{48,16},{64,96},{80,112},{96,64},{112,80},{1... | collective-permute-start | bytes 393224 | tf_op jit(solution)/shard_map/ppermute | solution.py:324
  18.9 6.4 %collective-permute-start.2 = (bf16[2,128,256]{2,1,0:T(8,128)(2,1)S(1)}, bf16[2,128,256]{2,1,0:T(8,128)(2,1)S(1)}, u32[]{:S(2)}, u32[]{:S(2)}) collective-permute-start(bf16[2,128,256]{2,1,0:T(8,128)(2,1)S(1)} %get-tuple-element.61), channel_id=1, source_target_pairs={{0,16},{16,32},{32,48},{48,0},{64,80},{80,96},{96,112},{112,64},{1... | collective-permute-start | bytes 393224 | tf_op jit(solution)/shard_map/ppermute | solution.py:324
  25.3 9.8 %collective-permute-start.10 = (bf16[8,128,256]{2,1,0:T(8,128)(2,1)S(1)}, bf16[8,128,256]{2,1,0:T(8,128)(2,1)S(1)}, u32[]{:S(2)}, u32[]{:S(2)}) collective-permute-start(bf16[8,128,256]{2,1,0:T(8,128)(2,1)S(1)} %get-tuple-element.29), channel_id=1, source_target_pairs={{0,2},{2,4},{4,6},{6,8},{8,10},{10,12},{12,14},{14,0},{1,3},{3,5},... | collective-permute-start | bytes 1572872 | tf_op jit(solution)/shard_map/ppermute | solution.py:334
  26.3 8.8 %collective-permute-start.4 = (bf16[128,768]{1,0:T(8,128)(2,1)S(1)}, bf16[128,768]{1,0:T(8,128)(2,1)S(1)}, u32[]{:S(2)}, u32[]{:S(2)}) collective-permute-start(bf16[128,768]{1,0:T(8,128)(2,1)S(1)} %constant_dynamic-slice_fusion.4), channel_id=1, source_target_pairs={{0,1},{1,0},{2,3},{3,2},{4,5},{5,4},{6,7},{7,6},{8,9},{9,8},{10,11... | collective-permute-start | bytes 589832 | tf_op jit(solution)/shard_map/ppermute | solution.py:311
  26.8 20.6 %collective-permute-start.12 = (bf16[8,128,256]{2,1,0:T(8,128)(2,1)S(1)}, bf16[8,128,256]{2,1,0:T(8,128)(2,1)S(1)}, u32[]{:S(2)}, u32[]{:S(2)}) collective-permute-start(bf16[8,128,256]{2,1,0:T(8,128)(2,1)S(1)} %get-tuple-element.34), channel_id=1, source_target_pairs={{0,2},{2,4},{4,6},{6,8},{8,10},{10,12},{12,14},{14,0},{1,3},{3,5},... | collective-permute-start | bytes 1572872 | tf_op jit(solution)/shard_map/ppermute | solution.py:334
  31.7 15.7 %collective-permute-start.11 = (bf16[2,128,768]{2,1,0:T(8,128)(2,1)S(1)}, bf16[2,128,768]{2,1,0:T(8,128)(2,1)S(1)}, u32[]{:S(2)}, u32[]{:S(2)}) collective-permute-start(bf16[2,128,768]{2,1,0:T(8,128)(2,1)S(1)} %get-tuple-element.33), channel_id=1, source_target_pairs={{0,1},{1,0},{2,3},{3,2},{4,5},{5,4},{6,7},{7,6},{8,9},{9,8},{10,11... | collective-permute-start | bytes 1179656 | tf_op jit(solution)/shard_map/ppermute | solution.py:311
  46.1 10.9 %collective-permute-start.13 = (bf16[128,768]{1,0:T(8,128)(2,1)S(1)}, bf16[128,768]{1,0:T(8,128)(2,1)S(1)}, u32[]{:S(2)}, u32[]{:S(2)}) collective-permute-start(bf16[128,768]{1,0:T(8,128)(2,1)S(1)} %get-tuple-element.41), channel_id=1, source_target_pairs={{0,1},{1,0},{2,3},{3,2},{4,5},{5,4},{6,7},{7,6},{8,9},{9,8},{10,11... | collective-permute-start | bytes 589832 | tf_op jit(solution)/shard_map/ppermute | solution.py:311
  46.8 10.2 %collective-permute-start.15 = (bf16[1024,256]{1,0:T(8,128)(2,1)S(1)}, bf16[1024,256]{1,0:T(8,128)(2,1)S(1)}, u32[]{:S(2)}, u32[]{:S(2)}) collective-permute-start(bf16[1024,256]{1,0:T(8,128)(2,1)S(1)} %get-tuple-element.44), channel_id=1, source_target_pairs={{0,14},{2,0},{4,2},{6,4},{8,6},{10,8},{12,10},{14,12},{1,15},{3,1}... | collective-permute-start | bytes 1572872 | tf_op jit(solution)/shard_map/ppermute | solution.py:334
  57.0 17.2 %collective-permute-start.19 = (bf16[1024,256]{1,0:T(8,128)(2,1)S(1)}, bf16[1024,256]{1,0:T(8,128)(2,1)S(1)}, u32[]{:S(2)}, u32[]{:S(2)}) collective-permute-start(bf16[1024,256]{1,0:T(8,128)(2,1)S(1)} %shard_map.84), channel_id=1, source_target_pairs={{0,14},{2,0},{4,2},{6,4},{8,6},{10,8},{12,10},{14,12},{1,15},{3,1}... | collective-permute-start | bytes 1572872 | tf_op jit(solution)/shard_map/ppermute | solution.py:334
  59.6 10.7 %collective-permute-start.16 = (bf16[256,256]{1,0:T(8,128)(2,1)S(1)}, bf16[256,256]{1,0:T(8,128)(2,1)S(1)}, u32[]{:S(2)}, u32[]{:S(2)}) collective-permute-start(bf16[256,256]{1,0:T(8,128)(2,1)S(1)} %get-tuple-element.56), channel_id=1, source_target_pairs={{0,112},{16,0},{32,16},{48,32},{64,48},{80,64},{96,80},{112,96},{1... | collective-permute-start | bytes 393224 | tf_op jit(solution)/shard_map/ppermute | solution.py:330
  60.3 10.0 %collective-permute-start.18 = (bf16[256,256]{1,0:T(8,128)(2,1)S(1)}, bf16[256,256]{1,0:T(8,128)(2,1)S(1)}, u32[]{:S(2)}, u32[]{:S(2)}) collective-permute-start(bf16[256,256]{1,0:T(8,128)(2,1)S(1)} %get-tuple-element.57), channel_id=1, source_target_pairs={{0,80},{16,96},{32,112},{48,0},{64,16},{80,32},{96,48},{112,64},{1... | collective-permute-start | bytes 393224 | tf_op jit(solution)/shard_map/ppermute | solution.py:330
  62.7 11.4 %collective-permute-start.17 = (bf16[256,256]{1,0:T(8,128)(2,1)S(1)}, bf16[256,256]{1,0:T(8,128)(2,1)S(1)}, u32[]{:S(2)}, u32[]{:S(2)}) collective-permute-start(bf16[256,256]{1,0:T(8,128)(2,1)S(1)} %get-tuple-element.58), channel_id=1, source_target_pairs={{0,96},{16,112},{32,0},{48,16},{64,32},{80,48},{96,64},{112,80},{1... | collective-permute-start | bytes 393224 | tf_op jit(solution)/shard_map/ppermute | solution.py:330
  68.5 18.7 %collective-permute-start.14 = (bf16[128,768]{1,0:T(8,128)(2,1)S(1)}, bf16[128,768]{1,0:T(8,128)(2,1)S(1)}, u32[]{:S(2)}, u32[]{:S(2)}) collective-permute-start(bf16[128,768]{1,0:T(8,128)(2,1)S(1)} %get-tuple-element.42), channel_id=1, source_target_pairs={{0,1},{1,0},{2,3},{3,2},{4,5},{5,4},{6,7},{7,6},{8,9},{9,8},{10,11... | collective-permute-start | bytes 589832 | tf_op jit(solution)/shard_map/ppermute | solution.py:311
  74.4 5.0 %collective-permute-start.20 = (bf16[256,256]{1,0:T(8,128)(2,1)S(1)}, bf16[256,256]{1,0:T(8,128)(2,1)S(1)}, u32[]{:S(2)}, u32[]{:S(2)}) collective-permute-start(bf16[256,256]{1,0:T(8,128)(2,1)S(1)} %get-tuple-element.53), channel_id=1, source_target_pairs={{0,112},{16,0},{32,16},{48,32},{64,48},{80,64},{96,80},{112,96},{1... | collective-permute-start | bytes 393224 | tf_op jit(solution)/shard_map/ppermute | solution.py:330
  74.5 6.7 %collective-permute-start.22 = (bf16[256,256]{1,0:T(8,128)(2,1)S(1)}, bf16[256,256]{1,0:T(8,128)(2,1)S(1)}, u32[]{:S(2)}, u32[]{:S(2)}) collective-permute-start(bf16[256,256]{1,0:T(8,128)(2,1)S(1)} %get-tuple-element.54), channel_id=1, source_target_pairs={{0,80},{16,96},{32,112},{48,0},{64,16},{80,32},{96,48},{112,64},{1... | collective-permute-start | bytes 393224 | tf_op jit(solution)/shard_map/ppermute | solution.py:330
  76.3 8.7 %collective-permute-start.21 = (bf16[256,256]{1,0:T(8,128)(2,1)S(1)}, bf16[256,256]{1,0:T(8,128)(2,1)S(1)}, u32[]{:S(2)}, u32[]{:S(2)}) collective-permute-start(bf16[256,256]{1,0:T(8,128)(2,1)S(1)} %get-tuple-element.55), channel_id=1, source_target_pairs={{0,96},{16,112},{32,0},{48,16},{64,32},{80,48},{96,64},{112,80},{1... | collective-permute-start | bytes 393224 | tf_op jit(solution)/shard_map/ppermute | solution.py:330
  85.1 6.6 %collective-permute-start.23 = (bf16[2,128,256]{2,1,0:T(8,128)(2,1)S(1)}, bf16[2,128,256]{2,1,0:T(8,128)(2,1)S(1)}, u32[]{:S(2)}, u32[]{:S(2)}) collective-permute-start(bf16[2,128,256]{2,1,0:T(8,128)(2,1)S(1)} %pad_maximum_fusion.2), channel_id=1, source_target_pairs={{0,1},{1,0},{2,3},{3,2},{4,5},{5,4},{6,7},{7,6},{8,9},{9,8},{10,11... | collective-permute-start | bytes 393224 | tf_op jit(solution)/shard_map/ppermute | solution.py:311
  (3 other events, 2.9 us)

commit v4 on v3

--- a/solution.py
+++ b/solution.py
@@ -372,7 +372,7 @@
     own, far, order = cut(queries, output_gradient, span_order, near[3])
     first_far = [cols(x, (1 - head) * KV * COLS, COLS) for x in (queries, output_gradient)]
     far = [[to_partner(x) for x in first_far], [to_partner(far)]]
-    far_in = [(along_outer(x, 1),) for x in pack(near, far[0][0])]
+    far_in = [(along_outer(x, 1),) for x in pack(near, far[0][0], first_far[1])]
     far_out0, near_out0, dq_own0, dq_far0 = attention(0, False, order, own[0], far[0], near, far_in[0])
     back0 = to_partner(dq_far0)
     arrived0 = along_outer(far_out0, -1)
@@ -380,8 +380,8 @@
     arrived1 = along_outer(tie(far_out1, arrived0), -1)
     total0, moved0 = send_terms(tie(near_out0, back0), arrived0)
     near_out1, dq_own1, dq_far1 = rest(kept)
-    back1 = to_partner(dq_far1)
     total1, moved1 = send_terms(tie(near_out1, *moved0), arrived1)
+    back1 = to_partner(tie(dq_far1, moved1[0]))
     sums = [total0, total1]
     for n, moved in enumerate((moved0, moved1)):
         for x in moved:

time: 92.8 us -> 95.1 us (1.025)
  the two profiles are of different devices: /device:TPU:16 before, /device:TPU:24 now
where the time goes in v4:
time: 95.1 us; the launch traced here: 94.7 us
  starting transfers between devices  38.7 us (41%)
  Pallas kernels  25.1 us (26%)
  waiting for transfers between devices  23.6 us (25%)
  local copies, waits for them, and re-layouts  5.78 us (6%)
    pallas_call x2, Pallas kernels, attention(): pl.pallas_call(functools.partial(early_kernel if split else whole_kernel,...  20.5 us
    ppermute x9, waiting for transfers between devices, along_inner(): return lax.ppermute(x, 'inner', [(i, (i + by) % 8) for i in range(8)])  15.2 us
    ppermute x7, starting transfers between devices, to_partner(): return lax.ppermute(x, 'head', [(0, 1), (1, 0)])  14.4 us
    ppermute x9, starting transfers between devices, along_inner(): return lax.ppermute(x, 'inner', [(i, (i + by) % 8) for i in range(8)])  11.7 us
    ppermute x7, waiting for transfers between devices, to_partner(): return lax.ppermute(x, 'head', [(0, 1), (1, 0)])  7.29 us
    ppermute x3, starting transfers between devices, along_y(): lax.ppermute(x, 'inner', [(lo * Y + y, lo * Y + (y + by) % Y) for lo in r...  4.9 us
    ppermute x4, starting transfers between devices, along_outer(): return lax.ppermute(x, 'outer', [(o, (o + by) % 8) for o in range(8)])  4.63 us
    ppermute x1, starting transfers between devices, across(): return lax.ppermute(x, ('inner', 'head'), perm)  3.04 us
  transfers between devices with their start and end apart: 24, of which 9 were waited for; matrix products, arithmetic and copies ran while one was open for 2% of the time, Pallas kernels for 25%

profile of v4, /device:TPU:24, one launch (start us, length us, event | category | flops | bytes accessed | tf_op | source)
XLA Modules:
  0.0 94.7 jit_solution(5560620393855748930)
XLA Ops:
  1.6 3.1 %collective-permute-start.1 = (bf16[2,128,256]{2,1,0:T(8,128)(2,1)S(1)}, bf16[2,128,256]{2,1,0:T(8,128)(2,1)S(1)}, u32[]{:S(2)}, u32[]{:S(2)}) collective-permute-start(bf16[2,128,256]{2,1,0:T(8,128)(2,1)S(1)} %pad_maximum_fusion), channel_id=1, source_target_pairs={{0,1},{1,0},{2,3},{3,2},{4,5},{5,4},{6,7},{7,6},{8,9},{9,8},{10,11... | collective-permute-start | bytes 393224 | tf_op jit(solution)/shard_map/ppermute | solution.py:311
  4.7 3.0 %collective-permute-start = (bf16[2,128,256]{2,1,0:T(8,128)(2,1)S(1)}, bf16[2,128,256]{2,1,0:T(8,128)(2,1)S(1)}, u32[]{:S(2)}, u32[]{:S(2)}) collective-permute-start(bf16[2,128,256]{2,1,0:T(8,128)(2,1)S(1)} %pad_maximum_fusion), channel_id=1, source_target_pairs={{16,81},{17,80},{32,97},{33,96},{48,113},{49,112},{80,17},{81,16},... | collective-permute-start | bytes 393224 | tf_op jit(solution)/shard_map/ppermute | solution.py:320
  8.1 4.5 %collective-permute-start.5 = (bf16[2,128,256]{2,1,0:T(8,128)(2,1)S(1)}, bf16[2,128,256]{2,1,0:T(8,128)(2,1)S(1)}, u32[]{:S(2)}, u32[]{:S(2)}) collective-permute-start(bf16[2,128,256]{2,1,0:T(8,128)(2,1)S(1)} %pad_maximum_fusion.1.refs_0_.refs_4_.refs_3_), channel_id=1, source_target_pairs={{0,16},{16,32},{32,48},{48,64},{64,80},{80,96},{96,112},{112,0},{1... | collective-permute-start | bytes 393224 | tf_op jit(solution)/shard_map/ppermute | solution.py:330
  13.6 1.8 %collective-permute-start.3 = (bf16[128,768]{1,0:T(8,128)(2,1)S(1)}, bf16[128,768]{1,0:T(8,128)(2,1)S(1)}, u32[]{:S(2)}, u32[]{:S(2)}) collective-permute-start(bf16[128,768]{1,0:T(8,128)(2,1)S(1)} %constant_dynamic-slice_fusion.5), channel_id=1, source_target_pairs={{0,1},{1,0},{2,3},{3,2},{4,5},{5,4},{6,7},{7,6},{8,9},{9,8},{10,11... | collective-permute-start | bytes 589832 | tf_op jit(solution)/shard_map/ppermute | solution.py:311
  16.6 1.7 %collective-permute-start.7 = (bf16[2,128,256]{2,1,0:T(8,128)(2,1)S(1)}, bf16[2,128,256]{2,1,0:T(8,128)(2,1)S(1)}, u32[]{:S(2)}, u32[]{:S(2)}) collective-permute-start(bf16[2,128,256]{2,1,0:T(8,128)(2,1)S(1)} %get-tuple-element.60), channel_id=1, source_target_pairs={{0,32},{16,48},{32,0},{48,16},{64,96},{80,112},{96,64},{112,80},{1... | collective-permute-start | bytes 393224 | tf_op jit(solution)/shard_map/ppermute | solution.py:324
  18.3 2.5 %collective-permute-start.2 = (bf16[2,128,256]{2,1,0:T(8,128)(2,1)S(1)}, bf16[2,128,256]{2,1,0:T(8,128)(2,1)S(1)}, u32[]{:S(2)}, u32[]{:S(2)}) collective-permute-start(bf16[2,128,256]{2,1,0:T(8,128)(2,1)S(1)} %get-tuple-element.61), channel_id=1, source_target_pairs={{0,16},{16,32},{32,48},{48,0},{64,80},{80,96},{96,112},{112,64},{1... | collective-permute-start | bytes 393224 | tf_op jit(solution)/shard_map/ppermute | solution.py:324
  21.8 2.3 %collective-permute-done.3.refs_8_.refs_2_ = bf16[128,768]{1,0:T(8,128)(2,1)S(1)} collective-permute-done((bf16[128,768]{1,0:T(8,128)(2,1)S(1)}, bf16[128,768]{1,0:T(8,128)(2,1)S(1)}, u32[]{:S(2)}, u32[]{:S(2)}) %collective-permute-start.3) | collective-permute-done | bytes 196640 | tf_op jit(solution)/shard_map/ppermute | solution.py:311
  24.2 1.7 %collective-permute-start.4 = (bf16[128,768]{1,0:T(8,128)(2,1)S(1)}, bf16[128,768]{1,0:T(8,128)(2,1)S(1)}, u32[]{:S(2)}, u32[]{:S(2)}) collective-permute-start(bf16[128,768]{1,0:T(8,128)(2,1)S(1)} %constant_dynamic-slice_fusion.4.refs_9_), channel_id=1, source_target_pairs={{0,1},{1,0},{2,3},{3,2},{4,5},{5,4},{6,7},{7,6},{8,9},{9,8},{10,11... | collective-permute-start | bytes 589832 | tf_op jit(solution)/shard_map/ppermute | solution.py:311
  25.9 1.7 %collective-permute-start.12 = (bf16[8,128,256]{2,1,0:T(8,128)(2,1)S(1)}, bf16[8,128,256]{2,1,0:T(8,128)(2,1)S(1)}, u32[]{:S(2)}, u32[]{:S(2)}) collective-permute-start(bf16[8,128,256]{2,1,0:T(8,128)(2,1)S(1)} %get-tuple-element.34), channel_id=1, source_target_pairs={{0,2},{2,4},{4,6},{6,8},{8,10},{10,12},{12,14},{14,0},{1,3},{3,5},... | collective-permute-start | bytes 1572872 | tf_op jit(solution)/shard_map/ppermute | solution.py:334
  27.6 1.1 %copy-done = bf16[128,3072]{1,0:T(8,128)(2,1)S(1)} copy-done((bf16[128,3072]{1,0:T(8,128)(2,1)S(1)}, bf16[128,3072]{1,0:T(8,128)(2,1)}, u32[]{:S(2)}) %copy-start) | copy-done | bytes 786456
  30.8 2.2 %collective-permute-start.11 = (bf16[2,128,768]{2,1,0:T(8,128)(2,1)S(1)}, bf16[2,128,768]{2,1,0:T(8,128)(2,1)S(1)}, u32[]{:S(2)}, u32[]{:S(2)}) collective-permute-start(bf16[2,128,768]{2,1,0:T(8,128)(2,1)S(1)} %get-tuple-element.33), channel_id=1, source_target_pairs={{0,1},{1,0},{2,3},{3,2},{4,5},{5,4},{6,7},{7,6},{8,9},{9,8},{10,11... | collective-permute-start | bytes 1179656 | tf_op jit(solution)/shard_map/ppermute | solution.py:311
  34.0 10.9 %shard_map.78 = (bf16[1024,256]{1,0:T(8,128)(2,1)S(1)}, bf16[1024,256]{1,0:T(8,128)(2,1)S(1)}, bf16[128,768]{1,0:T(8,128)(2,1)S(1)}, bf16[128,768]{1,0:T(8,128)(2,1)S(1)}) custom-call(s32[128]{0:T(128)S(1)} %get-tuple-element.26.order, bf16[128,768]{1,0:T(8,128)(2,1)S(1)} %get-tuple-element.27.refs_0_, bf16[128,768]{1,0:T(8,128)(2,1)S(1)} %get-tuple-element.28.refs_1_, ...), custom_call_target="tpu_custom_call" | custom-call | flops 16106127360 | bytes 5000000 | tf_op jit(solution)/shard_map/pallas_call | solution.py:168
  44.9 1.9 %collective-permute-start.13 = (bf16[128,768]{1,0:T(8,128)(2,1)S(1)}, bf16[128,768]{1,0:T(8,128)(2,1)S(1)}, u32[]{:S(2)}, u32[]{:S(2)}) collective-permute-start(bf16[128,768]{1,0:T(8,128)(2,1)S(1)} %get-tuple-element.41), channel_id=1, source_target_pairs={{0,1},{1,0},{2,3},{3,2},{4,5},{5,4},{6,7},{7,6},{8,9},{9,8},{10,11... | collective-permute-start | bytes 589832 | tf_op jit(solution)/shard_map/ppermute | solution.py:311
  46.9 9.6 %shard_map.79 = (bf16[1024,256]{1,0:T(8,128)(2,1)S(1)}, bf16[2048,1536]{1,0:T(8,128)(2,1)S(1)}, bf16[2048,1536]{1,0:T(8,128)(2,1)S(1)}, bf16[1536,128]{1,0:T(8,1...) custom-call(s32[128]{0:T(128)S(1)} %get-tuple-element.26.order, ...), custom_call_target="tpu_custom_call" | custom-call | flops 9663676416 | bytes 5000000 | tf_op jit(solution)/shard_map/pallas_call | solution.py:168
  56.5 2.9 %collective-permute-start.18 = (bf16[1024,256]{1,0:T(8,128)(2,1)S(1)}, bf16[1024,256]{1,0:T(8,128)(2,1)S(1)}, u32[]{:S(2)}, u32[]{:S(2)}) collective-permute-start(bf16[1024,256]{1,0:T(8,128)(2,1)S(1)} %shard_map.83), channel_id=1, source_target_pairs={{0,14},{2,0},{4,2},{6,4},{8,6},{10,8},{12,10},{14,12},{1,15},{3,1}... | collective-permute-start | bytes 1572872 | tf_op jit(solution)/shard_map/ppermute | solution.py:334
  59.6 3.3 %collective-permute-start.17 = (bf16[256,256]{1,0:T(8,128)(2,1)S(1)}, bf16[256,256]{1,0:T(8,128)(2,1)S(1)}, u32[]{:S(2)}, u32[]{:S(2)}) collective-permute-start(bf16[256,256]{1,0:T(8,128)(2,1)S(1)} %get-tuple-element.56), channel_id=1, source_target_pairs={{0,80},{16,96},{32,112},{48,0},{64,16},{80,32},{96,48},{112,64},{1... | collective-permute-start | bytes 393224 | tf_op jit(solution)/shard_map/ppermute | solution.py:330
  63.9 2.7 %shard_map.80 = (bf16[1024,256]{1,0:T(8,128)(2,1)S(1)}, bf16[128,768]{1,0:T(8,128)(2,1)S(1)}, bf16[128,768]{1,0:T(8,128)(2,1)S(1)}) custom-call(bf16[2048,1536]{1,0:T(8,128)(2,1)S(1)} %get-tuple-element.35.p, bf16[2048,1536]{1,0:T(8,128)(2,1)S(1)} %get-tuple-element.36.ds, bf16[1536,128]{1,0:T(8,128)(2,1)S(1)} %get-tuple-element.37.q, ...), custom_call_target="tpu_custom_call" | custom-call | flops 1000000 | bytes 1000000 | tf_op jit(solution)/shard_map/pallas_call | solution.py:189
  66.9 4.7 %collective-permute-done.16.refs_2_ = bf16[256,256]{1,0:T(8,128)(2,1)S(1)} collective-permute-done((bf16[256,256]{1,0:T(8,128)(2,1)S(1)}, bf16[256,256]{1,0:T(8,128)(2,1)S(1)}, u32[]{:S(2)}, u32[]{:S(2)}) %collective-permute-start.16) | collective-permute-done | bytes 131104 | tf_op jit(solution)/shard_map/ppermute | solution.py:330
  72.2 1.3 %collective-permute-start.22 = (bf16[256,256]{1,0:T(8,128)(2,1)S(1)}, bf16[256,256]{1,0:T(8,128)(2,1)S(1)}, u32[]{:S(2)}, u32[]{:S(2)}) collective-permute-start(bf16[256,256]{1,0:T(8,128)(2,1)S(1)} %get-tuple-element.54), channel_id=1, source_target_pairs={{0,80},{16,96},{32,112},{48,0},{64,16},{80,32},{96,48},{112,64},{1... | collective-permute-start | bytes 393224 | tf_op jit(solution)/shard_map/ppermute | solution.py:330
  73.5 1.2 %collective-permute-start.19 = (bf16[256,256]{1,0:T(8,128)(2,1)S(1)}, bf16[256,256]{1,0:T(8,128)(2,1)S(1)}, u32[]{:S(2)}, u32[]{:S(2)}) collective-permute-start(bf16[256,256]{1,0:T(8,128)(2,1)S(1)} %get-tuple-element.55), channel_id=1, source_target_pairs={{0,112},{16,0},{32,16},{48,32},{64,48},{80,64},{96,80},{112,96},{1... | collective-permute-start | bytes 393224 | tf_op jit(solution)/shard_map/ppermute | solution.py:330
  74.7 4.9 %collective-permute-done.21 = bf16[256,256]{1,0:T(8,128)(2,1)S(1)} collective-permute-done((bf16[256,256]{1,0:T(8,128)(2,1)S(1)}, bf16[256,256]{1,0:T(8,128)(2,1)S(1)}, u32[]{:S(2)}, u32[]{:S(2)}) %collective-permute-start.21) | collective-permute-done | bytes 131104 | tf_op jit(solution)/shard_map/ppermute | solution.py:330
  79.7 4.6 %collective-permute-done.19.refs_1_ = bf16[256,256]{1,0:T(8,128)(2,1)S(1)} collective-permute-done((bf16[256,256]{1,0:T(8,128)(2,1)S(1)}, bf16[256,256]{1,0:T(8,128)(2,1)S(1)}, u32[]{:S(2)}, u32[]{:S(2)}) %collective-permute-start.19) | collective-permute-done | bytes 131104 | tf_op jit(solution)/shard_map/ppermute | solution.py:330
  84.8 3.2 %collective-permute-start.23 = (bf16[2,128,256]{2,1,0:T(8,128)(2,1)S(1)}, bf16[2,128,256]{2,1,0:T(8,128)(2,1)S(1)}, u32[]{:S(2)}, u32[]{:S(2)}) collective-permute-start(bf16[2,128,256]{2,1,0:T(8,128)(2,1)S(1)} %pad_maximum_fusion.2), channel_id=1, source_target_pairs={{0,1},{1,0},{2,3},{3,2},{4,5},{5,4},{6,7},{7,6},{8,9},{9,8},{10,11... | collective-permute-start | bytes 393224 | tf_op jit(solution)/shard_map/ppermute | solution.py:311
  88.1 5.0 %collective-permute-done.23.theirs = bf16[2,128,256]{2,1,0:T(8,128)(2,1)S(1)} collective-permute-done((bf16[2,128,256]{2,1,0:T(8,128)(2,1)S(1)}, bf16[2,128,256]{2,1,0:T(8,128)(2,1)S(1)}, u32[]{:S(2)}, u32[]{:S(2)}) %collective-permute-start.23) | collective-permute-done | bytes 131104 | tf_op jit(solution)/shard_map/ppermute | solution.py:311
  (60 shorter events, 11.8 us)
Async XLA Ops:
  1.6 12.0 %collective-permute-start.1 = (bf16[2,128,256]{2,1,0:T(8,128)(2,1)S(1)}, bf16[2,128,256]{2,1,0:T(8,128)(2,1)S(1)}, u32[]{:S(2)}, u32[]{:S(2)}) collective-permute-start(bf16[2,128,256]{2,1,0:T(8,128)(2,1)S(1)} %pad_maximum_fusion), channel_id=1, source_target_pairs={{0,1},{1,0},{2,3},{3,2},{4,5},{5,4},{6,7},{7,6},{8,9},{9,8},{10,11... | collective-permute-start | bytes 393224 | tf_op jit(solution)/shard_map/ppermute | solution.py:311
  4.7 10.7 %collective-permute-start = (bf16[2,128,256]{2,1,0:T(8,128)(2,1)S(1)}, bf16[2,128,256]{2,1,0:T(8,128)(2,1)S(1)}, u32[]{:S(2)}, u32[]{:S(2)}) collective-permute-start(bf16[2,128,256]{2,1,0:T(8,128)(2,1)S(1)} %pad_maximum_fusion), channel_id=1, source_target_pairs={{16,81},{17,80},{32,97},{33,96},{48,113},{49,112},{80,17},{81,16},... | collective-permute-start | bytes 393224 | tf_op jit(solution)/shard_map/ppermute | solution.py:320
  7.8 8.8 %collective-permute-start.8 = (bf16[2,128,256]{2,1,0:T(8,128)(2,1)S(1)}, bf16[2,128,256]{2,1,0:T(8,128)(2,1)S(1)}, u32[]{:S(2)}, u32[]{:S(2)}) collective-permute-start(bf16[2,128,256]{2,1,0:T(8,128)(2,1)S(1)} %pad_maximum_fusion.1.refs_0_.refs_4_.refs_3_), channel_id=1, source_target_pairs={{0,48},{16,64},{32,80},{48,96},{64,112},{80,0},{96,16},{112,32},{1... | collective-permute-start | bytes 393224 | tf_op jit(solution)/shard_map/ppermute | solution.py:330
  7.9 10.4 %collective-permute-start.6 = (bf16[2,128,256]{2,1,0:T(8,128)(2,1)S(1)}, bf16[2,128,256]{2,1,0:T(8,128)(2,1)S(1)}, u32[]{:S(2)}, u32[]{:S(2)}) collective-permute-start(bf16[2,128,256]{2,1,0:T(8,128)(2,1)S(1)} %pad_maximum_fusion.1.refs_0_.refs_4_.refs_3_), channel_id=1, source_target_pairs={{0,32},{16,48},{32,64},{48,80},{64,96},{80,112},{96,0},{112,16},{1... | collective-permute-start | bytes 393224 | tf_op jit(solution)/shard_map/ppermute | solution.py:330
  8.1 13.7 %collective-permute-start.5 = (bf16[2,128,256]{2,1,0:T(8,128)(2,1)S(1)}, bf16[2,128,256]{2,1,0:T(8,128)(2,1)S(1)}, u32[]{:S(2)}, u32[]{:S(2)}) collective-permute-start(bf16[2,128,256]{2,1,0:T(8,128)(2,1)S(1)} %pad_maximum_fusion.1.refs_0_.refs_4_.refs_3_), channel_id=1, source_target_pairs={{0,16},{16,32},{32,48},{48,64},{64,80},{80,96},{96,112},{112,0},{1... | collective-permute-start | bytes 393224 | tf_op jit(solution)/shard_map/ppermute | solution.py:330
  13.6 10.5 %collective-permute-start.3 = (bf16[128,768]{1,0:T(8,128)(2,1)S(1)}, bf16[128,768]{1,0:T(8,128)(2,1)S(1)}, u32[]{:S(2)}, u32[]{:S(2)}) collective-permute-start(bf16[128,768]{1,0:T(8,128)(2,1)S(1)} %constant_dynamic-slice_fusion.5), channel_id=1, source_target_pairs={{0,1},{1,0},{2,3},{3,2},{4,5},{5,4},{6,7},{7,6},{8,9},{9,8},{10,11... | collective-permute-start | bytes 589832 | tf_op jit(solution)/shard_map/ppermute | solution.py:311
  15.4 8.7 %collective-permute-start.9 = (bf16[2,128,256]{2,1,0:T(8,128)(2,1)S(1)}, bf16[2,128,256]{2,1,0:T(8,128)(2,1)S(1)}, u32[]{:S(2)}, u32[]{:S(2)}) collective-permute-start(bf16[2,128,256]{2,1,0:T(8,128)(2,1)S(1)} %get-tuple-element.59), channel_id=1, source_target_pairs={{0,48},{16,0},{32,16},{48,32},{64,112},{80,64},{96,80},{112,96},{1... | collective-permute-start | bytes 393224 | tf_op jit(solution)/shard_map/ppermute | solution.py:324
  16.6 7.5 %collective-permute-start.7 = (bf16[2,128,256]{2,1,0:T(8,128)(2,1)S(1)}, bf16[2,128,256]{2,1,0:T(8,128)(2,1)S(1)}, u32[]{:S(2)}, u32[]{:S(2)}) collective-permute-start(bf16[2,128,256]{2,1,0:T(8,128)(2,1)S(1)} %get-tuple-element.60), channel_id=1, source_target_pairs={{0,32},{16,48},{32,0},{48,16},{64,96},{80,112},{96,64},{112,80},{1... | collective-permute-start | bytes 393224 | tf_op jit(solution)/shard_map/ppermute | solution.py:324
  18.3 5.8 %collective-permute-start.2 = (bf16[2,128,256]{2,1,0:T(8,128)(2,1)S(1)}, bf16[2,128,256]{2,1,0:T(8,128)(2,1)S(1)}, u32[]{:S(2)}, u32[]{:S(2)}) collective-permute-start(bf16[2,128,256]{2,1,0:T(8,128)(2,1)S(1)} %get-tuple-element.61), channel_id=1, source_target_pairs={{0,16},{16,32},{32,48},{48,0},{64,80},{80,96},{96,112},{112,64},{1... | collective-permute-start | bytes 393224 | tf_op jit(solution)/shard_map/ppermute | solution.py:324
  24.2 9.8 %collective-permute-start.10 = (bf16[8,128,256]{2,1,0:T(8,128)(2,1)S(1)}, bf16[8,128,256]{2,1,0:T(8,128)(2,1)S(1)}, u32[]{:S(2)}, u32[]{:S(2)}) collective-permute-start(bf16[8,128,256]{2,1,0:T(8,128)(2,1)S(1)} %get-tuple-element.29), channel_id=1, source_target_pairs={{0,2},{2,4},{4,6},{6,8},{8,10},{10,12},{12,14},{14,0},{1,3},{3,5},... | collective-permute-start | bytes 1572872 | tf_op jit(solution)/shard_map/ppermute | solution.py:334
  24.2 8.7 %collective-permute-start.4 = (bf16[128,768]{1,0:T(8,128)(2,1)S(1)}, bf16[128,768]{1,0:T(8,128)(2,1)S(1)}, u32[]{:S(2)}, u32[]{:S(2)}) collective-permute-start(bf16[128,768]{1,0:T(8,128)(2,1)S(1)} %constant_dynamic-slice_fusion.4.refs_9_), channel_id=1, source_target_pairs={{0,1},{1,0},{2,3},{3,2},{4,5},{5,4},{6,7},{7,6},{8,9},{9,8},{10,11... | collective-permute-start | bytes 589832 | tf_op jit(solution)/shard_map/ppermute | solution.py:311
  25.9 20.9 %collective-permute-start.12 = (bf16[8,128,256]{2,1,0:T(8,128)(2,1)S(1)}, bf16[8,128,256]{2,1,0:T(8,128)(2,1)S(1)}, u32[]{:S(2)}, u32[]{:S(2)}) collective-permute-start(bf16[8,128,256]{2,1,0:T(8,128)(2,1)S(1)} %get-tuple-element.34), channel_id=1, source_target_pairs={{0,2},{2,4},{4,6},{6,8},{8,10},{10,12},{12,14},{14,0},{1,3},{3,5},... | collective-permute-start | bytes 1572872 | tf_op jit(solution)/shard_map/ppermute | solution.py:334
  30.8 16.1 %collective-permute-start.11 = (bf16[2,128,768]{2,1,0:T(8,128)(2,1)S(1)}, bf16[2,128,768]{2,1,0:T(8,128)(2,1)S(1)}, u32[]{:S(2)}, u32[]{:S(2)}) collective-permute-start(bf16[2,128,768]{2,1,0:T(8,128)(2,1)S(1)} %get-tuple-element.33), channel_id=1, source_target_pairs={{0,1},{1,0},{2,3},{3,2},{4,5},{5,4},{6,7},{7,6},{8,9},{9,8},{10,11... | collective-permute-start | bytes 1179656 | tf_op jit(solution)/shard_map/ppermute | solution.py:311
  44.9 11.5 %collective-permute-start.13 = (bf16[128,768]{1,0:T(8,128)(2,1)S(1)}, bf16[128,768]{1,0:T(8,128)(2,1)S(1)}, u32[]{:S(2)}, u32[]{:S(2)}) collective-permute-start(bf16[128,768]{1,0:T(8,128)(2,1)S(1)} %get-tuple-element.41), channel_id=1, source_target_pairs={{0,1},{1,0},{2,3},{3,2},{4,5},{5,4},{6,7},{7,6},{8,9},{9,8},{10,11... | collective-permute-start | bytes 589832 | tf_op jit(solution)/shard_map/ppermute | solution.py:311
  46.9 9.6 %collective-permute-start.14 = (bf16[1024,256]{1,0:T(8,128)(2,1)S(1)}, bf16[1024,256]{1,0:T(8,128)(2,1)S(1)}, u32[]{:S(2)}, u32[]{:S(2)}) collective-permute-start(bf16[1024,256]{1,0:T(8,128)(2,1)S(1)} %get-tuple-element.45), channel_id=1, source_target_pairs={{0,14},{2,0},{4,2},{6,4},{8,6},{10,8},{12,10},{14,12},{1,15},{3,1}... | collective-permute-start | bytes 1572872 | tf_op jit(solution)/shard_map/ppermute | solution.py:334
  56.5 15.4 %collective-permute-start.18 = (bf16[1024,256]{1,0:T(8,128)(2,1)S(1)}, bf16[1024,256]{1,0:T(8,128)(2,1)S(1)}, u32[]{:S(2)}, u32[]{:S(2)}) collective-permute-start(bf16[1024,256]{1,0:T(8,128)(2,1)S(1)} %shard_map.83), channel_id=1, source_target_pairs={{0,14},{2,0},{4,2},{6,4},{8,6},{10,8},{12,10},{14,12},{1,15},{3,1}... | collective-permute-start | bytes 1572872 | tf_op jit(solution)/shard_map/ppermute | solution.py:334
  59.6 7.3 %collective-permute-start.17 = (bf16[256,256]{1,0:T(8,128)(2,1)S(1)}, bf16[256,256]{1,0:T(8,128)(2,1)S(1)}, u32[]{:S(2)}, u32[]{:S(2)}) collective-permute-start(bf16[256,256]{1,0:T(8,128)(2,1)S(1)} %get-tuple-element.56), channel_id=1, source_target_pairs={{0,80},{16,96},{32,112},{48,0},{64,16},{80,32},{96,48},{112,64},{1... | collective-permute-start | bytes 393224 | tf_op jit(solution)/shard_map/ppermute | solution.py:330
  63.0 8.7 %collective-permute-start.16 = (bf16[256,256]{1,0:T(8,128)(2,1)S(1)}, bf16[256,256]{1,0:T(8,128)(2,1)S(1)}, u32[]{:S(2)}, u32[]{:S(2)}) collective-permute-start(bf16[256,256]{1,0:T(8,128)(2,1)S(1)} %get-tuple-element.57), channel_id=1, source_target_pairs={{0,96},{16,112},{32,0},{48,16},{64,32},{80,48},{96,64},{112,80},{1... | collective-permute-start | bytes 393224 | tf_op jit(solution)/shard_map/ppermute | solution.py:330
  63.4 8.4 %collective-permute-start.15 = (bf16[256,256]{1,0:T(8,128)(2,1)S(1)}, bf16[256,256]{1,0:T(8,128)(2,1)S(1)}, u32[]{:S(2)}, u32[]{:S(2)}) collective-permute-start(bf16[256,256]{1,0:T(8,128)(2,1)S(1)} %get-tuple-element.58), channel_id=1, source_target_pairs={{0,112},{16,0},{32,16},{48,32},{64,48},{80,64},{96,80},{112,96},{1... | collective-permute-start | bytes 393224 | tf_op jit(solution)/shard_map/ppermute | solution.py:330
  72.1 7.5 %collective-permute-start.21 = (bf16[256,256]{1,0:T(8,128)(2,1)S(1)}, bf16[256,256]{1,0:T(8,128)(2,1)S(1)}, u32[]{:S(2)}, u32[]{:S(2)}) collective-permute-start(bf16[256,256]{1,0:T(8,128)(2,1)S(1)} %get-tuple-element.53), channel_id=1, source_target_pairs={{0,96},{16,112},{32,0},{48,16},{64,32},{80,48},{96,64},{112,80},{1... | collective-permute-start | bytes 393224 | tf_op jit(solution)/shard_map/ppermute | solution.py:330
  72.2 7.5 %collective-permute-start.22 = (bf16[256,256]{1,0:T(8,128)(2,1)S(1)}, bf16[256,256]{1,0:T(8,128)(2,1)S(1)}, u32[]{:S(2)}, u32[]{:S(2)}) collective-permute-start(bf16[256,256]{1,0:T(8,128)(2,1)S(1)} %get-tuple-element.54), channel_id=1, source_target_pairs={{0,80},{16,96},{32,112},{48,0},{64,16},{80,32},{96,48},{112,64},{1... | collective-permute-start | bytes 393224 | tf_op jit(solution)/shard_map/ppermute | solution.py:330
  73.5 10.7 %collective-permute-start.19 = (bf16[256,256]{1,0:T(8,128)(2,1)S(1)}, bf16[256,256]{1,0:T(8,128)(2,1)S(1)}, u32[]{:S(2)}, u32[]{:S(2)}) collective-permute-start(bf16[256,256]{1,0:T(8,128)(2,1)S(1)} %get-tuple-element.55), channel_id=1, source_target_pairs={{0,112},{16,0},{32,16},{48,32},{64,48},{80,64},{96,80},{112,96},{1... | collective-permute-start | bytes 393224 | tf_op jit(solution)/shard_map/ppermute | solution.py:330
  84.3 9.4 %collective-permute-start.20 = (bf16[128,768]{1,0:T(8,128)(2,1)S(1)}, bf16[128,768]{1,0:T(8,128)(2,1)S(1)}, u32[]{:S(2)}, u32[]{:S(2)}) collective-permute-start(bf16[128,768]{1,0:T(8,128)(2,1)S(1)} %shard_map.84), channel_id=1, source_target_pairs={{0,1},{1,0},{2,3},{3,2},{4,5},{5,4},{6,7},{7,6},{8,9},{9,8},{10,11... | collective-permute-start | bytes 589832 | tf_op jit(solution)/shard_map/ppermute | solution.py:311
  84.8 8.2 %collective-permute-start.23 = (bf16[2,128,256]{2,1,0:T(8,128)(2,1)S(1)}, bf16[2,128,256]{2,1,0:T(8,128)(2,1)S(1)}, u32[]{:S(2)}, u32[]{:S(2)}) collective-permute-start(bf16[2,128,256]{2,1,0:T(8,128)(2,1)S(1)} %pad_maximum_fusion.2), channel_id=1, source_target_pairs={{0,1},{1,0},{2,3},{3,2},{4,5},{5,4},{6,7},{7,6},{8,9},{9,8},{10,11... | collective-permute-start | bytes 393224 | tf_op jit(solution)/shard_map/ppermute | solution.py:311
  (3 other events, 2.9 us)

commit v5 on v4

--- a/solution.py
+++ b/solution.py
@@ -381,7 +381,7 @@
     total0, moved0 = send_terms(tie(near_out0, back0), arrived0)
     near_out1, dq_own1, dq_far1 = rest(kept)
     total1, moved1 = send_terms(tie(near_out1, *moved0), arrived1)
-    back1 = to_partner(tie(dq_far1, moved1[0]))
+    back1 = to_partner(tie(dq_far1, moved1[2]))
     sums = [total0, total1]
     for n, moved in enumerate((moved0, moved1)):
         for x in moved:

time: 95.1 us -> 96 us (level)
  the two profiles are of different devices: /device:TPU:24 before, /device:TPU:72 now
where the time goes in v5:
time: 96 us; the launch traced here: 95.7 us
  starting transfers between devices  41.1 us (43%)
  Pallas kernels  25.2 us (26%)
  waiting for transfers between devices  22.1 us (23%)
  local copies, waits for them, and re-layouts  5.78 us (6%)
    pallas_call x2, Pallas kernels, attention(): pl.pallas_call(functools.partial(early_kernel if split else whole_kernel,...  20.5 us
    ppermute x9, starting transfers between devices, along_inner(): return lax.ppermute(x, 'inner', [(i, (i + by) % 8) for i in range(8)])  17.6 us
    ppermute x7, starting transfers between devices, to_partner(): return lax.ppermute(x, 'head', [(0, 1), (1, 0)])  15.5 us
    ppermute x9, waiting for transfers between devices, along_inner(): return lax.ppermute(x, 'inner', [(i, (i + by) % 8) for i in range(8)])  11.4 us
    ppermute x7, waiting for transfers between devices, to_partner(): return lax.ppermute(x, 'head', [(0, 1), (1, 0)])  6.71 us
    ppermute x3, waiting for transfers between devices, along_y(): lax.ppermute(x, 'inner', [(lo * Y + y, lo * Y + (y + by) % Y) for lo in r...  4.02 us
    ppermute x3, starting transfers between devices, along_y(): lax.ppermute(x, 'inner', [(lo * Y + y, lo * Y + (y + by) % Y) for lo in r...  3.4 us
    ppermute x1, starting transfers between devices, across(): return lax.ppermute(x, ('inner', 'head'), perm)  3.04 us
  transfers between devices with their start and end apart: 24, of which 9 were waited for; matrix products, arithmetic and copies ran while one was open for 2% of the time, Pallas kernels for 25%

profile of v5, /device:TPU:72, one launch (start us, length us, event | category | flops | bytes accessed | tf_op | source)
XLA Modules:
  0.0 95.7 jit_solution(9616150966405999414)
XLA Ops:
  1.6 3.1 %collective-permute-start.1 = (bf16[2,128,256]{2,1,0:T(8,128)(2,1)S(1)}, bf16[2,128,256]{2,1,0:T(8,128)(2,1)S(1)}, u32[]{:S(2)}, u32[]{:S(2)}) collective-permute-start(bf16[2,128,256]{2,1,0:T(8,128)(2,1)S(1)} %pad_maximum_fusion), channel_id=1, source_target_pairs={{0,1},{1,0},{2,3},{3,2},{4,5},{5,4},{6,7},{7,6},{8,9},{9,8},{10,11... | collective-permute-start | bytes 393224 | tf_op jit(solution)/shard_map/ppermute | solution.py:311
  4.7 3.0 %collective-permute-start = (bf16[2,128,256]{2,1,0:T(8,128)(2,1)S(1)}, bf16[2,128,256]{2,1,0:T(8,128)(2,1)S(1)}, u32[]{:S(2)}, u32[]{:S(2)}) collective-permute-start(bf16[2,128,256]{2,1,0:T(8,128)(2,1)S(1)} %pad_maximum_fusion), channel_id=1, source_target_pairs={{16,81},{17,80},{32,97},{33,96},{48,113},{49,112},{80,17},{81,16},... | collective-permute-start | bytes 393224 | tf_op jit(solution)/shard_map/ppermute | solution.py:320
  7.9 2.4 %collective-permute-start.6 = (bf16[2,128,256]{2,1,0:T(8,128)(2,1)S(1)}, bf16[2,128,256]{2,1,0:T(8,128)(2,1)S(1)}, u32[]{:S(2)}, u32[]{:S(2)}) collective-permute-start(bf16[2,128,256]{2,1,0:T(8,128)(2,1)S(1)} %pad_maximum_fusion.1.refs_0_.refs_4_.refs_3_), channel_id=1, source_target_pairs={{0,32},{16,48},{32,64},{48,80},{64,96},{80,112},{96,0},{112,16},{1... | collective-permute-start | bytes 393224 | tf_op jit(solution)/shard_map/ppermute | solution.py:330
  10.3 1.4 %collective-permute-start.5 = (bf16[2,128,256]{2,1,0:T(8,128)(2,1)S(1)}, bf16[2,128,256]{2,1,0:T(8,128)(2,1)S(1)}, u32[]{:S(2)}, u32[]{:S(2)}) collective-permute-start(bf16[2,128,256]{2,1,0:T(8,128)(2,1)S(1)} %pad_maximum_fusion.1.refs_0_.refs_4_.refs_3_), channel_id=1, source_target_pairs={{0,16},{16,32},{32,48},{48,64},{64,80},{80,96},{96,112},{112,0},{1... | collective-permute-start | bytes 393224 | tf_op jit(solution)/shard_map/ppermute | solution.py:330
  12.7 4.2 %collective-permute-start.3 = (bf16[128,768]{1,0:T(8,128)(2,1)S(1)}, bf16[128,768]{1,0:T(8,128)(2,1)S(1)}, u32[]{:S(2)}, u32[]{:S(2)}) collective-permute-start(bf16[128,768]{1,0:T(8,128)(2,1)S(1)} %constant_dynamic-slice_fusion.5), channel_id=1, source_target_pairs={{0,1},{1,0},{2,3},{3,2},{4,5},{5,4},{6,7},{7,6},{8,9},{9,8},{10,11... | collective-permute-start | bytes 589832 | tf_op jit(solution)/shard_map/ppermute | solution.py:311
  17.1 1.8 %collective-permute-start.7 = (bf16[2,128,256]{2,1,0:T(8,128)(2,1)S(1)}, bf16[2,128,256]{2,1,0:T(8,128)(2,1)S(1)}, u32[]{:S(2)}, u32[]{:S(2)}) collective-permute-start(bf16[2,128,256]{2,1,0:T(8,128)(2,1)S(1)} %get-tuple-element.60), channel_id=1, source_target_pairs={{0,32},{16,48},{32,0},{48,16},{64,96},{80,112},{96,64},{112,80},{1... | collective-permute-start | bytes 393224 | tf_op jit(solution)/shard_map/ppermute | solution.py:324
  19.0 1.4 %collective-permute-start.2 = (bf16[2,128,256]{2,1,0:T(8,128)(2,1)S(1)}, bf16[2,128,256]{2,1,0:T(8,128)(2,1)S(1)}, u32[]{:S(2)}, u32[]{:S(2)}) collective-permute-start(bf16[2,128,256]{2,1,0:T(8,128)(2,1)S(1)} %get-tuple-element.61), channel_id=1, source_target_pairs={{0,16},{16,32},{32,48},{48,0},{64,80},{80,96},{96,112},{112,64},{1... | collective-permute-start | bytes 393224 | tf_op jit(solution)/shard_map/ppermute | solution.py:324
  21.4 2.7 %collective-permute-done.9.refs_7_.refs_11_.refs_10_ = bf16[2,128,256]{2,1,0:T(8,128)(2,1)S(1)} collective-permute-done((bf16[2,128,256]{2,1,0:T(8,128)(2,1)S(1)}, bf16[2,128,256]{2,1,0:T(8,128)(2,1)S(1)}, u32[]{:S(2)}, u32[]{:S(2)}) %collective-permute-start.9) | collective-permute-done | bytes 131104 | tf_op jit(solution)/shard_map/ppermute | solution.py:324
  30.5 3.5 %collective-permute-start.11 = (bf16[2,128,768]{2,1,0:T(8,128)(2,1)S(1)}, bf16[2,128,768]{2,1,0:T(8,128)(2,1)S(1)}, u32[]{:S(2)}, u32[]{:S(2)}) collective-permute-start(bf16[2,128,768]{2,1,0:T(8,128)(2,1)S(1)} %get-tuple-element.33), channel_id=1, source_target_pairs={{0,1},{1,0},{2,3},{3,2},{4,5},{5,4},{6,7},{7,6},{8,9},{9,8},{10,11... | collective-permute-start | bytes 1179656 | tf_op jit(solution)/shard_map/ppermute | solution.py:311
  34.3 10.9 %shard_map.78 = (bf16[1024,256]{1,0:T(8,128)(2,1)S(1)}, bf16[1024,256]{1,0:T(8,128)(2,1)S(1)}, bf16[128,768]{1,0:T(8,128)(2,1)S(1)}, bf16[128,768]{1,0:T(8,128)(2,1)S(1)}) custom-call(s32[128]{0:T(128)S(1)} %get-tuple-element.26.order, bf16[128,768]{1,0:T(8,128)(2,1)S(1)} %get-tuple-element.27.refs_0_, bf16[128,768]{1,0:T(8,128)(2,1)S(1)} %get-tuple-element.28.refs_1_, ...), custom_call_target="tpu_custom_call" | custom-call | flops 16106127360 | bytes 5000000 | tf_op jit(solution)/shard_map/pallas_call | solution.py:168
  45.8 9.6 %shard_map.79 = (bf16[1024,256]{1,0:T(8,128)(2,1)S(1)}, bf16[2048,1536]{1,0:T(8,128)(2,1)S(1)}, bf16[2048,1536]{1,0:T(8,128)(2,1)S(1)}, bf16[1536,128]{1,0:T(8,1...) custom-call(s32[128]{0:T(128)S(1)} %get-tuple-element.26.order, ...), custom_call_target="tpu_custom_call" | custom-call | flops 9663676416 | bytes 5000000 | tf_op jit(solution)/shard_map/pallas_call | solution.py:168
  55.9 2.5 %collective-permute-start.17 = (bf16[256,256]{1,0:T(8,128)(2,1)S(1)}, bf16[256,256]{1,0:T(8,128)(2,1)S(1)}, u32[]{:S(2)}, u32[]{:S(2)}) collective-permute-start(bf16[256,256]{1,0:T(8,128)(2,1)S(1)} %get-tuple-element.56), channel_id=1, source_target_pairs={{0,80},{16,96},{32,112},{48,0},{64,16},{80,32},{96,48},{112,64},{1... | collective-permute-start | bytes 393224 | tf_op jit(solution)/shard_map/ppermute | solution.py:330
  58.4 3.5 %collective-permute-start.16 = (bf16[256,256]{1,0:T(8,128)(2,1)S(1)}, bf16[256,256]{1,0:T(8,128)(2,1)S(1)}, u32[]{:S(2)}, u32[]{:S(2)}) collective-permute-start(bf16[256,256]{1,0:T(8,128)(2,1)S(1)} %get-tuple-element.57), channel_id=1, source_target_pairs={{0,96},{16,112},{32,0},{48,16},{64,32},{80,48},{96,64},{112,80},{1... | collective-permute-start | bytes 393224 | tf_op jit(solution)/shard_map/ppermute | solution.py:330
  61.9 2.7 %shard_map.80 = (bf16[1024,256]{1,0:T(8,128)(2,1)S(1)}, bf16[128,768]{1,0:T(8,128)(2,1)S(1)}, bf16[128,768]{1,0:T(8,128)(2,1)S(1)}) custom-call(bf16[2048,1536]{1,0:T(8,128)(2,1)S(1)} %get-tuple-element.35.p, bf16[2048,1536]{1,0:T(8,128)(2,1)S(1)} %get-tuple-element.36.ds, bf16[1536,128]{1,0:T(8,128)(2,1)S(1)} %get-tuple-element.37.q, ...), custom_call_target="tpu_custom_call" | custom-call | flops 1000000 | bytes 1000000 | tf_op jit(solution)/shard_map/pallas_call | solution.py:189
  64.6 1.7 %collective-permute-done.16.refs_2_ = bf16[256,256]{1,0:T(8,128)(2,1)S(1)} collective-permute-done((bf16[256,256]{1,0:T(8,128)(2,1)S(1)}, bf16[256,256]{1,0:T(8,128)(2,1)S(1)}, u32[]{:S(2)}, u32[]{:S(2)}) %collective-permute-start.16) | collective-permute-done | bytes 131104 | tf_op jit(solution)/shard_map/ppermute | solution.py:330
  66.3 1.9 %collective-permute-done.15.refs_1_ = bf16[256,256]{1,0:T(8,128)(2,1)S(1)} collective-permute-done((bf16[256,256]{1,0:T(8,128)(2,1)S(1)}, bf16[256,256]{1,0:T(8,128)(2,1)S(1)}, u32[]{:S(2)}, u32[]{:S(2)}) %collective-permute-start.15) | collective-permute-done | bytes 131104 | tf_op jit(solution)/shard_map/ppermute | solution.py:330
  68.4 2.0 %collective-permute-start.21 = (bf16[256,256]{1,0:T(8,128)(2,1)S(1)}, bf16[256,256]{1,0:T(8,128)(2,1)S(1)}, u32[]{:S(2)}, u32[]{:S(2)}) collective-permute-start(bf16[256,256]{1,0:T(8,128)(2,1)S(1)} %get-tuple-element.53), channel_id=1, source_target_pairs={{0,112},{16,0},{32,16},{48,32},{64,48},{80,64},{96,80},{112,96},{1... | collective-permute-start | bytes 393224 | tf_op jit(solution)/shard_map/ppermute | solution.py:330
  70.5 2.6 %collective-permute-start.22 = (bf16[256,256]{1,0:T(8,128)(2,1)S(1)}, bf16[256,256]{1,0:T(8,128)(2,1)S(1)}, u32[]{:S(2)}, u32[]{:S(2)}) collective-permute-start(bf16[256,256]{1,0:T(8,128)(2,1)S(1)} %get-tuple-element.54), channel_id=1, source_target_pairs={{0,96},{16,112},{32,0},{48,16},{64,32},{80,48},{96,64},{112,80},{1... | collective-permute-start | bytes 393224 | tf_op jit(solution)/shard_map/ppermute | solution.py:330
  73.0 3.1 %collective-permute-start.19 = (bf16[256,256]{1,0:T(8,128)(2,1)S(1)}, bf16[256,256]{1,0:T(8,128)(2,1)S(1)}, u32[]{:S(2)}, u32[]{:S(2)}) collective-permute-start(bf16[256,256]{1,0:T(8,128)(2,1)S(1)} %get-tuple-element.55), channel_id=1, source_target_pairs={{0,80},{16,96},{32,112},{48,0},{64,16},{80,32},{96,48},{112,64},{1... | collective-permute-start | bytes 393224 | tf_op jit(solution)/shard_map/ppermute | solution.py:330
  76.1 2.7 %collective-permute-done.22 = bf16[256,256]{1,0:T(8,128)(2,1)S(1)} collective-permute-done((bf16[256,256]{1,0:T(8,128)(2,1)S(1)}, bf16[256,256]{1,0:T(8,128)(2,1)S(1)}, u32[]{:S(2)}, u32[]{:S(2)}) %collective-permute-start.22) | collective-permute-done | bytes 131104 | tf_op jit(solution)/shard_map/ppermute | solution.py:330
  78.8 4.9 %collective-permute-done.19.refs_1_ = bf16[256,256]{1,0:T(8,128)(2,1)S(1)} collective-permute-done((bf16[256,256]{1,0:T(8,128)(2,1)S(1)}, bf16[256,256]{1,0:T(8,128)(2,1)S(1)}, u32[]{:S(2)}, u32[]{:S(2)}) %collective-permute-start.19) | collective-permute-done | bytes 131104 | tf_op jit(solution)/shard_map/ppermute | solution.py:330
  83.9 1.6 %collective-permute-start.20 = (bf16[128,768]{1,0:T(8,128)(2,1)S(1)}, bf16[128,768]{1,0:T(8,128)(2,1)S(1)}, u32[]{:S(2)}, u32[]{:S(2)}) collective-permute-start(bf16[128,768]{1,0:T(8,128)(2,1)S(1)} %shard_map.84), channel_id=1, source_target_pairs={{0,1},{1,0},{2,3},{3,2},{4,5},{5,4},{6,7},{7,6},{8,9},{9,8},{10,11... | collective-permute-start | bytes 589832 | tf_op jit(solution)/shard_map/ppermute | solution.py:311
  85.5 2.1 %collective-permute-start.23 = (bf16[2,128,256]{2,1,0:T(8,128)(2,1)S(1)}, bf16[2,128,256]{2,1,0:T(8,128)(2,1)S(1)}, u32[]{:S(2)}, u32[]{:S(2)}) collective-permute-start(bf16[2,128,256]{2,1,0:T(8,128)(2,1)S(1)} %pad_maximum_fusion.2), channel_id=1, source_target_pairs={{0,1},{1,0},{2,3},{3,2},{4,5},{5,4},{6,7},{7,6},{8,9},{9,8},{10,11... | collective-permute-start | bytes 393224 | tf_op jit(solution)/shard_map/ppermute | solution.py:311
  87.6 6.4 %collective-permute-done.23.theirs = bf16[2,128,256]{2,1,0:T(8,128)(2,1)S(1)} collective-permute-done((bf16[2,128,256]{2,1,0:T(8,128)(2,1)S(1)}, bf16[2,128,256]{2,1,0:T(8,128)(2,1)S(1)}, u32[]{:S(2)}, u32[]{:S(2)}) %collective-permute-start.23) | collective-permute-done | bytes 131104 | tf_op jit(solution)/shard_map/ppermute | solution.py:311
  (60 shorter events, 13.1 us)
Async XLA Ops:
  1.6 11.1 %collective-permute-start.1 = (bf16[2,128,256]{2,1,0:T(8,128)(2,1)S(1)}, bf16[2,128,256]{2,1,0:T(8,128)(2,1)S(1)}, u32[]{:S(2)}, u32[]{:S(2)}) collective-permute-start(bf16[2,128,256]{2,1,0:T(8,128)(2,1)S(1)} %pad_maximum_fusion), channel_id=1, source_target_pairs={{0,1},{1,0},{2,3},{3,2},{4,5},{5,4},{6,7},{7,6},{8,9},{9,8},{10,11... | collective-permute-start | bytes 393224 | tf_op jit(solution)/shard_map/ppermute | solution.py:311
  4.7 12.1 %collective-permute-start = (bf16[2,128,256]{2,1,0:T(8,128)(2,1)S(1)}, bf16[2,128,256]{2,1,0:T(8,128)(2,1)S(1)}, u32[]{:S(2)}, u32[]{:S(2)}) collective-permute-start(bf16[2,128,256]{2,1,0:T(8,128)(2,1)S(1)} %pad_maximum_fusion), channel_id=1, source_target_pairs={{16,81},{17,80},{32,97},{33,96},{48,113},{49,112},{80,17},{81,16},... | collective-permute-start | bytes 393224 | tf_op jit(solution)/shard_map/ppermute | solution.py:320
  7.8 9.3 %collective-permute-start.8 = (bf16[2,128,256]{2,1,0:T(8,128)(2,1)S(1)}, bf16[2,128,256]{2,1,0:T(8,128)(2,1)S(1)}, u32[]{:S(2)}, u32[]{:S(2)}) collective-permute-start(bf16[2,128,256]{2,1,0:T(8,128)(2,1)S(1)} %pad_maximum_fusion.1.refs_0_.refs_4_.refs_3_), channel_id=1, source_target_pairs={{0,48},{16,64},{32,80},{48,96},{64,112},{80,0},{96,16},{112,32},{1... | collective-permute-start | bytes 393224 | tf_op jit(solution)/shard_map/ppermute | solution.py:330
  7.9 11.1 %collective-permute-start.6 = (bf16[2,128,256]{2,1,0:T(8,128)(2,1)S(1)}, bf16[2,128,256]{2,1,0:T(8,128)(2,1)S(1)}, u32[]{:S(2)}, u32[]{:S(2)}) collective-permute-start(bf16[2,128,256]{2,1,0:T(8,128)(2,1)S(1)} %pad_maximum_fusion.1.refs_0_.refs_4_.refs_3_), channel_id=1, source_target_pairs={{0,32},{16,48},{32,64},{48,80},{64,96},{80,112},{96,0},{112,16},{1... | collective-permute-start | bytes 393224 | tf_op jit(solution)/shard_map/ppermute | solution.py:330
  10.3 11.1 %collective-permute-start.5 = (bf16[2,128,256]{2,1,0:T(8,128)(2,1)S(1)}, bf16[2,128,256]{2,1,0:T(8,128)(2,1)S(1)}, u32[]{:S(2)}, u32[]{:S(2)}) collective-permute-start(bf16[2,128,256]{2,1,0:T(8,128)(2,1)S(1)} %pad_maximum_fusion.1.refs_0_.refs_4_.refs_3_), channel_id=1, source_target_pairs={{0,16},{16,32},{32,48},{48,64},{64,80},{80,96},{96,112},{112,0},{1... | collective-permute-start | bytes 393224 | tf_op jit(solution)/shard_map/ppermute | solution.py:330
  12.7 8.7 %collective-permute-start.3 = (bf16[128,768]{1,0:T(8,128)(2,1)S(1)}, bf16[128,768]{1,0:T(8,128)(2,1)S(1)}, u32[]{:S(2)}, u32[]{:S(2)}) collective-permute-start(bf16[128,768]{1,0:T(8,128)(2,1)S(1)} %constant_dynamic-slice_fusion.5), channel_id=1, source_target_pairs={{0,1},{1,0},{2,3},{3,2},{4,5},{5,4},{6,7},{7,6},{8,9},{9,8},{10,11... | collective-permute-start | bytes 589832 | tf_op jit(solution)/shard_map/ppermute | solution.py:311
  16.9 7.2 %collective-permute-start.9 = (bf16[2,128,256]{2,1,0:T(8,128)(2,1)S(1)}, bf16[2,128,256]{2,1,0:T(8,128)(2,1)S(1)}, u32[]{:S(2)}, u32[]{:S(2)}) collective-permute-start(bf16[2,128,256]{2,1,0:T(8,128)(2,1)S(1)} %get-tuple-element.59), channel_id=1, source_target_pairs={{0,48},{16,0},{32,16},{48,32},{64,112},{80,64},{96,80},{112,96},{1... | collective-permute-start | bytes 393224 | tf_op jit(solution)/shard_map/ppermute | solution.py:324
  17.1 7.0 %collective-permute-start.7 = (bf16[2,128,256]{2,1,0:T(8,128)(2,1)S(1)}, bf16[2,128,256]{2,1,0:T(8,128)(2,1)S(1)}, u32[]{:S(2)}, u32[]{:S(2)}) collective-permute-start(bf16[2,128,256]{2,1,0:T(8,128)(2,1)S(1)} %get-tuple-element.60), channel_id=1, source_target_pairs={{0,32},{16,48},{32,0},{48,16},{64,96},{80,112},{96,64},{112,80},{1... | collective-permute-start | bytes 393224 | tf_op jit(solution)/shard_map/ppermute | solution.py:324
  19.0 6.4 %collective-permute-start.2 = (bf16[2,128,256]{2,1,0:T(8,128)(2,1)S(1)}, bf16[2,128,256]{2,1,0:T(8,128)(2,1)S(1)}, u32[]{:S(2)}, u32[]{:S(2)}) collective-permute-start(bf16[2,128,256]{2,1,0:T(8,128)(2,1)S(1)} %get-tuple-element.61), channel_id=1, source_target_pairs={{0,16},{16,32},{32,48},{48,0},{64,80},{80,96},{96,112},{112,64},{1... | collective-permute-start | bytes 393224 | tf_op jit(solution)/shard_map/ppermute | solution.py:324
  25.5 8.8 %collective-permute-start.10 = (bf16[8,128,256]{2,1,0:T(8,128)(2,1)S(1)}, bf16[8,128,256]{2,1,0:T(8,128)(2,1)S(1)}, u32[]{:S(2)}, u32[]{:S(2)}) collective-permute-start(bf16[8,128,256]{2,1,0:T(8,128)(2,1)S(1)} %get-tuple-element.29), channel_id=1, source_target_pairs={{0,2},{2,4},{4,6},{6,8},{8,10},{10,12},{12,14},{14,0},{1,3},{3,5},... | collective-permute-start | bytes 1572872 | tf_op jit(solution)/shard_map/ppermute | solution.py:334
  25.5 8.7 %collective-permute-start.4 = (bf16[128,768]{1,0:T(8,128)(2,1)S(1)}, bf16[128,768]{1,0:T(8,128)(2,1)S(1)}, u32[]{:S(2)}, u32[]{:S(2)}) collective-permute-start(bf16[128,768]{1,0:T(8,128)(2,1)S(1)} %constant_dynamic-slice_fusion.4.refs_9_), channel_id=1, source_target_pairs={{0,1},{1,0},{2,3},{3,2},{4,5},{5,4},{6,7},{7,6},{8,9},{9,8},{10,11... | collective-permute-start | bytes 589832 | tf_op jit(solution)/shard_map/ppermute | solution.py:311
  26.0 19.9 %collective-permute-start.12 = (bf16[8,128,256]{2,1,0:T(8,128)(2,1)S(1)}, bf16[8,128,256]{2,1,0:T(8,128)(2,1)S(1)}, u32[]{:S(2)}, u32[]{:S(2)}) collective-permute-start(bf16[8,128,256]{2,1,0:T(8,128)(2,1)S(1)} %get-tuple-element.34), channel_id=1, source_target_pairs={{0,2},{2,4},{4,6},{6,8},{8,10},{10,12},{12,14},{14,0},{1,3},{3,5},... | collective-permute-start | bytes 1572872 | tf_op jit(solution)/shard_map/ppermute | solution.py:334
  30.5 15.3 %collective-permute-start.11 = (bf16[2,128,768]{2,1,0:T(8,128)(2,1)S(1)}, bf16[2,128,768]{2,1,0:T(8,128)(2,1)S(1)}, u32[]{:S(2)}, u32[]{:S(2)}) collective-permute-start(bf16[2,128,768]{2,1,0:T(8,128)(2,1)S(1)} %get-tuple-element.33), channel_id=1, source_target_pairs={{0,1},{1,0},{2,3},{3,2},{4,5},{5,4},{6,7},{7,6},{8,9},{9,8},{10,11... | collective-permute-start | bytes 1179656 | tf_op jit(solution)/shard_map/ppermute | solution.py:311
  45.2 10.2 %collective-permute-start.13 = (bf16[128,768]{1,0:T(8,128)(2,1)S(1)}, bf16[128,768]{1,0:T(8,128)(2,1)S(1)}, u32[]{:S(2)}, u32[]{:S(2)}) collective-permute-start(bf16[128,768]{1,0:T(8,128)(2,1)S(1)} %get-tuple-element.41), channel_id=1, source_target_pairs={{0,1},{1,0},{2,3},{3,2},{4,5},{5,4},{6,7},{7,6},{8,9},{9,8},{10,11... | collective-permute-start | bytes 589832 | tf_op jit(solution)/shard_map/ppermute | solution.py:311
  45.8 9.6 %collective-permute-start.14 = (bf16[1024,256]{1,0:T(8,128)(2,1)S(1)}, bf16[1024,256]{1,0:T(8,128)(2,1)S(1)}, u32[]{:S(2)}, u32[]{:S(2)}) collective-permute-start(bf16[1024,256]{1,0:T(8,128)(2,1)S(1)} %get-tuple-element.45), channel_id=1, source_target_pairs={{0,14},{2,0},{4,2},{6,4},{8,6},{10,8},{12,10},{14,12},{1,15},{3,1}... | collective-permute-start | bytes 1572872 | tf_op jit(solution)/shard_map/ppermute | solution.py:334
  55.4 12.8 %collective-permute-start.18 = (bf16[1024,256]{1,0:T(8,128)(2,1)S(1)}, bf16[1024,256]{1,0:T(8,128)(2,1)S(1)}, u32[]{:S(2)}, u32[]{:S(2)}) collective-permute-start(bf16[1024,256]{1,0:T(8,128)(2,1)S(1)} %shard_map.83), channel_id=1, source_target_pairs={{0,14},{2,0},{4,2},{6,4},{8,6},{10,8},{12,10},{14,12},{1,15},{3,1}... | collective-permute-start | bytes 1572872 | tf_op jit(solution)/shard_map/ppermute | solution.py:334
  55.9 8.7 %collective-permute-start.17 = (bf16[256,256]{1,0:T(8,128)(2,1)S(1)}, bf16[256,256]{1,0:T(8,128)(2,1)S(1)}, u32[]{:S(2)}, u32[]{:S(2)}) collective-permute-start(bf16[256,256]{1,0:T(8,128)(2,1)S(1)} %get-tuple-element.56), channel_id=1, source_target_pairs={{0,80},{16,96},{32,112},{48,0},{64,16},{80,32},{96,48},{112,64},{1... | collective-permute-start | bytes 393224 | tf_op jit(solution)/shard_map/ppermute | solution.py:330
  58.4 7.9 %collective-permute-start.16 = (bf16[256,256]{1,0:T(8,128)(2,1)S(1)}, bf16[256,256]{1,0:T(8,128)(2,1)S(1)}, u32[]{:S(2)}, u32[]{:S(2)}) collective-permute-start(bf16[256,256]{1,0:T(8,128)(2,1)S(1)} %get-tuple-element.57), channel_id=1, source_target_pairs={{0,96},{16,112},{32,0},{48,16},{64,32},{80,48},{96,64},{112,80},{1... | collective-permute-start | bytes 393224 | tf_op jit(solution)/shard_map/ppermute | solution.py:330
  61.9 6.3 %collective-permute-start.15 = (bf16[256,256]{1,0:T(8,128)(2,1)S(1)}, bf16[256,256]{1,0:T(8,128)(2,1)S(1)}, u32[]{:S(2)}, u32[]{:S(2)}) collective-permute-start(bf16[256,256]{1,0:T(8,128)(2,1)S(1)} %get-tuple-element.58), channel_id=1, source_target_pairs={{0,112},{16,0},{32,16},{48,32},{64,48},{80,64},{96,80},{112,96},{1... | collective-permute-start | bytes 393224 | tf_op jit(solution)/shard_map/ppermute | solution.py:330
  68.4 7.7 %collective-permute-start.21 = (bf16[256,256]{1,0:T(8,128)(2,1)S(1)}, bf16[256,256]{1,0:T(8,128)(2,1)S(1)}, u32[]{:S(2)}, u32[]{:S(2)}) collective-permute-start(bf16[256,256]{1,0:T(8,128)(2,1)S(1)} %get-tuple-element.53), channel_id=1, source_target_pairs={{0,112},{16,0},{32,16},{48,32},{64,48},{80,64},{96,80},{112,96},{1... | collective-permute-start | bytes 393224 | tf_op jit(solution)/shard_map/ppermute | solution.py:330
  70.5 8.4 %collective-permute-start.22 = (bf16[256,256]{1,0:T(8,128)(2,1)S(1)}, bf16[256,256]{1,0:T(8,128)(2,1)S(1)}, u32[]{:S(2)}, u32[]{:S(2)}) collective-permute-start(bf16[256,256]{1,0:T(8,128)(2,1)S(1)} %get-tuple-element.54), channel_id=1, source_target_pairs={{0,96},{16,112},{32,0},{48,16},{64,32},{80,48},{96,64},{112,80},{1... | collective-permute-start | bytes 393224 | tf_op jit(solution)/shard_map/ppermute | solution.py:330
  73.0 10.7 %collective-permute-start.19 = (bf16[256,256]{1,0:T(8,128)(2,1)S(1)}, bf16[256,256]{1,0:T(8,128)(2,1)S(1)}, u32[]{:S(2)}, u32[]{:S(2)}) collective-permute-start(bf16[256,256]{1,0:T(8,128)(2,1)S(1)} %get-tuple-element.55), channel_id=1, source_target_pairs={{0,80},{16,96},{32,112},{48,0},{64,16},{80,32},{96,48},{112,64},{1... | collective-permute-start | bytes 393224 | tf_op jit(solution)/shard_map/ppermute | solution.py:330
  83.9 10.8 %collective-permute-start.20 = (bf16[128,768]{1,0:T(8,128)(2,1)S(1)}, bf16[128,768]{1,0:T(8,128)(2,1)S(1)}, u32[]{:S(2)}, u32[]{:S(2)}) collective-permute-start(bf16[128,768]{1,0:T(8,128)(2,1)S(1)} %shard_map.84), channel_id=1, source_target_pairs={{0,1},{1,0},{2,3},{3,2},{4,5},{5,4},{6,7},{7,6},{8,9},{9,8},{10,11... | collective-permute-start | bytes 589832 | tf_op jit(solution)/shard_map/ppermute | solution.py:311
  85.5 8.4 %collective-permute-start.23 = (bf16[2,128,256]{2,1,0:T(8,128)(2,1)S(1)}, bf16[2,128,256]{2,1,0:T(8,128)(2,1)S(1)}, u32[]{:S(2)}, u32[]{:S(2)}) collective-permute-start(bf16[2,128,256]{2,1,0:T(8,128)(2,1)S(1)} %pad_maximum_fusion.2), channel_id=1, source_target_pairs={{0,1},{1,0},{2,3},{3,2},{4,5},{5,4},{6,7},{7,6},{8,9},{9,8},{10,11... | collective-permute-start | bytes 393224 | tf_op jit(solution)/shard_map/ppermute | solution.py:311
  (3 other events, 2.9 us)
